TPU v7x, 32 devices: a whole 2x2x4 slice. The times are simulated.
32 devices in a mesh: seq: 4 (over x, core), expert: 8 (over z, y).
Axes of the slice: x: 2, y: 2, z: 4, core: 2. Of those that a mesh axis runs over, the one named last changes fastest.
Arguments:
- tokens: bfloat16 [8, 512, 2048], P('expert', 'seq'), may hold values from -6 to 6
- lengths: int32 [8, 4], P('expert'), may hold values from 1 to 512, as said below
- routes: int32 [8, 512, 8], P('expert', 'seq'), may hold values from 0 to 15, all different within a row; in each aligned block of 128 rows (0 to 127, 128 to 255, ..., all dimensions but the last counted through in order) at most 64 rows name the same one
- gain_attn: float32 [2048], replicated, may hold values from 0.5 to 1.5
- w_query: bfloat16 [2048, 2048], P(('seq', 'expert')), may hold values from -0.125 to 0.125
- w_key: bfloat16 [2048, 2048], P(('seq', 'expert')), may hold values from -0.125 to 0.125
- w_value: bfloat16 [2048, 2048], P(('seq', 'expert')), may hold values from -0.125 to 0.125
- gain_query: float32 [2048], replicated, may hold values from 0.5 to 1.5
- gain_key: float32 [2048], replicated, may hold values from 0.5 to 1.5
- w_out: bfloat16 [2048, 2048], P(('seq', 'expert')), may hold values from -0.75 to 0.75
- gain_mlp: float32 [2048], replicated, may hold values from 0.5 to 1.5
- router: bfloat16 [2048, 16], replicated, may hold values from -0.0625 to 0.0625
- w_gate: bfloat16 [16, 2048, 1024], P('expert'), may hold values from -0.125 to 0.125
- w_up: bfloat16 [16, 2048, 1024], P('expert'), may hold values from -0.125 to 0.125
- w_down: bfloat16 [16, 1024, 2048], P('expert'), may hold values from -3 to 3
- cotangent: bfloat16 [8, 512, 2048], P('expert', 'seq'), may hold values from -6 to 6
Outputs:
- mixed: bfloat16 [8, 512, 2048], P('expert', 'seq')
- d_tokens: float32 [8, 512, 2048], P('expert', 'seq')
- d_gain_attn: float32 [2048], replicated
- d_w_query: float32 [2048, 2048], P(('seq', 'expert'))
- d_w_key: float32 [2048, 2048], P(('seq', 'expert'))
- d_w_value: float32 [2048, 2048], P(('seq', 'expert'))
- d_gain_query: float32 [2048], replicated
- d_gain_key: float32 [2048], replicated
- d_w_out: float32 [2048, 2048], P(('seq', 'expert'))
- d_gain_mlp: float32 [2048], replicated
- d_router: float32 [2048, 16], replicated
- d_w_gate: float32 [16, 2048, 1024], P('expert', 'seq')
- d_w_up: float32 [16, 2048, 1024], P('expert', 'seq')
- d_w_down: float32 [16, 1024, 2048], P('expert', 'seq')
Inputs may be any that keep to these rules, and one draw needn't show every extreme that they name: `routes`: in the tokens of one device no expert is named by more than 64 of them. Each pack's 4 document lengths are positive and add up to 512.
All inputs are finite; a program needn't handle non-finite values.
Results may differ from a plain program's by a relative error of at most 0.02.
Values may be sent and summed in bfloat16 or wider, within the bound.
A program may use at most 320 MiB of HBM per device.

v0:
```python
from functools import partial

import jax
import jax.numpy as jnp
from jax import lax
from jax.sharding import PartitionSpec as P

HEADS = 16
MOST = 64


norm_eps = 1e-05
masked_score = -1e30


def product(left_matrix, right_matrix):
    return jnp.dot(left_matrix, right_matrix, preferred_element_type=jnp.float32)


def rms_norm(values, norm_gain):
    return (
        values * lax.rsqrt(jnp.mean(values * values, axis=-1, keepdims=True) + norm_eps) * norm_gain
    )


def rotate(values, offsets):
    half_dim = values.shape[-1] // 2
    inverse = 10000.0 ** (-jnp.arange(half_dim, dtype=jnp.float32) / half_dim)
    angles = offsets.astype(jnp.float32)[:, None] * inverse[None, :]
    cosine = jnp.cos(angles)[:, None, :]
    sine_table = jnp.sin(angles)[:, None, :]
    first_half = values[..., :half_dim]
    second = values[..., half_dim:]
    return jnp.concatenate(
        [first_half * cosine - second * sine_table, second * cosine + first_half * sine_table],
        axis=-1,
    )


def doc_tables(lengths_row, places):
    doc_ends = jnp.cumsum(lengths_row)
    passed = (places[:, None] >= doc_ends[None, :]).astype(jnp.int32)
    return (jnp.sum(passed, axis=1), places - jnp.sum(passed * lengths_row[None, :], axis=1))


def head_norm(raw_values, norm_gain, offsets, head_count):
    normed = rms_norm(raw_values, norm_gain)
    return rotate(normed.reshape(raw_values.shape[0], head_count, -1), offsets)


def local(
    tokens,
    lengths,
    routes,
    gain_attn,
    w_query,
    w_key,
    w_value,
    gain_query,
    gain_key,
    w_out,
    gain_mlp,
    router,
    w_gate,
    w_up,
    w_down,
    cotangent,
):
    seq_count = lax.axis_size("seq")
    group_count = lax.axis_size("expert")
    tok_rows = tokens.shape[1]
    model_width = tokens.shape[2]
    head_count = HEADS
    head_dim = model_width // head_count
    experts_local = w_gate.shape[0]
    total_experts = experts_local * group_count
    top_count = routes.shape[2]
    slot_count = MOST
    length = tok_rows * seq_count
    score_scale = head_dim ** (-0.5)
    inputs = tokens[0].astype(jnp.float32)
    places_all = jnp.arange(length, dtype=jnp.int32)
    doc_all, offset_all = doc_tables(lengths[0], places_all)
    first_place = lax.axis_index("seq") * tok_rows
    doc_mine = lax.dynamic_slice_in_dim(doc_all, first_place, tok_rows)
    offset_mine = lax.dynamic_slice_in_dim(offset_all, first_place, tok_rows)
    places_mine = first_place + jnp.arange(tok_rows, dtype=jnp.int32)
    allowed = (doc_mine[:, None] == doc_all[None, :]) & (
        places_all[None, :] <= places_mine[:, None]
    )
    full_query, full_key, full_value, full_out = (
        lax.all_gather(w_query, ("seq", "expert"), axis=0, tiled=True),
        lax.all_gather(w_key, ("seq", "expert"), axis=0, tiled=True),
        lax.all_gather(w_value, ("seq", "expert"), axis=0, tiled=True),
        lax.all_gather(w_out, ("seq", "expert"), axis=0, tiled=True),
    )
    normed, attn_norm_back = jax.vjp(rms_norm, inputs, gain_attn)
    normed_low = normed.astype(jnp.bfloat16)
    query_raw = product(normed_low, full_query)
    key_raw = product(normed_low, full_key)
    value_low = product(normed_low, full_value).astype(jnp.bfloat16)
    rope_norm = partial(head_norm, offsets=offset_mine, head_count=head_count)
    query_rot, query_back = jax.vjp(rope_norm, query_raw, gain_query)
    key_rot, key_back = jax.vjp(rope_norm, key_raw, gain_key)
    query_low = query_rot.astype(jnp.bfloat16)
    key_low = key_rot.astype(jnp.bfloat16).reshape(tok_rows, model_width)
    keys_all, values_all = (
        lax.all_gather(key_low, "seq", axis=0, tiled=True),
        lax.all_gather(value_low, "seq", axis=0, tiled=True),
    )
    key_heads = keys_all.reshape(length, head_count, head_dim)
    value_heads = values_all.reshape(length, head_count, head_dim)

    def scores_for():
        raw_scores = (
            jnp.einsum("qhd,khd->hqk", query_low, key_heads, preferred_element_type=jnp.float32)
            * score_scale
        )
        return jnp.where(allowed[None], raw_scores, masked_score)

    scores = scores_for()
    top_score = jnp.max(scores, axis=-1, keepdims=True)
    log_total = top_score + jnp.log(jnp.sum(jnp.exp(scores - top_score), axis=-1, keepdims=True))
    probs_low = jnp.exp(scores - log_total).astype(jnp.bfloat16)
    attended = jnp.einsum(
        "hqk,khd->qhd", probs_low, value_heads, preferred_element_type=jnp.float32
    )
    attended_low = attended.reshape(tok_rows, model_width).astype(jnp.bfloat16)
    hidden = inputs + product(attended_low, full_out)
    normed2, mlp_norm_back = jax.vjp(rms_norm, hidden, gain_mlp)
    normed2_low = normed2.astype(jnp.bfloat16)
    logits = product(normed2_low, router)
    router_probs, softmax_back = jax.vjp(partial(jax.nn.softmax, axis=-1), logits)
    picks = routes[0]
    expert_ids = jnp.arange(total_experts, dtype=jnp.int32)
    select = (picks[:, :, None] == expert_ids[None, None, :]).astype(jnp.float32)
    gate_values = jnp.einsum("tke,te->tk", select, router_probs)
    flat_experts = picks.reshape(tok_rows * top_count)
    expert_hits = (flat_experts[:, None] == expert_ids[None, :]).astype(jnp.int32)
    slot_rank = jnp.sum((jnp.cumsum(expert_hits, axis=0) - 1) * expert_hits, axis=1)
    targets = flat_experts * slot_count + slot_rank

    def pack_rows(values):
        empty_rows = jnp.zeros((total_experts * slot_count, model_width), values.dtype)
        return (
            empty_rows.at[targets]
            .set(values)
            .reshape(group_count, experts_local, slot_count, model_width)
        )

    def unpack_rows(packed):
        return packed.reshape(total_experts * slot_count, model_width)[targets].reshape(
            tok_rows, top_count, model_width
        )

    def expert_hidden(arrived):
        gate_pre = jnp.einsum("sjmd,jdf->sjmf", arrived, w_gate, preferred_element_type=jnp.float32)
        up_pre = jnp.einsum("sjmd,jdf->sjmf", arrived, w_up, preferred_element_type=jnp.float32)
        return (gate_pre, up_pre)

    send_rows = pack_rows(jnp.repeat(normed2_low, top_count, axis=0))
    routed = lax.all_to_all(send_rows, "expert", split_axis=0, concat_axis=0, tiled=True)
    gate_pre, up_pre = expert_hidden(routed)
    active_low = (jax.nn.silu(gate_pre) * up_pre).astype(jnp.bfloat16)
    expert_out = jnp.einsum(
        "sjmf,jfd->sjmd", active_low, w_down, preferred_element_type=jnp.float32
    ).astype(jnp.bfloat16)
    returned = unpack_rows(
        lax.all_to_all(expert_out, "expert", split_axis=0, concat_axis=0, tiled=True)
    )
    moe_sum = jnp.einsum("tk,tkd->td", gate_values, returned.astype(jnp.float32))
    final_sum = hidden + moe_sum
    grad_final = cotangent[0].astype(jnp.float32)
    grad_gates = jnp.einsum("td,tkd->tk", grad_final, returned.astype(jnp.float32))
    grad_rows = (gate_values[:, :, None] * grad_final[:, None, :]).astype(jnp.bfloat16)
    grad_packed = pack_rows(grad_rows.reshape(tok_rows * top_count, model_width))
    grad_arrived = lax.all_to_all(grad_packed, "expert", split_axis=0, concat_axis=0, tiled=True)
    gate_again, up_again = expert_hidden(routed)
    sigmoid_gate = jax.nn.sigmoid(gate_again)
    silu_gate = gate_again * sigmoid_gate
    active_again = (silu_gate * up_again).astype(jnp.bfloat16)
    grad_active = jnp.einsum(
        "sjmd,jfd->sjmf", grad_arrived, w_down, preferred_element_type=jnp.float32
    )
    grad_gate_low = (
        grad_active * up_again * sigmoid_gate * (1.0 + gate_again * (1.0 - sigmoid_gate))
    ).astype(jnp.bfloat16)
    grad_up_low = (grad_active * silu_gate).astype(jnp.bfloat16)
    grad_routed = jnp.einsum(
        "sjmf,jdf->sjmd", grad_gate_low, w_gate, preferred_element_type=jnp.float32
    )
    grad_routed = (
        grad_routed
        + jnp.einsum("sjmf,jdf->sjmd", grad_up_low, w_up, preferred_element_type=jnp.float32)
    ).astype(jnp.bfloat16)
    grad_w_gate = jnp.einsum(
        "sjmd,sjmf->jdf", routed, grad_gate_low, preferred_element_type=jnp.float32
    )
    grad_w_up = jnp.einsum(
        "sjmd,sjmf->jdf", routed, grad_up_low, preferred_element_type=jnp.float32
    )
    grad_w_down = jnp.einsum(
        "sjmf,sjmd->jfd", active_again, grad_arrived, preferred_element_type=jnp.float32
    )
    back_rows = unpack_rows(
        lax.all_to_all(grad_routed, "expert", split_axis=0, concat_axis=0, tiled=True)
    )
    d_w_gate, d_w_up, d_w_down = (
        lax.psum_scatter(
            grad_w_gate.astype(jnp.bfloat16), "seq", scatter_dimension=1, tiled=True
        ).astype(jnp.float32),
        lax.psum_scatter(
            grad_w_up.astype(jnp.bfloat16), "seq", scatter_dimension=1, tiled=True
        ).astype(jnp.float32),
        lax.psum_scatter(
            grad_w_down.astype(jnp.bfloat16), "seq", scatter_dimension=1, tiled=True
        ).astype(jnp.float32),
    )
    grad_probs = jnp.einsum("tke,tk->te", select, grad_gates)
    (grad_logits,) = softmax_back(grad_probs)
    grad_logits_low = grad_logits.astype(jnp.bfloat16)
    grad_router = jnp.einsum(
        "td,te->de", normed2_low, grad_logits_low, preferred_element_type=jnp.float32
    )
    grad_normed2 = jnp.sum(back_rows.astype(jnp.float32), axis=1)
    grad_normed2 = grad_normed2 + jnp.einsum(
        "te,de->td", grad_logits_low, router, preferred_element_type=jnp.float32
    )
    grad_hidden_part, grad_gain_mlp = mlp_norm_back(grad_normed2)
    grad_hidden = grad_final + grad_hidden_part
    back_query, back_key, back_value, back_out = (
        lax.all_gather(w_query, ("seq", "expert"), axis=0, tiled=True),
        lax.all_gather(w_key, ("seq", "expert"), axis=0, tiled=True),
        lax.all_gather(w_value, ("seq", "expert"), axis=0, tiled=True),
        lax.all_gather(w_out, ("seq", "expert"), axis=0, tiled=True),
    )
    grad_hidden_low = grad_hidden.astype(jnp.bfloat16)
    grad_w_out = jnp.einsum(
        "td,te->de", attended_low, grad_hidden_low, preferred_element_type=jnp.float32
    )
    grad_attended = jnp.einsum(
        "te,de->td", grad_hidden_low, back_out, preferred_element_type=jnp.float32
    ).astype(jnp.bfloat16)
    grad_attended = grad_attended.reshape(tok_rows, head_count, head_dim)
    probs_again = jnp.exp(scores_for() - log_total)
    probs_again_low = probs_again.astype(jnp.bfloat16)
    grad_probs_attn = jnp.einsum(
        "qhd,khd->hqk", grad_attended, value_heads, preferred_element_type=jnp.float32
    )
    row_dot = jnp.sum(probs_again * grad_probs_attn, axis=-1, keepdims=True)
    grad_scores_low = (probs_again * (grad_probs_attn - row_dot)).astype(jnp.bfloat16)
    grad_query = (
        jnp.einsum("hqk,khd->qhd", grad_scores_low, key_heads, preferred_element_type=jnp.float32)
        * score_scale
    )
    grad_keys_all = (
        jnp.einsum("hqk,qhd->khd", grad_scores_low, query_low, preferred_element_type=jnp.float32)
        * score_scale
    )
    grad_values_all = jnp.einsum(
        "hqk,qhd->khd", probs_again_low, grad_attended, preferred_element_type=jnp.float32
    )
    grad_key_rot, grad_value = (
        lax.psum_scatter(
            grad_keys_all.reshape(length, model_width).astype(jnp.bfloat16),
            "seq",
            scatter_dimension=0,
            tiled=True,
        ).astype(jnp.float32),
        lax.psum_scatter(
            grad_values_all.reshape(length, model_width).astype(jnp.bfloat16),
            "seq",
            scatter_dimension=0,
            tiled=True,
        ).astype(jnp.float32),
    )
    grad_query_pre, grad_gain_query = query_back(grad_query)
    grad_key_pre, grad_gain_key = key_back(grad_key_rot.reshape(tok_rows, head_count, head_dim))
    grad_query_low = grad_query_pre.astype(jnp.bfloat16)
    grad_key_low = grad_key_pre.astype(jnp.bfloat16)
    grad_value_low = grad_value.astype(jnp.bfloat16)
    grad_w_query = jnp.einsum(
        "td,te->de", normed_low, grad_query_low, preferred_element_type=jnp.float32
    )
    grad_w_key = jnp.einsum(
        "td,te->de", normed_low, grad_key_low, preferred_element_type=jnp.float32
    )
    grad_w_value = jnp.einsum(
        "td,te->de", normed_low, grad_value_low, preferred_element_type=jnp.float32
    )
    grad_normed = jnp.einsum(
        "te,de->td", grad_query_low, back_query, preferred_element_type=jnp.float32
    )
    grad_normed = grad_normed + jnp.einsum(
        "te,de->td", grad_key_low, back_key, preferred_element_type=jnp.float32
    )
    grad_normed = grad_normed + jnp.einsum(
        "te,de->td", grad_value_low, back_value, preferred_element_type=jnp.float32
    )
    grad_inputs_part, grad_gain_attn = attn_norm_back(grad_normed)
    grad_inputs = grad_hidden + grad_inputs_part
    d_w_query, d_w_key, d_w_value, d_w_out = (
        lax.psum_scatter(grad_w_query, ("seq", "expert"), scatter_dimension=0, tiled=True),
        lax.psum_scatter(grad_w_key, ("seq", "expert"), scatter_dimension=0, tiled=True),
        lax.psum_scatter(grad_w_value, ("seq", "expert"), scatter_dimension=0, tiled=True),
        lax.psum_scatter(grad_w_out, ("seq", "expert"), scatter_dimension=0, tiled=True),
    )
    d_gain_attn, d_gain_query, d_gain_key, d_gain_mlp, d_router = lax.psum(
        (grad_gain_attn, grad_gain_query, grad_gain_key, grad_gain_mlp, grad_router),
        ("seq", "expert"),
    )
    return (
        final_sum.astype(jnp.bfloat16)[None],
        grad_inputs[None],
        d_gain_attn,
        d_w_query,
        d_w_key,
        d_w_value,
        d_gain_query,
        d_gain_key,
        d_w_out,
        d_gain_mlp,
        d_router,
        d_w_gate,
        d_w_up,
        d_w_down,
    )


def solution(mesh):
    return jax.shard_map(
        local,
        mesh=mesh,
        in_specs=(
            P("expert", "seq", None),
            P("expert", None),
            P("expert", "seq", None),
            P(),
            P(("seq", "expert"), None),
            P(("seq", "expert"), None),
            P(("seq", "expert"), None),
            P(),
            P(),
            P(("seq", "expert"), None),
            P(),
            P(),
            P("expert", None, None),
            P("expert", None, None),
            P("expert", None, None),
            P("expert", "seq", None),
        ),
        out_specs=(
            P("expert", "seq", None),
            P("expert", "seq", None),
            P(),
            P(("seq", "expert"), None),
            P(("seq", "expert"), None),
            P(("seq", "expert"), None),
            P(),
            P(),
            P(("seq", "expert"), None),
            P(),
            P(),
            P("expert", "seq", None),
            P("expert", "seq", None),
            P("expert", "seq", None),
        ),
        check_vma=False,
    )
```

profile of v0, /device:TPU:0, one launch (start us, length us, event | category | flops | bytes accessed | tf_op | source)
XLA Modules:
  0.0 2738.7 jit_solution(3503397110148621406)
XLA Ops:
  12.7 78.4 %all-gather.11.cloned.1.call-done = bf16[2048,2048]{1,0:T(8,128)(2,1)} async-done(((bf16[64,2048]{1,0:T(8,128)(2,1)}), bf16[2048,2048]{1,0:T(8,128)(2,1)}) %all-gather.11.cloned.1.call-update) | async-done | bytes 8388624 | tf_op jit(solution)/shard_map/all_gather | solution.py:92
  97.5 72.6 %all-gather.13.cloned.1.call-done = bf16[2048,2048]{1,0:T(8,128)(2,1)} async-done(((bf16[64,2048]{1,0:T(8,128)(2,1)}), bf16[2048,2048]{1,0:T(8,128)(2,1)}) %all-gather.13.cloned.1.call-update) | async-done | bytes 8388624 | tf_op jit(solution)/shard_map/all_gather | solution.py:93
  179.8 69.4 %all-gather.7.cloned.1.call-done = bf16[2048,2048]{1,0:T(8,128)(2,1)} async-done(((bf16[64,2048]{1,0:T(8,128)(2,1)}), bf16[2048,2048]{1,0:T(8,128)(2,1)}) %all-gather.7.cloned.1.call-update) | async-done | bytes 8388624 | tf_op jit(solution)/shard_map/all_gather | solution.py:94
  261.0 11.7 all-gather.15.cloned.1.call-done
  278.7 18.6 all-gather.9.cloned.1.call-done
  301.6 75.9 %all-gather.17.cloned.1.call-done = bf16[2048,2048]{1,0:T(8,128)(2,1)} async-done(((bf16[64,2048]{1,0:T(8,128)(2,1)}), bf16[2048,2048]{1,0:T(8,128)(2,1)}) %all-gather.17.cloned.1.call-update) | async-done | bytes 8388624 | tf_op jit(solution)/shard_map/all_gather | solution.py:95
  397.6 9.4 scatter_custom_fusion.1
  407.0 83.3 %all-to-all-done = bf16[8,2,64,2048]{3,2,1,0:T(8,128)(2,1)} async-done(((bf16[8,2,64,2048]{3,2,1,0:T(8,128)(2,1)}), bf16[8,2,64,2048]{3,2,1,0:T(8,128)(2,1)}, u32[]{:S(2)}, u32[]{:S(2)}) %all-to-all-start) | async-done | bytes 4194336 | tf_op jit(solution)/shard_map/all_to_all | solution.py:162
  494.9 11.2 fusion.2
  506.0 11.2 fusion.6
  517.2 70.7 %all-to-all-done.2 = bf16[8,2,64,2048]{3,2,1,0:T(8,128)(2,1)} async-done(((bf16[8,2,64,2048]{3,2,1,0:T(8,128)(2,1)}), bf16[8,2,64,2048]{3,2,1,0:T(8,128)(2,1)}, u32[]{:S(2)}, u32[]{:S(2)}) %all-to-all-start.2) | async-done | bytes 4194336 | tf_op jit(solution)/shard_map/all_to_all | solution.py:177
  587.9 15.5 fusion.18
  603.4 12.2 fusion
  615.7 12.9 fusion.13
  648.8 81.7 %all-to-all-done.3 = bf16[8,2,64,2048]{3,2,1,0:T(8,128)(2,1)} async-done(((bf16[8,2,64,2048]{3,2,1,0:T(8,128)(2,1)}), bf16[8,2,64,2048]{3,2,1,0:T(8,128)(2,1)}, u32[]{:S(2)}, u32[]{:S(2)}) %all-to-all-start.3) | async-done | bytes 4194336 | tf_op jit(solution)/shard_map/all_to_all | solution.py:206
  735.1 11.5 gather_fusion.1
  751.7 75.8 %all-to-all-done.1 = bf16[8,2,64,2048]{3,2,1,0:T(8,128)(2,1)} async-done(((bf16[8,2,64,2048]{3,2,1,0:T(8,128)(2,1)}), bf16[8,2,64,2048]{3,2,1,0:T(8,128)(2,1)}, u32[]{:S(2)}, u32[]{:S(2)}) %all-to-all-start.1) | async-done | bytes 4194336 | tf_op jit(solution)/shard_map/all_to_all | solution.py:169
  827.6 11.7 gather_fusion
  880.8 10.7 bitcast_convert_fusion.2
  891.6 10.8 bitcast_convert_fusion.1
  902.7 10.8 bitcast_convert_fusion
  915.5 9.3 fusion.82
  938.2 9.5 fusion.115
  964.1 9.3 fusion.111
  989.6 39.2 %all-reduce.4 = (f32[2048]{0:T(1024)}, f32[2048]{0:T(1024)}, f32[2048]{0:T(1024)}, f32[2048]{0:T(1024)}) all-reduce(f32[2048]{0:T(1024)S(1)} %get-tuple-element.20, f32[2048]{0:T(1024)S(1)} %get-tuple-element.18, f32[2048]{0:T(1024)S(1)} %get-tuple-element.16, ...), channel_id=1, replica_groups=mesh['seq'=4,'expert'=8] {'seq','expert'}, use_global_device_ids=true, to_apply=%region_26.27 | all-reduce | flops 8192 | bytes 65536 | tf_op jit(solution)/shard_map/psum | solution.py:308
  1034.2 51.9 %reduce-scatter.24.cloned.1.call-done = bf16[2,512,1024]{2,1,0:T(8,128)(2,1)} async-done(((bf16[2,2048,1024]{2,1,0:T(8,128)(2,1)}), bf16[2,512,1024]{2,1,0:T(8,128)(2,1)}) %reduce-scatter.24.cloned.1.call-update) | async-done | bytes 2097168 | tf_op jit(solution)/shard_map/reduce_scatter | solution.py:212
  1090.1 70.2 %reduce-scatter.26.cloned.1.call-done = bf16[2,256,2048]{2,1,0:T(8,128)(2,1)} async-done(((bf16[2,1024,2048]{2,1,0:T(8,128)(2,1)}), bf16[2,256,2048]{2,1,0:T(8,128)(2,1)}) %reduce-scatter.26.cloned.1.call-update) | async-done | bytes 2097168 | tf_op jit(solution)/shard_map/reduce_scatter | solution.py:215
  1164.5 125.3 %all-reduce.7.cloned.1.call-done = f32[2048,16]{0,1:T(8,128)} async-done(((f32[2048,16]{0,1:T(8,128)}), f32[2048,16]{0,1:T(8,128)}) %all-reduce.7.cloned.1.call-update) | async-done | bytes 131088 | tf_op jit(solution)/shard_map/psum | solution.py:308
  1289.8 360.1 %reduce-scatter.20.cloned.1.call-done = f32[64,2048]{1,0:T(8,128)} async-done(((f32[2048,2048]{1,0:T(8,128)}), f32[64,2048]{1,0:T(8,128)}) %reduce-scatter.20.cloned.1.call-update) | async-done | bytes 524304 | tf_op jit(solution)/shard_map/reduce_scatter | solution.py:306
  1649.9 360.2 %reduce-scatter.14.cloned.1.call-done = f32[64,2048]{1,0:T(8,128)} async-done(((f32[2048,2048]{1,0:T(8,128)}), f32[64,2048]{1,0:T(8,128)}) %reduce-scatter.14.cloned.1.call-update) | async-done | bytes 524304 | tf_op jit(solution)/shard_map/reduce_scatter | solution.py:303
  2010.0 360.2 %reduce-scatter.16.cloned.1.call-done = f32[64,2048]{1,0:T(8,128)} async-done(((f32[2048,2048]{1,0:T(8,128)}), f32[64,2048]{1,0:T(8,128)}) %reduce-scatter.16.cloned.1.call-update) | async-done | bytes 524304 | tf_op jit(solution)/shard_map/reduce_scatter | solution.py:304
  2370.2 360.2 %reduce-scatter.18.cloned.1.call-done = f32[64,2048]{1,0:T(8,128)} async-done(((f32[2048,2048]{1,0:T(8,128)}), f32[64,2048]{1,0:T(8,128)}) %reduce-scatter.18.cloned.1.call-update) | async-done | bytes 524304 | tf_op jit(solution)/shard_map/reduce_scatter | solution.py:305
  (238 shorter events, 202.3 us)
Async XLA Ops:
  7.2 389.5 %copy-start = (bf16[2048,16]{0,1:T(8,128)(2,1)S(1)}, bf16[2048,16]{0,1:T(8,128)(2,1)}, u32[]{:S(2)}) copy-start(bf16[2048,16]{0,1:T(8,128)(2,1)} %param.27) | copy-start | bytes 196612
  7.2 84.0 %all-gather.11.cloned.1.call-start = ((), (), s32[]{:S(2)}) async-start(), calls=%async_computation.15 | async-start | bytes 8650752 | tf_op jit(solution)/shard_map/all_gather | solution.py:92
  7.9 162.2 %all-gather.13.cloned.1.call-start = ((), (), s32[]{:S(2)}) async-start(), calls=%async_computation.16 | async-start | bytes 8650752 | tf_op jit(solution)/shard_map/all_gather | solution.py:93
  8.7 240.5 %all-gather.7.cloned.1.call-start = ((), (), s32[]{:S(2)}) async-start(), calls=%async_computation.13 | async-start | bytes 8650752 | tf_op jit(solution)/shard_map/all_gather | solution.py:94
  9.4 263.2 %all-gather.15.cloned.1.call-start = ((), (), s32[]{:S(2)}) async-start(), calls=%async_computation.17 | async-start | bytes 2621440 | tf_op jit(solution)/shard_map/all_gather | solution.py:108
  12.4 83.7 %copy-start.40 = (f32[128]{0:T(128)}, f32[128]{0:T(128)S(1)}, u32[]{:S(2)}) copy-start(f32[128]{0:T(128)S(1)} %fusion.73) | copy-start | bytes 1540
  12.4 236.8 %copy-start.28 = (f32[128]{0:T(128)}, f32[128]{0:T(128)S(1)}, u32[]{:S(2)}) copy-start(f32[128]{0:T(128)S(1)} %fusion.101) | copy-start | bytes 1540
  12.7 164.3 %copy-start.24 = (f32[128,64]{1,0:T(8,128)}, f32[128,64]{1,0:T(8,128)S(1)}, u32[]{:S(2)}) copy-start(f32[128,64]{1,0:T(8,128)S(1)} %get-tuple-element.51) | copy-start | bytes 98308
  12.7 164.3 %copy-start.26 = (f32[128,64]{1,0:T(8,128)}, f32[128,64]{1,0:T(8,128)S(1)}, u32[]{:S(2)}) copy-start(f32[128,64]{1,0:T(8,128)S(1)} %get-tuple-element.52) | copy-start | bytes 98308
  12.7 84.4 %copy-start.31 = (f32[2048]{0:T(1024)S(1)}, f32[2048]{0:T(1024)}, u32[]{:S(2)}) copy-start(f32[2048]{0:T(1024)} %param.23) | copy-start | bytes 24580
  96.2 78.8 %copy-start.38 = (f32[128]{0:T(128)}, f32[128]{0:T(128)S(1)}, u32[]{:S(2)}) copy-start(f32[128]{0:T(128)S(1)} %fusion.102) | copy-start | bytes 1540
  97.5 78.4 %copy-start.33 = (f32[2048]{0:T(1024)S(1)}, f32[2048]{0:T(1024)}, u32[]{:S(2)}) copy-start(f32[2048]{0:T(1024)} %param.24) | copy-start | bytes 24580
  178.4 94.3 %copy-start.11 = (bf16[128,16,64]{2,0,1:T(8,128)(2,1)}, bf16[128,16,64]{2,0,1:T(8,128)(2,1)S(1)}, u32[]{:S(2)}) copy-start(bf16[128,16,64]{2,0,1:T(8,128)(2,1)S(1)} %get-tuple-element.33) | copy-start | bytes 786436
  178.4 94.3 %copy-start.13 = (bf16[128,16,64]{2,0,1:T(8,128)(2,1)}, bf16[128,16,64]{2,0,1:T(8,128)(2,1)S(1)}, u32[]{:S(2)}) copy-start(bf16[128,16,64]{2,0,1:T(8,128)(2,1)S(1)} %get-tuple-element.34) | copy-start | bytes 786436
  179.7 117.5 %all-gather.9.cloned.1.call-start = ((), (), s32[]{:S(2)}) async-start(), calls=%async_computation.14 | async-start | bytes 2621440 | tf_op jit(solution)/shard_map/all_gather | solution.py:109
  254.7 122.9 %all-gather.17.cloned.1.call-start = ((), (), s32[]{:S(2)}) async-start(), calls=%async_computation.18 | async-start | bytes 8650752 | tf_op jit(solution)/shard_map/all_gather | solution.py:95
  301.6 80.7 %copy-start.18 = (bf16[16,128,128]{2,1,0:T(8,128)(2,1)}, bf16[16,128,128]{2,1,0:T(8,128)(2,1)S(1)}, u32[]{:S(2)}) copy-start(bf16[16,128,128]{2,1,0:T(8,128)(2,1)S(1)} %fusion.55) | copy-start | bytes 1572868
  391.6 98.7 %all-to-all-start = ((bf16[8,2,64,2048]{3,2,1,0:T(8,128)(2,1)}), bf16[8,2,64,2048]{3,2,1,0:T(8,128)(2,1)}, u32[]{:S(2)}, u32[]{:S(2)}) async-start(bf16[8,2,64,2048]{3,2,1,0:T(8,128)(2,1)} %bitcast.295), calls=%async_computation | async-start | bytes 8388608 | tf_op jit(solution)/shard_map/all_to_all | solution.py:162
  490.3 97.6 %all-to-all-start.2 = ((bf16[8,2,64,2048]{3,2,1,0:T(8,128)(2,1)}), bf16[8,2,64,2048]{3,2,1,0:T(8,128)(2,1)}, u32[]{:S(2)}, u32[]{:S(2)}) async-start(bf16[8,2,64,2048]{3,2,1,0:T(8,128)(2,1)} %bitcast.296), calls=%async_computation.2 | async-start | bytes 8388608 | tf_op jit(solution)/shard_map/all_to_all | solution.py:177
  633.4 97.1 %all-to-all-start.3 = ((bf16[8,2,64,2048]{3,2,1,0:T(8,128)(2,1)}), bf16[8,2,64,2048]{3,2,1,0:T(8,128)(2,1)}, u32[]{:S(2)}, u32[]{:S(2)}) async-start(bf16[8,2,64,2048]{3,2,1,0:T(8,128)(2,1)} %copy.119), calls=%async_computation.3 | async-start | bytes 8388608 | tf_op jit(solution)/shard_map/all_to_all | solution.py:206
  730.5 97.1 %all-to-all-start.1 = ((bf16[8,2,64,2048]{3,2,1,0:T(8,128)(2,1)}), bf16[8,2,64,2048]{3,2,1,0:T(8,128)(2,1)}, u32[]{:S(2)}, u32[]{:S(2)}) async-start(bf16[8,2,64,2048]{3,2,1,0:T(8,128)(2,1)} %copy.117), calls=%async_computation.1 | async-start | bytes 8388608 | tf_op jit(solution)/shard_map/all_to_all | solution.py:169
  735.1 193.6 %reduce-scatter.28.cloned.1.call-start = ((), (), s32[]{:S(2)}) async-start(), calls=%async_computation.27 | async-start | bytes 2621440
  871.3 92.8 %reduce-scatter.30.cloned.1.call-start = ((), (), s32[]{:S(2)}) async-start(), calls=%async_computation.28 | async-start | bytes 2621440
  880.5 149.5 %reduce-scatter.22.cloned.1.call-start = ((), (), s32[]{:S(2)}) async-start(), calls=%async_computation.24 | async-start | bytes 10485760 | tf_op jit(solution)/shard_map/reduce_scatter | solution.py:209
  891.5 194.5 %reduce-scatter.24.cloned.1.call-start = ((), (), s32[]{:S(2)}) async-start(), calls=%async_computation.25 | async-start | bytes 10485760 | tf_op jit(solution)/shard_map/reduce_scatter | solution.py:212
  902.4 258.0 %reduce-scatter.26.cloned.1.call-start = ((), (), s32[]{:S(2)}) async-start(), calls=%async_computation.26 | async-start | bytes 10485760 | tf_op jit(solution)/shard_map/reduce_scatter | solution.py:215
  913.5 376.3 %all-reduce.7.cloned.1.call-start = ((), (), s32[]{:S(2)}) async-start(), calls=%async_computation.23 | async-start | bytes 262144 | tf_op jit(solution)/shard_map/psum | solution.py:308
  915.5 734.4 %reduce-scatter.20.cloned.1.call-start = ((), (), s32[]{:S(2)}) async-start(), calls=%async_computation.22 | async-start | bytes 17301504 | tf_op jit(solution)/shard_map/reduce_scatter | solution.py:306
  924.8 1085.2 %reduce-scatter.14.cloned.1.call-start = ((), (), s32[]{:S(2)}) async-start(), calls=%async_computation.19 | async-start | bytes 17301504 | tf_op jit(solution)/shard_map/reduce_scatter | solution.py:303
  947.8 1422.4 %reduce-scatter.16.cloned.1.call-start = ((), (), s32[]{:S(2)}) async-start(), calls=%async_computation.20 | async-start | bytes 17301504 | tf_op jit(solution)/shard_map/reduce_scatter | solution.py:304
  963.8 1766.6 %reduce-scatter.18.cloned.1.call-start = ((), (), s32[]{:S(2)}) async-start(), calls=%async_computation.21 | async-start | bytes 17301504 | tf_op jit(solution)/shard_map/reduce_scatter | solution.py:305
  1086.0 1645.9 %copy-start.1 = (bf16[2048,16]{0,1:T(8,128)(2,1)S(1)}, bf16[2048,16]{0,1:T(8,128)(2,1)}, u32[]{:S(2)}) copy-start(bf16[2048,16]{0,1:T(8,128)(2,1)} %param.27) | copy-start | bytes 196612
  (36 other events, 389.2 us)
Sparse Core Ops, SparseCore 0:
  11.0 80.0 all-gather.10
  94.1 75.9 all-gather.12
  173.1 75.9 all-gather.6
  251.2 21.4 all-gather.14
  274.6 22.5 all-gather.8
  300.1 77.4 all-gather.16
  871.4 30.3 reduce-scatter.27
  905.1 31.4 reduce-scatter.29
  939.2 72.4 reduce-scatter.21
  1014.3 71.7 reduce-scatter.23
  1088.6 71.7 reduce-scatter.25
  1167.3 122.4 all-reduce.6
  1292.7 357.1 reduce-scatter.19
  1652.7 357.2 reduce-scatter.13
  2012.9 357.3 reduce-scatter.15
  2373.0 357.3 reduce-scatter.17
where the time goes:
time: 2750 us; the launch traced here: 2740 us
  waiting for transfers between devices  2330 us (85%)
  matrix products  218 us (8%)
  local copies, waits for them, and re-layouts  62.8 us (2%)
  other arithmetic  54.2 us (2%)
  blocking collectives  39.2 us (1%)
    reduce_scatter x1, waiting for transfers between devices, local(): lax.psum_scatter(grad_w_value, ('seq', 'expert'), scatter_dimension=0, ti...  360 us
    reduce_scatter x1, waiting for transfers between devices, local(): lax.psum_scatter(grad_w_key, ('seq', 'expert'), scatter_dimension=0, tile...  360 us
    reduce_scatter x1, waiting for transfers between devices, local(): lax.psum_scatter(grad_w_query, ('seq', 'expert'), scatter_dimension=0, ti...  360 us
    reduce_scatter x1, waiting for transfers between devices, local(): lax.psum_scatter(grad_w_out, ('seq', 'expert'), scatter_dimension=0, tile...  360 us
    psum x1, waiting for transfers between devices, local(): lax.psum((grad_gain_attn, grad_gain_query, grad_gain_key, grad_gain_mlp,...  125 us
    all_to_all x1, waiting for transfers between devices, local(): lax.all_to_all(send_rows, 'expert', split_axis=0, concat_axis=0, tiled=True)  83.3 us
    all_to_all x1, waiting for transfers between devices, local(): lax.all_to_all(grad_routed, 'expert', split_axis=0, concat_axis=0, tiled=...  81.7 us
    all_gather x1, waiting for transfers between devices, local(): lax.all_gather(w_query, ('seq', 'expert'), axis=0, tiled=True)  78.4 us
  transfers between devices with their start and end apart: 20, of which 17 were waited for; matrix products, arithmetic and copies ran while one was open for 8% of the time, Pallas kernels for 0%

commit v1 on v0

v1 whole, which is shorter than its diff:
```python
from functools import partial

import jax
import jax.numpy as jnp
from jax import lax
from jax.sharding import PartitionSpec as P

HEADS = 16
MOST = 64
BF = jnp.bfloat16
F32 = jnp.float32

norm_eps = 1e-05
masked_score = -1e30


def product(left, right):
    return jnp.dot(left, right, preferred_element_type=F32)


def rms_norm(values, norm_gain):
    return (
        values * lax.rsqrt(jnp.mean(values * values, axis=-1, keepdims=True) + norm_eps) * norm_gain
    )


def swap(value, axis):
    n = lax.axis_size(axis)
    return lax.ppermute(value, axis, [(i, i ^ 1) for i in range(n)])


def shift(value, axis):
    n = lax.axis_size(axis)
    return lax.ppermute(value, axis, [(i, (i + 2) % n) for i in range(n)])


def flip(value, axis, delta):
    n = lax.axis_size(axis)
    return lax.ppermute(value, axis, [(i, i ^ delta) for i in range(n)])


def owners(axis):
    n = lax.axis_size(axis)
    me = lax.axis_index(axis)
    outer, inner = me // 2, me % 2
    return [((outer - i) % (n // 2)) * 2 + (inner ^ b) for i in range(n // 2) for b in range(2)]


def gather_blocks(value, axis):
    blocks = []
    current = value
    for i in range(lax.axis_size(axis) // 2):
        if i:
            current = shift(current, axis)
        blocks += [current, swap(current, axis)]
    return blocks


def add_low(left, right):
    return (left.astype(F32) + right.astype(F32)).astype(BF)


def scatter_sum(blocks, axis):
    outer_count = lax.axis_size(axis) // 2
    pairs = {}
    for t in list(range(1, outer_count)) + [0]:
        arrived = swap(blocks[2 * t + 1], axis)
        pairs[t] = blocks[2 * t].astype(F32) + arrived.astype(F32)
    total = pairs[1 % outer_count]
    for t in range(1, outer_count):
        arrived = shift(total.astype(BF), axis)
        total = arrived.astype(F32) + pairs[(t + 1) % outer_count]
    return total


def all_sum(value, axes):
    for axis in axes:
        delta = 1
        while delta < lax.axis_size(axis):
            value = value + flip(value, axis, delta)
            delta *= 2
    return value


def exchange(parts, axis):
    n = lax.axis_size(axis)
    me = lax.axis_index(axis)
    out = parts
    for delta in range(1, n):
        other = me ^ delta
        got = flip(lax.dynamic_index_in_dim(parts, other, 0, keepdims=False), axis, delta)
        out = lax.dynamic_update_index_in_dim(out, got, other, 0)
    return out


def after(value, *others):
    return lax.optimization_barrier((value,) + others)[0]


def local(
    tokens,
    lengths,
    routes,
    gain_attn,
    w_query,
    w_key,
    w_value,
    gain_query,
    gain_key,
    w_out,
    gain_mlp,
    router,
    w_gate,
    w_up,
    w_down,
    cotangent,
):
    seq_count = lax.axis_size("seq")
    group_count = lax.axis_size("expert")
    seq_me = lax.axis_index("seq")
    group_me = lax.axis_index("expert")
    tok_rows, width = tokens.shape[1], tokens.shape[2]
    head_dim = width // HEADS
    heads = HEADS // seq_count
    cols = width // seq_count
    wrows = w_query.shape[0]
    length = tok_rows * seq_count
    experts_local = w_gate.shape[0]
    total_experts = experts_local * group_count
    slots = MOST
    score_scale = head_dim ** (-0.5)
    inputs = tokens[0].astype(F32)

    seq_owners = jnp.stack(owners("seq"))
    places = (seq_owners[:, None] * tok_rows + jnp.arange(tok_rows)[None, :]).reshape(length)
    doc_ends = jnp.cumsum(lengths[0])
    passed = (places[:, None] >= doc_ends[None, :]).astype(jnp.int32)
    docs = jnp.sum(passed, axis=1)
    offsets = places - jnp.sum(passed * lengths[0][None, :], axis=1)
    allowed = (docs[:, None] == docs[None, :]) & (places[None, :] <= places[:, None])
    half = head_dim // 2
    inverse = 10000.0 ** (-jnp.arange(half, dtype=F32) / half)
    angles = offsets.astype(F32)[:, None] * inverse[None, :]
    cosine = jnp.cos(angles)[:, None, :]
    sine = jnp.sin(angles)[:, None, :]

    def turn(values, sine_table):
        first, second = values[..., :half], values[..., half:]
        return jnp.concatenate(
            [first * cosine - second * sine_table, second * cosine + first * sine_table], axis=-1
        )

    w_three = jnp.stack([w_query, w_key, w_value], axis=1)
    w_parts = w_three.reshape(wrows, 3, seq_count, cols).transpose(2, 0, 1, 3)
    w_mine = exchange(w_parts.reshape(seq_count, wrows, 3 * cols), "seq")
    group_owners = owners("expert")
    w_blocks = gather_blocks(w_mine, "expert")
    w_cols = jnp.zeros((seq_count, group_count, wrows, 3 * cols), BF)
    for owner, block in zip(group_owners, w_blocks):
        w_cols = lax.dynamic_update_slice(w_cols, block[:, None], (0, owner, 0, 0))
    w_cols = w_cols.reshape(width, 3 * cols)
    out_blocks = gather_blocks(after(w_out, w_blocks[-1]), "expert")
    w_rows = jnp.zeros((group_count, wrows, width), BF)
    for owner, block in zip(group_owners, out_blocks):
        w_rows = lax.dynamic_update_slice(w_rows, block[None], (owner, 0, 0))
    w_rows = w_rows.reshape(cols, width)

    normed, attn_norm_back = jax.vjp(rms_norm, inputs, gain_attn)
    normed_all = jnp.concatenate(gather_blocks(normed.astype(BF), "seq"), axis=0)
    raw = product(normed_all, w_cols)
    query_raw, key_raw = raw[:, :cols], raw[:, cols : 2 * cols]
    value_low = raw[:, 2 * cols :].astype(BF).reshape(length, heads, head_dim)

    def row_sums(left, right):
        sums = jnp.stack([jnp.sum(left, axis=1), jnp.sum(right, axis=1)])
        sums = sums.reshape(2, seq_count, tok_rows)
        ordered = jnp.zeros_like(sums).at[:, seq_owners].set(sums)
        return lax.psum(ordered, "seq")[:, seq_owners].reshape(2, length) / width

    inv_rms = lax.rsqrt(row_sums(query_raw**2, key_raw**2) + norm_eps)
    gain_q = lax.dynamic_slice_in_dim(gain_query, seq_me * cols, cols)
    gain_k = lax.dynamic_slice_in_dim(gain_key, seq_me * cols, cols)
    query_unit = query_raw * inv_rms[0][:, None]
    key_unit = key_raw * inv_rms[1][:, None]
    query_low = turn((query_unit * gain_q).reshape(length, heads, head_dim), sine).astype(BF)
    key_low = turn((key_unit * gain_k).reshape(length, heads, head_dim), sine).astype(BF)
    scores = jnp.einsum("qhd,khd->hqk", query_low, key_low, preferred_element_type=F32)
    scores = jnp.where(allowed[None], scores * score_scale, masked_score)
    top_score = jnp.max(scores, axis=-1, keepdims=True)
    weights = jnp.exp(scores - top_score)
    probs = weights / jnp.sum(weights, axis=-1, keepdims=True)
    probs_low = probs.astype(BF)
    attended = jnp.einsum("hqk,khd->qhd", probs_low, value_low, preferred_element_type=F32)
    attended_low = attended.reshape(length, cols).astype(BF)
    hidden_parts = product(attended_low, w_rows).astype(BF).reshape(seq_count, tok_rows, width)
    hidden = inputs + scatter_sum([hidden_parts[i] for i in range(seq_count)], "seq")

    normed2, mlp_norm_back = jax.vjp(rms_norm, hidden, gain_mlp)
    normed2_low = normed2.astype(BF)

    order = jnp.stack(group_owners)
    picks = lax.all_gather(routes[0], "expert", axis=0)[order]
    first_expert = group_me * experts_local
    local_ids = first_expert + jnp.arange(experts_local, dtype=jnp.int32)
    hit = jnp.any(picks[:, None, :, :] == local_ids[None, :, None, None], axis=-1)
    before = (jnp.arange(tok_rows)[:, None] < jnp.arange(tok_rows)[None, :]).astype(BF)
    rank = jnp.einsum("ejt,tu->eju", hit.astype(BF), before, preferred_element_type=F32)
    slot_ids = jnp.arange(slots, dtype=jnp.int32)
    chosen = hit[:, :, None, :] & (rank.astype(jnp.int32)[:, :, None, :] == slot_ids[None, None, :, None])
    chosen_low = chosen.astype(BF)

    normed2_all = jnp.stack(gather_blocks(normed2_low, "expert"))
    cot_all = jnp.stack(gather_blocks(after(cotangent[0], out_blocks[-1]), "expert"))
    logits_all = jnp.einsum("etd,dn->etn", normed2_all, router, preferred_element_type=F32)
    probs_all = jax.nn.softmax(logits_all, axis=-1)
    mine = lax.dynamic_slice_in_dim(probs_all, first_expert, experts_local, axis=2)
    gate_rows = jnp.einsum(
        "ejmt,etj->jem", chosen.astype(F32), mine, precision=lax.Precision.HIGHEST
    )[..., None]

    def pick_rows(values):
        return jnp.einsum("ejmt,etd->jemd", chosen_low, values, preferred_element_type=F32).astype(BF)

    def place_rows(values):
        return jnp.einsum("ejmt,jemd->etd", chosen_low, values, preferred_element_type=F32).astype(BF)

    routed = pick_rows(normed2_all)
    cot_rows = pick_rows(cot_all)

    def each(left, right, how):
        return jnp.einsum(how, left, right, preferred_element_type=F32)

    gate_pre = each(routed, w_gate, "jemd,jdf->jemf")
    up_pre = each(routed, w_up, "jemd,jdf->jemf")
    sigmoid_gate = jax.nn.sigmoid(gate_pre)
    silu_gate = gate_pre * sigmoid_gate
    active = silu_gate * up_pre
    active_low = active.astype(BF)
    grad_unit = each(cot_rows, w_down, "jemd,jfd->jemf")
    grad_gate_rows = jnp.sum(grad_unit * active_low.astype(F32), axis=-1)
    grad_active = grad_unit * gate_rows
    grad_gate_low = (
        grad_active * up_pre * sigmoid_gate * (1.0 + gate_pre * (1.0 - sigmoid_gate))
    ).astype(BF)
    grad_up_low = (grad_active * silu_gate).astype(BF)
    grad_routed = each(grad_gate_low, w_gate, "jemf,jdf->jemd")
    grad_routed = (grad_routed + each(grad_up_low, w_up, "jemf,jdf->jemd")).astype(BF)
    grad_parts = place_rows(grad_routed)
    grad_normed2 = scatter_sum([grad_parts[i] for i in range(group_count)], "expert")
    grad_probs_parts = jnp.einsum(
        "ejmt,jem->etj", chosen.astype(F32), grad_gate_rows, precision=lax.Precision.HIGHEST
    )
    to_owner = jnp.zeros_like(grad_probs_parts).at[order].set(grad_probs_parts)
    grad_probs = lax.all_to_all(to_owner, "expert", split_axis=0, concat_axis=0, tiled=True)
    grad_probs = grad_probs.transpose(1, 0, 2).reshape(tok_rows, total_experts)

    expert_out = each(active_low, w_down, "jemf,jfd->jemd") * gate_rows
    out_parts = place_rows(expert_out.astype(BF))
    out_parts = after(out_parts, grad_normed2)
    mixed = hidden + scatter_sum([out_parts[i] for i in range(group_count)], "expert")

    active_scaled = (active_low.astype(F32) * gate_rows).astype(BF)

    def expert_grad(left, right):
        grad = jnp.einsum("jemd,jemf->jdf", left, right, preferred_element_type=F32).astype(BF)
        rows = grad.shape[1] // seq_count
        grad = grad.reshape(experts_local, seq_count, rows, grad.shape[2])
        return scatter_sum(
            [lax.dynamic_index_in_dim(grad, o, 1, keepdims=False) for o in owners("seq")], "seq"
        )

    d_w_gate = expert_grad(routed, grad_gate_low)
    d_w_up = expert_grad(routed, grad_up_low)
    d_w_down = expert_grad(active_scaled, cot_rows)

    router_probs, softmax_back = jax.vjp(
        partial(jax.nn.softmax, axis=-1), product(normed2_low, router)
    )
    (grad_logits,) = softmax_back(grad_probs)
    grad_logits_low = grad_logits.astype(BF)
    grad_router = jnp.einsum("td,te->ed", normed2_low, grad_logits_low, preferred_element_type=F32)
    grad_normed2 = grad_normed2 + jnp.einsum(
        "te,de->td", grad_logits_low, router, preferred_element_type=F32
    )
    grad_hidden_part, grad_gain_mlp = mlp_norm_back(grad_normed2)
    grad_hidden = cotangent[0].astype(F32) + grad_hidden_part

    grad_hidden_all = jnp.concatenate(gather_blocks(grad_hidden.astype(BF), "seq"), axis=0)
    grad_attended = jnp.einsum(
        "te,de->td", grad_hidden_all, w_rows, preferred_element_type=F32
    ).astype(BF)
    grad_attended = grad_attended.reshape(length, heads, head_dim)
    grad_w_out = jnp.einsum(
        "td,te->de", attended_low, grad_hidden_all, preferred_element_type=F32
    ).astype(BF).reshape(group_count, wrows, width)
    grad_probs_attn = jnp.einsum(
        "qhd,khd->hqk", grad_attended, value_low, preferred_element_type=F32
    )
    row_dot = jnp.sum(probs * grad_probs_attn, axis=-1, keepdims=True)
    grad_scores = (probs * (grad_probs_attn - row_dot)).astype(BF)
    grad_query = jnp.einsum("hqk,khd->qhd", grad_scores, key_low, preferred_element_type=F32)
    grad_key = jnp.einsum("hqk,qhd->khd", grad_scores, query_low, preferred_element_type=F32)
    grad_value = jnp.einsum("hqk,qhd->khd", probs_low, grad_attended, preferred_element_type=F32)
    grad_query = turn(grad_query * score_scale, -sine).reshape(length, cols)
    grad_key = turn(grad_key * score_scale, -sine).reshape(length, cols)
    grad_gain_query = jnp.sum(grad_query * query_unit, axis=0)
    grad_gain_key = jnp.sum(grad_key * key_unit, axis=0)
    grad_query_g, grad_key_g = grad_query * gain_q, grad_key * gain_k
    means = row_sums(grad_query_g * query_unit, grad_key_g * key_unit)
    grad_query_low = (
        inv_rms[0][:, None] * (grad_query_g - query_unit * means[0][:, None])
    ).astype(BF)
    grad_key_low = (inv_rms[1][:, None] * (grad_key_g - key_unit * means[1][:, None])).astype(BF)
    grad_value_low = grad_value.reshape(length, cols).astype(BF)
    grad_three = jnp.concatenate([grad_query_low, grad_key_low, grad_value_low], axis=1)
    grad_normed_parts = jnp.einsum(
        "te,de->td", grad_three, w_cols, preferred_element_type=F32
    ).astype(BF).reshape(seq_count, tok_rows, width)
    grad_normed = scatter_sum([grad_normed_parts[i] for i in range(seq_count)], "seq")
    grad_inputs_part, grad_gain_attn = attn_norm_back(grad_normed)
    d_tokens = grad_hidden + grad_inputs_part

    grad_w_three = jnp.einsum(
        "td,te->de", normed_all, grad_three, preferred_element_type=F32
    ).astype(BF).reshape(seq_count, group_count, wrows, 3 * cols)
    d_w_out = scatter_sum(
        [lax.dynamic_index_in_dim(grad_w_out, o, 0, keepdims=False) for o in group_owners], "expert"
    )
    d_three = scatter_sum(
        [lax.dynamic_index_in_dim(grad_w_three, o, 1, keepdims=False) for o in group_owners],
        "expert",
    )
    d_three = exchange(d_three.astype(BF), "seq")
    d_three = d_three.reshape(seq_count, wrows, 3, cols).transpose(2, 1, 0, 3)
    d_three = d_three.reshape(3, wrows, width).astype(F32)

    def full(value):
        return lax.dynamic_update_slice(jnp.zeros((width,), F32), value, (seq_me * cols,))

    axes = ("seq", "expert")
    early = all_sum(jnp.concatenate([grad_router, grad_gain_mlp[None]]), axes)
    late = all_sum(jnp.stack([full(grad_gain_query), full(grad_gain_key), grad_gain_attn]), axes)
    return (
        mixed.astype(BF)[None],
        d_tokens[None],
        late[2],
        d_three[0],
        d_three[1],
        d_three[2],
        late[0],
        late[1],
        d_w_out,
        early[total_experts],
        early[:total_experts].T,
        d_w_gate,
        d_w_up,
        d_w_down,
    )


def solution(mesh):
    return jax.shard_map(
        local,
        mesh=mesh,
        in_specs=(
            P("expert", "seq", None),
            P("expert", None),
            P("expert", "seq", None),
            P(),
            P(("seq", "expert"), None),
            P(("seq", "expert"), None),
            P(("seq", "expert"), None),
            P(),
            P(),
            P(("seq", "expert"), None),
            P(),
            P(),
            P("expert", None, None),
            P("expert", None, None),
            P("expert", None, None),
            P("expert", "seq", None),
        ),
        out_specs=(
            P("expert", "seq", None),
            P("expert", "seq", None),
            P(),
            P(("seq", "expert"), None),
            P(("seq", "expert"), None),
            P(("seq", "expert"), None),
            P(),
            P(),
            P(("seq", "expert"), None),
            P(),
            P(),
            P("expert", "seq", None),
            P("expert", "seq", None),
            P("expert", "seq", None),
        ),
        check_vma=False,
    )
```

time: 2750 us -> 848 us (0.31)
  waiting for transfers between devices: 2330 us -> 461 us
  matrix products: 218 us -> 136 us
  starting transfers between devices: 20.8 us -> 62 us
    reduce_scatter x7 -> x0, waiting for transfers between devices: 1560 us -> none  [the longest x1 360 us: local(): lax.psum_scatter(grad_w_value, ('seq', 'expert'), scatter_dimension=0, ti...]
    ppermute x0 -> x93, waiting for transfers between devices: none -> 461 us  [the longest x31 261 us: shift(): return lax.ppermute(value, axis, [(i, (i + 2) % n) for i in range(n)])]
    all_gather x6 -> x0, waiting for transfers between devices: 327 us -> none  [the longest x1 78.4 us: local(): lax.all_gather(w_query, ('seq', 'expert'), axis=0, tiled=True)]
    all_to_all x4 -> x1, waiting for transfers between devices: 312 us -> 0.01 us  [local(): lax.all_to_all(to_owner, 'expert', split_axis=0, concat_axis=0, tiled=True)]
    psum x1 -> x0, waiting for transfers between devices: 125 us -> none  [local(): lax.psum((grad_gain_attn, grad_gain_query, grad_gain_key, grad_gain_mlp,...]
    dot_general x33 -> x31, matrix products: 218 us -> 130 us  [the longest x6 65 us: each(): return jnp.einsum(how, left, right, preferred_element_type=F32)]
    ppermute x0 -> x93, starting transfers between devices: none -> 58.3 us  [the longest x46 36.2 us: swap(): return lax.ppermute(value, axis, [(i, i ^ 1) for i in range(n)])]
    all_gather x0 -> x1, blocking collectives: none -> 30.7 us  [local(): picks = lax.all_gather(routes[0], 'expert', axis=0)[order]]
  transfers between devices with their start and end apart: 20 -> 94, of which waited for: 17 -> 41; matrix products, arithmetic and copies ran while one was open for 8% -> 20% of each run, Pallas kernels for 0% -> 0%
where the time goes in v1:
time: 848 us; the launch traced here: 838 us
  waiting for transfers between devices  461 us (54%)
  matrix products  136 us (16%)
  other arithmetic  71.2 us (8%)
  starting transfers between devices  62 us (7%)
  local copies, waits for them, and re-layouts  58.6 us (7%)
  blocking collectives  46.5 us (5%)
    ppermute x31, waiting for transfers between devices, shift(): return lax.ppermute(value, axis, [(i, (i + 2) % n) for i in range(n)])  261 us
    ppermute x46, waiting for transfers between devices, swap(): return lax.ppermute(value, axis, [(i, i ^ 1) for i in range(n)])  124 us
    ppermute x16, waiting for transfers between devices, flip(): return lax.ppermute(value, axis, [(i, i ^ delta) for i in range(n)])  75.7 us
    dot_general x6, matrix products, each(): return jnp.einsum(how, left, right, preferred_element_type=F32)  65 us
    ppermute x46, starting transfers between devices, swap(): return lax.ppermute(value, axis, [(i, i ^ 1) for i in range(n)])  36.2 us
    all_gather x1, blocking collectives, local(): picks = lax.all_gather(routes[0], 'expert', axis=0)[order]  30.7 us
    convert_element_type x17, other arithmetic, scatter_sum(): arrived = shift(total.astype(BF), axis)  26.4 us
    dot_general x3, matrix products, expert_grad(): jnp.einsum('jemd,jemf->jdf', left, right, preferred_element_type=F32)  23.2 us
  transfers between devices with their start and end apart: 94, of which 41 were waited for; matrix products, arithmetic and copies ran while one was open for 20% of the time, Pallas kernels for 0%

profile of v1, /device:TPU:0, one launch (start us, length us, event | category | flops | bytes accessed | tf_op | source)
XLA Modules:
  0.0 837.8 jit_solution(13236968989732719062)
XLA Ops:
  14.5 30.7 %all_gather.3 = s32[8,128,8]{1,2,0:T(8,128)S(1)} all-gather(s32[1,128,8]{1,2,0:T(8,128)S(1)} %copy-done.62), channel_id=1, replica_groups=mesh['seq'=4,'expert'=8] {'expert'}, dimensions={0}, use_global_device_ids=true | all-gather | bytes 36864 | tf_op jit(solution)/shard_map/all_gather | solution.py:202
  61.6 18.6 %collective-permute-done.7 = bf16[4,64,1536]{2,1,0:T(8,128)(2,1)S(1)} collective-permute-done((bf16[4,64,1536]{2,1,0:T(8,128)(2,1)S(1)}, bf16[4,64,1536]{2,1,0:T(8,128)(2,1)S(1)}, u32[]{:S(2)}, u32[]{:S(2)}) %collective-permute-start.7) | collective-permute-done | bytes 786464 | tf_op jit(solution)/shard_map/ppermute | solution.py:34
  80.8 20.7 %collective-permute-done.9 = bf16[4,64,1536]{2,1,0:T(8,128)(2,1)S(1)} collective-permute-done((bf16[4,64,1536]{2,1,0:T(8,128)(2,1)S(1)}, bf16[4,64,1536]{2,1,0:T(8,128)(2,1)S(1)}, u32[]{:S(2)}, u32[]{:S(2)}) %collective-permute-start.9) | collective-permute-done | bytes 786464 | tf_op jit(solution)/shard_map/ppermute | solution.py:34
  103.2 19.5 %collective-permute-done.11 = bf16[4,64,1536]{2,1,0:T(8,128)(2,1)S(1)} collective-permute-done((bf16[4,64,1536]{2,1,0:T(8,128)(2,1)S(1)}, bf16[4,64,1536]{2,1,0:T(8,128)(2,1)S(1)}, u32[]{:S(2)}, u32[]{:S(2)}) %collective-permute-start.11) | collective-permute-done | bytes 786464 | tf_op jit(solution)/shard_map/ppermute | solution.py:34
  123.3 16.8 %collective-permute-done.12 = bf16[4,64,1536]{2,1,0:T(8,128)(2,1)S(1)} collective-permute-done((bf16[4,64,1536]{2,1,0:T(8,128)(2,1)S(1)}, bf16[4,64,1536]{2,1,0:T(8,128)(2,1)S(1)}, u32[]{:S(2)}, u32[]{:S(2)}) %collective-permute-start.12) | collective-permute-done | bytes 786464 | tf_op jit(solution)/shard_map/ppermute | solution.py:29
  178.7 8.1 collective-permute-done.16
  187.3 8.5 %collective-permute-done.18 = bf16[64,2048]{1,0:T(8,128)(2,1)S(1)} collective-permute-done((bf16[64,2048]{1,0:T(8,128)(2,1)S(1)}, bf16[64,2048]{1,0:T(8,128)(2,1)S(1)}, u32[]{:S(2)}, u32[]{:S(2)}) %collective-permute-start.18) | collective-permute-done | bytes 262176 | tf_op jit(solution)/shard_map/ppermute | solution.py:34
  210.9 13.1 %collective-permute-done.31 = bf16[128,2048]{1,0:T(8,128)(2,1)S(1)} collective-permute-done((bf16[128,2048]{1,0:T(8,128)(2,1)S(1)}, bf16[128,2048]{1,0:T(8,128)(2,1)S(1)}, u32[]{:S(2)}, u32[]{:S(2)}) %collective-permute-start.31) | collective-permute-done | bytes 524320 | tf_op jit(solution)/shard_map/ppermute | solution.py:34
  227.8 13.3 %collective-permute-done.33 = bf16[128,2048]{1,0:T(8,128)(2,1)S(1)} collective-permute-done((bf16[128,2048]{1,0:T(8,128)(2,1)S(1)}, bf16[128,2048]{1,0:T(8,128)(2,1)S(1)}, u32[]{:S(2)}, u32[]{:S(2)}) %collective-permute-start.33) | collective-permute-done | bytes 524320 | tf_op jit(solution)/shard_map/ppermute | solution.py:34
  243.1 9.3 %collective-permute-done.24 = bf16[128,2048]{1,0:T(8,128)(2,1)S(1)} collective-permute-done((bf16[128,2048]{1,0:T(8,128)(2,1)S(1)}, bf16[128,2048]{1,0:T(8,128)(2,1)S(1)}, u32[]{:S(2)}, u32[]{:S(2)}) %collective-permute-start.24) | collective-permute-done | bytes 524320 | tf_op jit(solution)/shard_map/ppermute | solution.py:34
  253.9 9.7 %collective-permute-done.35 = bf16[128,2048]{1,0:T(8,128)(2,1)S(1)} collective-permute-done((bf16[128,2048]{1,0:T(8,128)(2,1)S(1)}, bf16[128,2048]{1,0:T(8,128)(2,1)S(1)}, u32[]{:S(2)}, u32[]{:S(2)}) %collective-permute-start.35) | collective-permute-done | bytes 524320 | tf_op jit(solution)/shard_map/ppermute | solution.py:34
  274.5 9.3 %collective-permute-done.36 = bf16[128,2048]{1,0:T(8,128)(2,1)S(1)} collective-permute-done((bf16[128,2048]{1,0:T(8,128)(2,1)S(1)}, bf16[128,2048]{1,0:T(8,128)(2,1)S(1)}, u32[]{:S(2)}, u32[]{:S(2)}) %collective-permute-start.36) | collective-permute-done | bytes 524320 | tf_op jit(solution)/shard_map/ppermute | solution.py:29
  295.1 9.5 %collective-permute-done.29 = bf16[128,2048]{1,0:T(8,128)(2,1)S(1)} collective-permute-done((bf16[128,2048]{1,0:T(8,128)(2,1)S(1)}, bf16[128,2048]{1,0:T(8,128)(2,1)S(1)}, u32[]{:S(2)}, u32[]{:S(2)}) %collective-permute-start.29) | collective-permute-done | bytes 524320 | tf_op jit(solution)/shard_map/ppermute | solution.py:29
  313.6 9.4 %fusion.5 = f32[2,8,64,1024]{3,2,1,0:T(8,128)} fusion(bf16[2,2048,1024]{2,1,0:T(8,128)(2,1)} %param.28, bf16[2,8,64,2048]{3,2,0,1:T(8,128)(2,1)S(1)} %convert_bitcast_fusion.1), kind=kOutput, calls=%fused_computation.14 | convolution fusion | flops 4294967296 | bytes 16777216 | tf_op jit(solution)/shard_map/jemd,jdf->jemf/dot_general | solution.py:231
  323.5 13.0 %fusion.17 = (f32[2,8,64]{2,1,0:T(8,128)S(1)}, bf16[2,8,64,1024]{3,2,1,0:T(8,128)(2,1)}, bf16[2,8,64,1024]{3,2,1,0:T(8,128)(2,1)}, bf16[2,8,64,1024]{3,2,1,0:T(8,128)(2,1)}) fusion(f32[2,8,64,1024]{3,2,1,0:T(8,128)} %fusion.3, f32[2,8,64,1024]{3,2,1,0:T(8,128)} %fusion.5, f32[2,8,64]{2,1,0:T(8,128)S(1)} %bitcast.538, bf16[2,1024,2048]{2,1,0:T(8,128)(2,1)} %param.30, ...), kind=kOutput, calls=%fused_computation.29 | convolution fusion | flops 4314889216 | bytes 27271168 | tf_op jit(solution)/shard_map/jemd,jfd->jemf/dot_general | solution.py:231
  336.6 12.1 %fusion.9 = f32[2,8,64,2048]{3,2,0,1:T(8,128)} fusion(bf16[2,2048,1024]{2,1,0:T(8,128)(2,1)} %param.29, bf16[2,8,64,1024]{3,2,1,0:T(8,128)(2,1)} %get-tuple-element.49), kind=kOutput, calls=%fused_computation.20 | convolution fusion | flops 4294967296 | bytes 18874368 | tf_op jit(solution)/shard_map/jemf,jdf->jemd/dot_general | solution.py:231
  348.6 8.8 %bitcast_convert_fusion.1 = bf16[2,2048,1024]{2,1,0:T(8,128)(2,1)} fusion(bf16[2,8,64,2048]{3,2,0,1:T(8,128)(2,1)S(1)} %copy-done.18, bf16[2,8,64,1024]{3,2,1,0:T(8,128)(2,1)} %get-tuple-element.49), kind=kOutput, calls=%fused_computation.8 | convolution fusion | flops 4299161600 | bytes 14680064 | tf_op jit(solution)/shard_map/jemd,jemf->jdf/dot_general | solution.py:265
  364.2 12.9 %add_convert_fusion = bf16[2,8,64,2048]{3,2,0,1:T(8,128)(2,1)} fusion(f32[2,8,64,2048]{3,2,0,1:T(8,128)} %fusion.9, bf16[2,2048,1024]{2,1,0:T(8,128)(2,1)} %param.28, bf16[2,8,64,1024]{3,2,1,0:T(8,128)(2,1)} %get-tuple-element.42), kind=kOutput, calls=%fused_computation.24 | convolution fusion | flops 4299161600 | bytes 23068672 | tf_op jit(solution)/shard_map/jemf,jdf->jemd/dot_general | solution.py:231
  394.8 7.6 bitcast_convert_fusion
  402.4 11.1 %multiply_convert_fusion = bf16[2,8,64,2048]{3,2,0,1:T(8,128)(2,1)S(1)} fusion(bf16[2,1024,2048]{2,1,0:T(8,128)(2,1)} %param.30, f32[2,8,64]{2,0,1:T(2,128)S(1)} %copy.248, bf16[2,8,64,1024]{3,2,1,0:T(8,128)(2,1)S(1)} %copy-done.77), kind=kOutput, calls=%fused_computation.25 | convolution fusion | flops 4299161600 | bytes 14684160 | tf_op jit(solution)/shard_map/jemf,jfd->jemd/dot_general | solution.py:231
  421.0 9.3 %collective-permute-done.37 = bf16[128,2048]{1,0:T(8,128)(2,1)S(1)} collective-permute-done((bf16[128,2048]{1,0:T(8,128)(2,1)}, bf16[128,2048]{1,0:T(8,128)(2,1)S(1)}, u32[]{:S(2)}, u32[]{:S(2)}) %collective-permute-start.37) | collective-permute-done | bytes 524320 | tf_op jit(solution)/shard_map/ppermute | solution.py:29
  447.3 12.1 %collective-permute-done.40 = bf16[128,2048]{1,0:T(8,128)(2,1)S(1)} collective-permute-done((bf16[128,2048]{1,0:T(8,128)(2,1)}, bf16[128,2048]{1,0:T(8,128)(2,1)S(1)}, u32[]{:S(2)}, u32[]{:S(2)}) %collective-permute-start.40) | collective-permute-done | bytes 524320 | tf_op jit(solution)/shard_map/ppermute | solution.py:34
  465.4 11.7 %collective-permute-done.42 = bf16[128,2048]{1,0:T(8,128)(2,1)S(1)} collective-permute-done((bf16[128,2048]{1,0:T(8,128)(2,1)S(1)}, bf16[128,2048]{1,0:T(8,128)(2,1)S(1)}, u32[]{:S(2)}, u32[]{:S(2)}) %collective-permute-start.42) | collective-permute-done | bytes 524320 | tf_op jit(solution)/shard_map/ppermute | solution.py:34
  482.9 15.0 %collective-permute-done.80 = f32[17,2048]{1,0:T(8,128)S(1)} collective-permute-done((f32[17,2048]{1,0:T(8,128)S(1)}, f32[17,2048]{1,0:T(8,128)S(1)}, u32[]{:S(2)}, u32[]{:S(2)}) %collective-permute-start.80) | collective-permute-done | bytes 139296 | tf_op jit(solution)/shard_map/ppermute | solution.py:39
  504.6 11.1 %collective-permute-done.81 = f32[17,2048]{1,0:T(8,128)S(1)} collective-permute-done((f32[17,2048]{1,0:T(8,128)S(1)}, f32[17,2048]{1,0:T(8,128)S(1)}, u32[]{:S(2)}, u32[]{:S(2)}) %collective-permute-start.81) | collective-permute-done | bytes 139296 | tf_op jit(solution)/shard_map/ppermute | solution.py:39
  523.8 11.2 %collective-permute-done.83 = f32[17,2048]{1,0:T(8,128)S(1)} collective-permute-done((f32[17,2048]{1,0:T(8,128)S(1)}, f32[17,2048]{1,0:T(8,128)S(1)}, u32[]{:S(2)}, u32[]{:S(2)}) %collective-permute-start.83) | collective-permute-done | bytes 139296 | tf_op jit(solution)/shard_map/ppermute | solution.py:39
  554.9 9.8 %psum.15 = f32[2,4,128]{2,0,1:T(2,128)S(1)} all-reduce(f32[2,4,128]{2,0,1:T(2,128)S(1)} %scatter_fusion.2), channel_id=1, replica_groups=mesh['seq'=4,'expert'=8] {'seq'}, use_global_device_ids=true, to_apply=%region_24.25 | all-reduce | flops 1024 | bytes 8192 | tf_op jit(solution)/shard_map/psum | solution.py:178
  601.1 19.5 %collective-permute-done.76 = bf16[64,2048]{1,0:T(8,128)(2,1)S(1)} collective-permute-done((bf16[64,2048]{1,0:T(8,128)(2,1)S(1)}, bf16[64,2048]{1,0:T(8,128)(2,1)S(1)}, u32[]{:S(2)}, u32[]{:S(2)}) %collective-permute-start.76) | collective-permute-done | bytes 262176 | tf_op jit(solution)/shard_map/ppermute | solution.py:29
  633.6 91.2 %collective-permute-done.55 = bf16[128,2048]{1,0:T(8,128)(2,1)S(1)} collective-permute-done((bf16[128,2048]{1,0:T(8,128)(2,1)S(1)}, bf16[128,2048]{1,0:T(8,128)(2,1)S(1)}, u32[]{:S(2)}, u32[]{:S(2)}) %collective-permute-start.55) | collective-permute-done | bytes 524320 | tf_op jit(solution)/shard_map/ppermute | solution.py:34
  732.9 12.7 %collective-permute-done.64 = bf16[4,64,1536]{2,1,0:T(8,128)(2,1)} collective-permute-done((bf16[4,64,1536]{2,1,0:T(8,128)(2,1)}, bf16[4,64,1536]{2,1,0:T(8,128)(2,1)}, u32[]{:S(2)}, u32[]{:S(2)}) %collective-permute-start.64) | collective-permute-done | bytes 786464 | tf_op jit(solution)/shard_map/ppermute | solution.py:29
  758.1 31.0 %collective-permute-done.66 = bf16[4,64,1536]{2,1,0:T(8,128)(2,1)S(1)} collective-permute-done((bf16[4,64,1536]{2,1,0:T(8,128)(2,1)S(1)}, bf16[4,64,1536]{2,1,0:T(8,128)(2,1)S(1)}, u32[]{:S(2)}, u32[]{:S(2)}) %collective-permute-start.66) | collective-permute-done | bytes 786464 | tf_op jit(solution)/shard_map/ppermute | solution.py:29
  799.8 17.4 %collective-permute-done.60 = f32[3,2048]{1,0:T(4,128)S(1)} collective-permute-done((f32[3,2048]{1,0:T(4,128)S(1)}, f32[3,2048]{1,0:T(4,128)S(1)}, u32[]{:S(2)}, u32[]{:S(2)}) %collective-permute-start.60) | collective-permute-done | bytes 24608 | tf_op jit(solution)/shard_map/ppermute | solution.py:39
  (528 shorter events, 320.5 us)
Async XLA Ops:
  3.7 57.1 %collective-permute-start.1 = (bf16[128,2048]{1,0:T(8,128)(2,1)S(1)}, bf16[128,2048]{1,0:T(8,128)(2,1)}, u32[]{:S(2)}, u32[]{:S(2)}) collective-permute-start(bf16[128,2048]{1,0:T(8,128)(2,1)S(1)} %fusion.60), channel_id=1, source_target_pairs={{0,16},{8,24},{16,0},{24,8},{1,17},{9,25},{17,1},{25,9},{2,18},{10... | collective-permute-start | bytes 1572872 | tf_op jit(solution)/shard_map/ppermute | solution.py:34
  6.7 134.0 %collective-permute-start = (bf16[128,2048]{1,0:T(8,128)(2,1)S(1)}, bf16[128,2048]{1,0:T(8,128)(2,1)}, u32[]{:S(2)}, u32[]{:S(2)}) collective-permute-start(bf16[128,2048]{1,0:T(8,128)(2,1)S(1)} %fusion.60), channel_id=1, source_target_pairs={{0,8},{8,0},{16,24},{24,16},{1,9},{9,1},{17,25},{25,17},{2,10},{10... | collective-permute-start | bytes 1572872 | tf_op jit(solution)/shard_map/ppermute | solution.py:29
  13.4 34.3 %collective-permute-start.3 = (bf16[64,1536]{1,0:T(8,128)(2,1)S(1)}, bf16[64,1536]{1,0:T(8,128)(2,1)S(1)}, u32[]{:S(2)}, u32[]{:S(2)}) collective-permute-start(bf16[64,1536]{1,0:T(8,128)(2,1)S(1)} %dynamic-slice_bitcast_fusion.19), channel_id=1, source_target_pairs={{0,8},{8,0},{16,24},{24,16},{1,9},{9,1},{17,25},{25,17},{2,10},{10... | collective-permute-start | bytes 589832 | tf_op jit(solution)/shard_map/ppermute | solution.py:39
  60.8 80.0 %collective-permute-start.2 = (bf16[128,2048]{1,0:T(8,128)(2,1)}, bf16[128,2048]{1,0:T(8,128)(2,1)S(1)}, u32[]{:S(2)}, u32[]{:S(2)}) collective-permute-start(bf16[128,2048]{1,0:T(8,128)(2,1)} %collective-permute-done.1), channel_id=1, source_target_pairs={{0,8},{8,0},{16,24},{24,16},{1,9},{9,1},{17,25},{25,17},{2,10},{10... | collective-permute-start | bytes 1572872 | tf_op jit(solution)/shard_map/ppermute | solution.py:29
  140.2 36.6 %collective-permute-start.13 = (bf16[64,2048]{1,0:T(8,128)(2,1)}, bf16[64,2048]{1,0:T(8,128)(2,1)}, u32[]{:S(2)}, u32[]{:S(2)}) collective-permute-start(bf16[64,2048]{1,0:T(8,128)(2,1)} %param.25), channel_id=1, source_target_pairs={{0,1},{1,0},{2,3},{3,2},{4,5},{5,4},{6,7},{7,6},{8,9},{9,8},{10,11... | collective-permute-start | bytes 786440 | tf_op jit(solution)/shard_map/ppermute | solution.py:29
  140.7 34.5 %collective-permute-start.14 = (bf16[64,2048]{1,0:T(8,128)(2,1)}, bf16[64,2048]{1,0:T(8,128)(2,1)}, u32[]{:S(2)}, u32[]{:S(2)}) collective-permute-start(bf16[64,2048]{1,0:T(8,128)(2,1)} %param.25), channel_id=1, source_target_pairs={{0,2},{1,3},{2,4},{3,5},{4,6},{5,7},{6,0},{7,1},{8,10},{9,11},{10,... | collective-permute-start | bytes 786440 | tf_op jit(solution)/shard_map/ppermute | solution.py:34
  226.2 38.9 %collective-permute-start.23 = (bf16[128,2048]{1,0:T(8,128)(2,1)S(1)}, bf16[128,2048]{1,0:T(8,128)(2,1)S(1)}, u32[]{:S(2)}, u32[]{:S(2)}) collective-permute-start(bf16[128,2048]{1,0:T(8,128)(2,1)S(1)} %get-tuple-element.39), channel_id=1, source_target_pairs={{0,1},{1,0},{2,3},{3,2},{4,5},{5,4},{6,7},{7,6},{8,9},{9,8},{10,11... | collective-permute-start | bytes 1572872 | tf_op jit(solution)/shard_map/ppermute | solution.py:29
  384.1 81.3 %collective-permute-start.43 = (bf16[128,2048]{1,0:T(8,128)(2,1)}, bf16[128,2048]{1,0:T(8,128)(2,1)S(1)}, u32[]{:S(2)}, u32[]{:S(2)}) collective-permute-start(bf16[128,2048]{1,0:T(8,128)(2,1)} %get-tuple-element.59), channel_id=1, source_target_pairs={{0,1},{1,0},{2,3},{3,2},{4,5},{5,4},{6,7},{7,6},{8,9},{9,8},{10,11... | collective-permute-start | bytes 1572872 | tf_op jit(solution)/shard_map/ppermute | solution.py:29
  384.6 62.7 %collective-permute-start.41 = (bf16[128,2048]{1,0:T(8,128)(2,1)}, bf16[128,2048]{1,0:T(8,128)(2,1)}, u32[]{:S(2)}, u32[]{:S(2)}) collective-permute-start(bf16[128,2048]{1,0:T(8,128)(2,1)} %get-tuple-element.60), channel_id=1, source_target_pairs={{0,1},{1,0},{2,3},{3,2},{4,5},{5,4},{6,7},{7,6},{8,9},{9,8},{10,11... | collective-permute-start | bytes 1572872 | tf_op jit(solution)/shard_map/ppermute | solution.py:29
  386.1 51.3 %collective-permute-start.39 = (bf16[128,2048]{1,0:T(8,128)(2,1)}, bf16[128,2048]{1,0:T(8,128)(2,1)}, u32[]{:S(2)}, u32[]{:S(2)}) collective-permute-start(bf16[128,2048]{1,0:T(8,128)(2,1)} %get-tuple-element.61), channel_id=1, source_target_pairs={{0,1},{1,0},{2,3},{3,2},{4,5},{5,4},{6,7},{7,6},{8,9},{9,8},{10,11... | collective-permute-start | bytes 1572872 | tf_op jit(solution)/shard_map/ppermute | solution.py:29
  386.6 43.8 %collective-permute-start.37 = (bf16[128,2048]{1,0:T(8,128)(2,1)}, bf16[128,2048]{1,0:T(8,128)(2,1)S(1)}, u32[]{:S(2)}, u32[]{:S(2)}) collective-permute-start(bf16[128,2048]{1,0:T(8,128)(2,1)} %get-tuple-element.58), channel_id=1, source_target_pairs={{0,1},{1,0},{2,3},{3,2},{4,5},{5,4},{6,7},{7,6},{8,9},{9,8},{10,11... | collective-permute-start | bytes 1572872 | tf_op jit(solution)/shard_map/ppermute | solution.py:29
  391.0 56.0 %all-to-all-start = ((f32[8,128,2]{1,2,0:T(2,128)}), f32[8,128,2]{1,2,0:T(2,128)S(1)}, u32[]{:S(2)}, u32[]{:S(2)}) async-start(f32[8,128,2]{1,2,0:T(2,128)} %scatter_fusion.1), calls=%async_computation | async-start | bytes 16384 | tf_op jit(solution)/shard_map/all_to_all | solution.py:254
  416.0 44.9 %collective-permute-start.90 = (bf16[2,256,2048]{2,1,0:T(8,128)(2,1)}, bf16[2,256,2048]{2,1,0:T(8,128)(2,1)}, u32[]{:S(2)}, u32[]{:S(2)}) collective-permute-start(bf16[2,256,2048]{2,1,0:T(8,128)(2,1)} %get-tuple-element.43), channel_id=1, source_target_pairs={{0,8},{8,0},{16,24},{24,16},{1,9},{9,1},{17,25},{25,17},{2,10},{10... | collective-permute-start | bytes 6291464 | tf_op jit(solution)/shard_map/ppermute | solution.py:29
  437.4 61.0 %collective-permute-start.84 = (bf16[2,512,1024]{2,1,0:T(8,128)(2,1)}, bf16[2,512,1024]{2,1,0:T(8,128)(2,1)}, u32[]{:S(2)}, u32[]{:S(2)}) collective-permute-start(bf16[2,512,1024]{2,1,0:T(8,128)(2,1)} %get-tuple-element.47), channel_id=1, source_target_pairs={{0,8},{8,0},{16,24},{24,16},{1,9},{9,1},{17,25},{25,17},{2,10},{10... | collective-permute-start | bytes 6291464 | tf_op jit(solution)/shard_map/ppermute | solution.py:29
  447.2 69.7 %collective-permute-start.87 = (bf16[2,512,1024]{2,1,0:T(8,128)(2,1)}, bf16[2,512,1024]{2,1,0:T(8,128)(2,1)S(1)}, u32[]{:S(2)}, u32[]{:S(2)}) collective-permute-start(bf16[2,512,1024]{2,1,0:T(8,128)(2,1)} %get-tuple-element.45), channel_id=1, source_target_pairs={{0,8},{8,0},{16,24},{24,16},{1,9},{9,1},{17,25},{25,17},{2,10},{10... | collective-permute-start | bytes 6291464 | tf_op jit(solution)/shard_map/ppermute | solution.py:29
  459.4 163.6 %collective-permute-start.92 = (bf16[2,256,2048]{2,1,0:T(8,128)(2,1)}, bf16[2,256,2048]{2,1,0:T(8,128)(2,1)}, u32[]{:S(2)}, u32[]{:S(2)}) collective-permute-start(bf16[2,256,2048]{2,1,0:T(8,128)(2,1)} %get-tuple-element.44), channel_id=1, source_target_pairs={{0,8},{8,0},{16,24},{24,16},{1,9},{9,1},{17,25},{25,17},{2,10},{10... | collective-permute-start | bytes 6291464 | tf_op jit(solution)/shard_map/ppermute | solution.py:29
  479.3 41.7 %collective-permute-start.52 = (bf16[128,2048]{1,0:T(8,128)(2,1)S(1)}, bf16[128,2048]{1,0:T(8,128)(2,1)S(1)}, u32[]{:S(2)}, u32[]{:S(2)}) collective-permute-start(bf16[128,2048]{1,0:T(8,128)(2,1)S(1)} %fusion.133), channel_id=1, source_target_pairs={{0,16},{8,24},{16,0},{24,8},{1,17},{9,25},{17,1},{25,9},{2,18},{10... | collective-permute-start | bytes 1572872 | tf_op jit(solution)/shard_map/ppermute | solution.py:34
  515.7 111.0 %collective-permute-start.91 = (bf16[2,256,2048]{2,1,0:T(8,128)(2,1)}, bf16[2,256,2048]{2,1,0:T(8,128)(2,1)}, u32[]{:S(2)}, u32[]{:S(2)}) collective-permute-start(bf16[2,256,2048]{2,1,0:T(8,128)(2,1)} %fusion.20), channel_id=1, source_target_pairs={{0,16},{8,24},{16,0},{24,8},{1,17},{9,25},{17,1},{25,9},{2,18},{10... | collective-permute-start | bytes 6291464 | tf_op jit(solution)/shard_map/ppermute | solution.py:34
  535.0 52.0 %collective-permute-start.48 = (bf16[128,2048]{1,0:T(8,128)(2,1)}, bf16[128,2048]{1,0:T(8,128)(2,1)}, u32[]{:S(2)}, u32[]{:S(2)}) collective-permute-start(bf16[128,2048]{1,0:T(8,128)(2,1)} %get-tuple-element.56), channel_id=1, source_target_pairs={{0,1},{1,0},{2,3},{3,2},{4,5},{5,4},{6,7},{7,6},{8,9},{9,8},{10,11... | collective-permute-start | bytes 1572872 | tf_op jit(solution)/shard_map/ppermute | solution.py:29
  536.8 39.1 %collective-permute-start.46 = (bf16[128,2048]{1,0:T(8,128)(2,1)}, bf16[128,2048]{1,0:T(8,128)(2,1)}, u32[]{:S(2)}, u32[]{:S(2)}) collective-permute-start(bf16[128,2048]{1,0:T(8,128)(2,1)} %get-tuple-element.57), channel_id=1, source_target_pairs={{0,1},{1,0},{2,3},{3,2},{4,5},{5,4},{6,7},{7,6},{8,9},{9,8},{10,11... | collective-permute-start | bytes 1572872 | tf_op jit(solution)/shard_map/ppermute | solution.py:29
  538.4 37.4 %collective-permute-start.45 = (bf16[128,2048]{1,0:T(8,128)(2,1)}, bf16[128,2048]{1,0:T(8,128)(2,1)}, u32[]{:S(2)}, u32[]{:S(2)}) collective-permute-start(bf16[128,2048]{1,0:T(8,128)(2,1)} %fusion.76), channel_id=1, source_target_pairs={{0,2},{1,3},{2,4},{3,5},{4,6},{5,7},{6,0},{7,1},{8,10},{9,11},{10,... | collective-permute-start | bytes 1572872 | tf_op jit(solution)/shard_map/ppermute | solution.py:34
  620.6 106.4 %collective-permute-start.86 = (bf16[2,512,1024]{2,1,0:T(8,128)(2,1)S(1)}, bf16[2,512,1024]{2,1,0:T(8,128)(2,1)S(1)}, u32[]{:S(2)}, u32[]{:S(2)}) collective-permute-start(bf16[2,512,1024]{2,1,0:T(8,128)(2,1)S(1)} %copy-done.22), channel_id=1, source_target_pairs={{0,8},{8,0},{16,24},{24,16},{1,9},{9,1},{17,25},{25,17},{2,10},{10... | collective-permute-start | bytes 6291464 | tf_op jit(solution)/shard_map/ppermute | solution.py:29
  620.6 106.5 %collective-permute-start.85 = (bf16[2,512,1024]{2,1,0:T(8,128)(2,1)S(1)}, bf16[2,512,1024]{2,1,0:T(8,128)(2,1)S(1)}, u32[]{:S(2)}, u32[]{:S(2)}) collective-permute-start(bf16[2,512,1024]{2,1,0:T(8,128)(2,1)S(1)} %copy-done.24), channel_id=1, source_target_pairs={{0,16},{8,24},{16,0},{24,8},{1,17},{9,25},{17,1},{25,9},{2,18},{10... | collective-permute-start | bytes 6291464 | tf_op jit(solution)/shard_map/ppermute | solution.py:34
  623.1 127.9 %collective-permute-start.89 = (bf16[2,512,1024]{2,1,0:T(8,128)(2,1)S(1)}, bf16[2,512,1024]{2,1,0:T(8,128)(2,1)S(1)}, u32[]{:S(2)}, u32[]{:S(2)}) collective-permute-start(bf16[2,512,1024]{2,1,0:T(8,128)(2,1)S(1)} %copy-done.21), channel_id=1, source_target_pairs={{0,8},{8,0},{16,24},{24,16},{1,9},{9,1},{17,25},{25,17},{2,10},{10... | collective-permute-start | bytes 6291464 | tf_op jit(solution)/shard_map/ppermute | solution.py:29
  625.5 126.7 %collective-permute-start.88 = (bf16[2,512,1024]{2,1,0:T(8,128)(2,1)S(1)}, bf16[2,512,1024]{2,1,0:T(8,128)(2,1)S(1)}, u32[]{:S(2)}, u32[]{:S(2)}) collective-permute-start(bf16[2,512,1024]{2,1,0:T(8,128)(2,1)S(1)} %copy-done.23), channel_id=1, source_target_pairs={{0,16},{8,24},{16,0},{24,8},{1,17},{9,25},{17,1},{25,9},{2,18},{10... | collective-permute-start | bytes 6291464 | tf_op jit(solution)/shard_map/ppermute | solution.py:34
  626.7 98.1 %collective-permute-start.55 = (bf16[128,2048]{1,0:T(8,128)(2,1)S(1)}, bf16[128,2048]{1,0:T(8,128)(2,1)S(1)}, u32[]{:S(2)}, u32[]{:S(2)}) collective-permute-start(bf16[128,2048]{1,0:T(8,128)(2,1)S(1)} %add_convert_fusion.1), channel_id=1, source_target_pairs={{0,16},{8,24},{16,0},{24,8},{1,17},{9,25},{17,1},{25,9},{2,18},{10... | collective-permute-start | bytes 1572872 | tf_op jit(solution)/shard_map/ppermute | solution.py:34
  732.3 62.2 %collective-permute-start.50 = (bf16[128,2048]{1,0:T(8,128)(2,1)S(1)}, bf16[128,2048]{1,0:T(8,128)(2,1)S(1)}, u32[]{:S(2)}, u32[]{:S(2)}) collective-permute-start(bf16[128,2048]{1,0:T(8,128)(2,1)S(1)} %copy-done.41), channel_id=1, source_target_pairs={{0,1},{1,0},{2,3},{3,2},{4,5},{5,4},{6,7},{7,6},{8,9},{9,8},{10,11... | collective-permute-start | bytes 1572872 | tf_op jit(solution)/shard_map/ppermute | solution.py:29
  745.6 72.2 %collective-permute-start.68 = (bf16[4,64,1536]{2,1,0:T(8,128)(2,1)S(1)}, bf16[4,64,1536]{2,1,0:T(8,128)(2,1)S(1)}, u32[]{:S(2)}, u32[]{:S(2)}) collective-permute-start(bf16[4,64,1536]{2,1,0:T(8,128)(2,1)S(1)} %get-tuple-element.53), channel_id=1, source_target_pairs={{0,1},{1,0},{2,3},{3,2},{4,5},{5,4},{6,7},{7,6},{8,9},{9,8},{10,11... | collective-permute-start | bytes 2359304 | tf_op jit(solution)/shard_map/ppermute | solution.py:29
  748.8 40.3 %collective-permute-start.66 = (bf16[4,64,1536]{2,1,0:T(8,128)(2,1)S(1)}, bf16[4,64,1536]{2,1,0:T(8,128)(2,1)S(1)}, u32[]{:S(2)}, u32[]{:S(2)}) collective-permute-start(bf16[4,64,1536]{2,1,0:T(8,128)(2,1)S(1)} %copy-done.33), channel_id=1, source_target_pairs={{0,1},{1,0},{2,3},{3,2},{4,5},{5,4},{6,7},{7,6},{8,9},{9,8},{10,11... | collective-permute-start | bytes 2359304 | tf_op jit(solution)/shard_map/ppermute | solution.py:29
  752.1 38.4 %collective-permute-start.65 = (bf16[4,64,1536]{2,1,0:T(8,128)(2,1)S(1)}, bf16[4,64,1536]{2,1,0:T(8,128)(2,1)S(1)}, u32[]{:S(2)}, u32[]{:S(2)}) collective-permute-start(bf16[4,64,1536]{2,1,0:T(8,128)(2,1)S(1)} %fusion.54), channel_id=1, source_target_pairs={{0,2},{1,3},{2,4},{3,5},{4,6},{5,7},{6,0},{7,1},{8,10},{9,11},{10,... | collective-permute-start | bytes 2359304 | tf_op jit(solution)/shard_map/ppermute | solution.py:34
  757.4 37.1 %collective-permute-start.49 = (bf16[128,2048]{1,0:T(8,128)(2,1)S(1)}, bf16[128,2048]{1,0:T(8,128)(2,1)S(1)}, u32[]{:S(2)}, u32[]{:S(2)}) collective-permute-start(bf16[128,2048]{1,0:T(8,128)(2,1)S(1)} %fusion.73), channel_id=1, source_target_pairs={{0,2},{1,3},{2,4},{3,5},{4,6},{5,7},{6,0},{7,1},{8,10},{9,11},{10,... | collective-permute-start | bytes 1572872 | tf_op jit(solution)/shard_map/ppermute | solution.py:34
  790.8 27.0 %collective-permute-start.67 = (bf16[4,64,1536]{2,1,0:T(8,128)(2,1)S(1)}, bf16[4,64,1536]{2,1,0:T(8,128)(2,1)S(1)}, u32[]{:S(2)}, u32[]{:S(2)}) collective-permute-start(bf16[4,64,1536]{2,1,0:T(8,128)(2,1)S(1)} %fusion.52), channel_id=1, source_target_pairs={{0,2},{1,3},{2,4},{3,5},{4,6},{5,7},{6,0},{7,1},{8,10},{9,11},{10,... | collective-permute-start | bytes 2359304 | tf_op jit(solution)/shard_map/ppermute | solution.py:34
  (144 other events, 2853.3 us)

commit v2 on v1

v2 whole, which is shorter than its diff:
```python
from functools import partial

import jax
import jax.numpy as jnp
from jax import lax
from jax.experimental import pallas as pl
from jax.experimental.pallas import tpu as pltpu
from jax.sharding import PartitionSpec as P

HEADS = 16
MOST = 64
BF = jnp.bfloat16
F32 = jnp.float32

norm_eps = 1e-05
masked_score = -1e30


MESH = pl.DeviceIdType.MESH
ANY = pl.BlockSpec(memory_space=pl.ANY)
IN_VMEM = pl.BlockSpec(memory_space=pltpu.VMEM)
VMEM_BYTES = 63 << 20


def product(left, right):
    return jnp.dot(left, right, preferred_element_type=F32)


def rms_norm(values, norm_gain):
    return (
        values * lax.rsqrt(jnp.mean(values * values, axis=-1, keepdims=True) + norm_eps) * norm_gain
    )


def swap(value, axis):
    n = lax.axis_size(axis)
    return lax.ppermute(value, axis, [(i, i ^ 1) for i in range(n)])


def shift(value, axis):
    n = lax.axis_size(axis)
    return lax.ppermute(value, axis, [(i, (i + 2) % n) for i in range(n)])


def flip(value, axis, delta):
    n = lax.axis_size(axis)
    return lax.ppermute(value, axis, [(i, i ^ delta) for i in range(n)])


def owners(axis):
    n = lax.axis_size(axis)
    me = lax.axis_index(axis)
    outer, inner = me // 2, me % 2
    return [((outer - i) % (n // 2)) * 2 + (inner ^ b) for i in range(n // 2) for b in range(2)]


def gather_blocks(value, axis):
    blocks = []
    current = value
    for i in range(lax.axis_size(axis) // 2):
        if i:
            current = shift(current, axis)
        blocks += [current, swap(current, axis)]
    return blocks


def add_low(left, right):
    return (left.astype(F32) + right.astype(F32)).astype(BF)


def scatter_sum(blocks, axis):
    outer_count = lax.axis_size(axis) // 2
    pairs = {}
    for t in list(range(1, outer_count)) + [0]:
        arrived = swap(blocks[2 * t + 1], axis)
        pairs[t] = blocks[2 * t].astype(F32) + arrived.astype(F32)
    total = pairs[1 % outer_count]
    for t in range(1, outer_count):
        arrived = shift(total.astype(BF), axis)
        total = arrived.astype(F32) + pairs[(t + 1) % outer_count]
    return total


def all_sum(value, axes):
    for axis in axes:
        delta = 1
        while delta < lax.axis_size(axis):
            value = value + flip(value, axis, delta)
            delta *= 2
    return value


def exchange(parts, axis):
    n = lax.axis_size(axis)
    me = lax.axis_index(axis)
    out = parts
    for delta in range(1, n):
        other = me ^ delta
        got = flip(lax.dynamic_index_in_dim(parts, other, 0, keepdims=False), axis, delta)
        out = lax.dynamic_update_index_in_dim(out, got, other, 0)
    return out


def after(value, *others):
    return lax.optimization_barrier((value,) + others)[0]


def remote(src, dst, send_sem, recv_sem, device):
    return pltpu.make_async_remote_copy(
        src_ref=src,
        dst_ref=dst,
        send_sem=send_sem,
        recv_sem=recv_sem,
        device_id=device,
        device_id_type=MESH,
    )


def greet(devices):
    barrier = pltpu.get_barrier_semaphore()
    for device in devices:
        pl.semaphore_signal(barrier, inc=1, device_id=device, device_id_type=MESH)
    pl.semaphore_wait(barrier, len(devices))


class Ring:
    def __init__(self, axis):
        self.axis = axis
        self.size = lax.axis_size(axis)
        self.outer_count = self.size // 2
        self.me = lax.axis_index(axis)
        self.outer, self.inner = self.me // 2, self.me % 2
        self.pair = {axis: self.outer * 2 + (1 - self.inner)}
        self.next = {axis: self.at(-1) * 2 + self.inner}
        self.last = {axis: self.at(1) * 2 + self.inner}

    def at(self, back):
        return lax.rem(self.outer - back + self.outer_count, self.outer_count)

    def partners(self):
        if self.outer_count == 1:
            return [self.pair]
        if self.outer_count == 2:
            return [self.pair, self.next]
        return [self.pair, self.next, self.last]


class Gather:
    def __init__(self, ring, place, send_sems, recv_sems):
        self.ring, self.place = ring, place
        self.send_sems, self.recv_sems = send_sems, recv_sems
        self.copies = []

    def block(self, back):
        return self.place(self.ring.at(back) * 2 + self.ring.inner)

    def _send(self, back, src):
        ring = self.ring
        if back < ring.outer_count - 1:
            copy = remote(src, self.block(back), self.send_sems.at[back, 0],
                          self.recv_sems.at[back + 1, 0], ring.next)
            copy.start()
            self.copies.append(copy)
        copy = remote(src, self.block(back), self.send_sems.at[back, 1],
                      self.recv_sems.at[back, 1], ring.pair)
        copy.start()
        self.copies.append(copy)

    def start(self, src):
        self._send(0, src)

    def relay(self, back):
        dst = self.block(back)
        remote(dst, dst, self.send_sems.at[back - 1, 0], self.recv_sems.at[back, 0],
               self.ring.next).wait_recv()
        self._send(back, dst)

    def finish(self):
        ring = self.ring
        for back in range(ring.outer_count):
            dst = self.place(ring.at(back) * 2 + 1 - ring.inner)
            remote(dst, dst, self.send_sems.at[back, 1], self.recv_sems.at[back, 1],
                   ring.pair).wait_recv()
        for copy in self.copies:
            copy.wait_send()


def gather_sems(ring, chunks):
    shape = (chunks, ring.outer_count, 2)
    return [pltpu.SemaphoreType.DMA(shape), pltpu.SemaphoreType.DMA(shape)]


class Scatter:
    def __init__(self, ring, x_ref, chunks, own, land, ringbuf, out, own_sems, sems):
        self.ring, self.x_ref, self.chunks = ring, x_ref, chunks
        self.own, self.land, self.ringbuf, self.out = own, land, ringbuf, out
        self.own_sems, self.sems = own_sems, sems
        self.order = list(range(1, ring.outer_count)) + [0]
        self.rows = x_ref.shape[1] // chunks

    def cut(self, c):
        return pl.ds(c * self.rows, self.rows)

    def pair_copy(self, t, c):
        ring = self.ring
        src = self.x_ref.at[ring.at(t) * 2 + 1 - ring.inner, self.cut(c)]
        return remote(src, self.land.at[t, self.cut(c)], self.sems.at[0, t, c],
                      self.sems.at[1, t, c], ring.pair)

    def slot(self, t):
        return (t - 2) % self.ring.outer_count

    def own_copy(self, t):
        src = self.x_ref.at[self.ring.at(t) * 2 + self.ring.inner]
        return pltpu.make_async_copy(src, self.own.at[t], self.own_sems.at[t])

    def ring_copy(self, t, c):
        to = (t + 1) % self.ring.outer_count
        return remote(self.out.at[t - 1, self.cut(c)], self.ringbuf.at[self.slot(to), self.cut(c)],
                      self.sems.at[2, t, c], self.sems.at[3, to, c], self.ring.next)

    def start_place(self, t):
        self.own_copy(t).start()
        for c in range(self.chunks):
            self.pair_copy(t, c).start()

    def start(self):
        for t in self.order:
            self.start_place(t)

    def mine(self, t, c):
        return self.own[t, self.cut(c)]

    def arrive(self, t, c):
        if c == 0:
            self.own_copy(t).wait()
        self.pair_copy(t, c).wait_recv()

    def step(self, t, c):
        self.arrive(t, c)
        cut = self.cut(c)
        total = self.mine(t, c).astype(F32) + self.land[t, cut].astype(F32)
        if t != self.order[0]:
            self.ring_copy((t - 1) % self.ring.outer_count, c).wait_recv()
            total = total + self.ringbuf[self.slot(t), cut].astype(F32)
        if t:
            self.out[t - 1, cut] = total.astype(BF)
            self.ring_copy(t, c).start()
        return total

    def finish(self):
        for t in self.order:
            for c in range(self.chunks):
                self.pair_copy(t, c).wait_send()
                if t:
                    self.ring_copy(t, c).wait_send()


class KeptScatter(Scatter):
    def __init__(self, ring, x_ref, chunks, own, land, ringbuf, out, sems):
        super().__init__(ring, x_ref, chunks, own, land, ringbuf, out, None, sems)

    def start_place(self, t):
        for c in range(self.chunks):
            self.pair_copy(t, c).start()

    def mine(self, t, c):
        return self.own[pl.ds(t * self.x_ref.shape[1] + c * self.rows, self.rows)]

    def arrive(self, t, c):
        self.pair_copy(t, c).wait_recv()


class PlaceScatter(Scatter):
    def __init__(self, ring, parts, chunks, land, ringbuf, sems):
        super().__init__(ring, parts, chunks, None, land, ringbuf, None, None, sems)

    def block(self, t):
        return self.ring.at(t) * 2 + self.ring.inner

    def ring_copy(self, t, c):
        to = (t + 1) % self.ring.outer_count
        return remote(self.x_ref.at[self.block(t), self.cut(c)], self.ringbuf.at[self.slot(to), self.cut(c)],
                      self.sems.at[2, t, c], self.sems.at[3, to, c], self.ring.next)

    def start_place(self, t):
        for c in range(self.chunks):
            self.pair_copy(t, c).start()

    def step(self, t, c):
        self.pair_copy(t, c).wait_recv()
        cut, mine = self.cut(c), self.block(t)
        total = self.x_ref[mine, cut].astype(F32) + self.land[t, cut].astype(F32)
        if t != self.order[0]:
            self.ring_copy((t - 1) % self.ring.outer_count, c).wait_recv()
            total = total + self.ringbuf[self.slot(t), cut].astype(F32)
        if t:
            self.x_ref[mine, cut] = total.astype(BF)
            self.ring_copy(t, c).start()
        return total


def scatter_scratch(axis, rows, columns, chunks):
    outer_count = lax.axis_size(axis) // 2
    buf = pltpu.VMEM((outer_count, rows, columns), BF)
    less = pltpu.VMEM((max(outer_count - 1, 1), rows, columns), BF)
    return [buf, buf, less, less, pltpu.SemaphoreType.DMA((outer_count,)),
            pltpu.SemaphoreType.DMA((4, outer_count, chunks))]


def kept_scratch(axis, rows, columns, chunks):
    scratch = scatter_scratch(axis, rows, columns, chunks)
    return scratch[1:4] + scratch[5:]


SCATTER_REFS = 6


def kernel_params(number):
    return pltpu.CompilerParams(
        collective_id=number, has_side_effects=True, vmem_limit_bytes=VMEM_BYTES
    )


def call(kernel, number, micros, outs, scratch, *args, specs=None, out_specs=None):
    return pl.pallas_call(
        kernel,
        out_shape=outs,
        in_specs=specs or [ANY] * len(args),
        out_specs=out_specs or jax.tree.map(lambda _: ANY, outs),
        scratch_shapes=scratch,
        compiler_params=kernel_params(number),
        cost_estimate=pl.CostEstimate(
            flops=0, bytes_accessed=micros * 3_000_000, transcendentals=0
        ),
    )(*args)


def weights_kernel(
    wq, wk, wv, normed, hits, q_out, k_out, v_out, normed_out, hits_out,
    own_sems, swap_send, swap_recv, tok_send, tok_recv, g_send, g_recv,
):
    seq, group = Ring("seq"), Ring("expert")
    others = [{"seq": seq.me ^ d} for d in range(1, seq.size)]
    greet(others + group.partners())
    wrows = wq.shape[0]
    cols = wq.shape[1] // seq.size
    rows_mine = pl.ds(group.me * wrows, wrows)
    weights = [(wq, q_out), (wk, k_out), (wv, v_out)]

    def columns_of(ref, s):
        return ref.at[:, pl.ds(pl.multiple_of(s * cols, cols), cols)]

    def swap_copy(i, d):
        src, dst = weights[i]
        return remote(columns_of(src, seq.me ^ d), dst.at[seq.me, rows_mine],
                      swap_send.at[i, d], swap_recv.at[i, d], others[d - 1])

    def token_copy(d):
        return remote(normed, normed_out.at[seq.me], tok_send.at[d], tok_recv.at[d], others[d - 1])

    own = [
        pltpu.make_async_copy(columns_of(src, seq.me), dst.at[seq.me, rows_mine], own_sems.at[i])
        for i, (src, dst) in enumerate(weights)
    ]
    own.append(pltpu.make_async_copy(normed, normed_out.at[seq.me], own_sems.at[3]))
    own.append(pltpu.make_async_copy(hits, hits_out.at[group.me], own_sems.at[4]))
    for i in range(3):
        own[i].start()
        for d in range(1, seq.size):
            swap_copy(i, d).start()
    own[3].start()
    own[4].start()
    for d in range(1, seq.size):
        token_copy(d).start()

    def placed(ref):
        return lambda e: ref.at[:, pl.ds(e * wrows, wrows)]

    gathers = [
        Gather(group, placed(dst), g_send.at[i], g_recv.at[i])
        for i, (_, dst) in enumerate(weights)
    ]
    gathers.append(Gather(group, lambda e: hits_out.at[e], g_send.at[3], g_recv.at[3]))
    gathers[3].start(hits)
    for i in range(3):
        own[i].wait()
        for d in range(1, seq.size):
            remote(weights[i][1].at[seq.me ^ d, rows_mine], weights[i][1].at[seq.me ^ d, rows_mine],
                   swap_send.at[i, d], swap_recv.at[i, d], others[d - 1]).wait_recv()
        gathers[i].start(weights[i][1].at[:, rows_mine])
    for back in range(1, group.outer_count):
        for gather in gathers:
            gather.relay(back)
    for gather in gathers:
        gather.finish()
    for d in range(1, seq.size):
        there = normed_out.at[seq.me ^ d]
        remote(there, there, tok_send.at[d], tok_recv.at[d], others[d - 1]).wait_recv()
        token_copy(d).wait_send()
        for i in range(3):
            swap_copy(i, d).wait_send()
    own[3].wait()
    own[4].wait()


def gather_weights(wq, wk, wv, normed, hits):
    seq_count, group_count = lax.axis_size("seq"), lax.axis_size("expert")
    width = wq.shape[1]
    w_shape = jax.ShapeDtypeStruct((seq_count, width // seq_count, width // seq_count), BF)
    dma = pltpu.SemaphoreType.DMA
    return call(
        weights_kernel, 1, 90,
        (w_shape, w_shape, w_shape,
         jax.ShapeDtypeStruct((seq_count,) + normed.shape, BF),
         jax.ShapeDtypeStruct((group_count,) + hits.shape, BF)),
        [dma((5,)), dma((3, seq_count)), dma((3, seq_count)), dma((seq_count,)), dma((seq_count,)),
         dma((4, group_count // 2, 2)), dma((4, group_count // 2, 2))],
        wq, wk, wv, normed, hits,
    )


HIDDEN_CHUNKS = 2


def hidden_kernel(parts, tokens, gain, hidden_out, all_out, *scratch):
    seq, group = Ring("seq"), Ring("expert")
    greet(seq.partners() + group.partners())
    scatter = Scatter(seq, parts, HIDDEN_CHUNKS, *scratch[:SCATTER_REFS])
    low, low_sems, g_send, g_recv = scratch[SCATTER_REFS:]
    scatter.start()
    for t in scatter.order[:-1]:
        for c in range(HIDDEN_CHUNKS):
            scatter.step(t, c)
    gathers, own = [], []
    for c in range(HIDDEN_CHUNKS):
        cut = scatter.cut(c)
        hidden = tokens[cut].astype(F32) + scatter.step(0, c)
        hidden_out[cut] = hidden
        scale = lax.rsqrt(jnp.mean(hidden * hidden, axis=-1, keepdims=True) + norm_eps)
        low[cut] = (hidden * scale * gain[...]).astype(BF)
        own.append(pltpu.make_async_copy(low.at[cut], all_out.at[group.me, cut], low_sems.at[c]))
        own[c].start()
        gathers.append(
            Gather(group, lambda e, cut=cut: all_out.at[e, cut], g_send.at[c], g_recv.at[c])
        )
        gathers[c].start(low.at[cut])
    for back in range(1, group.outer_count):
        for gather in gathers:
            gather.relay(back)
    for c in range(HIDDEN_CHUNKS):
        gathers[c].finish()
        own[c].wait()
    scatter.finish()


def hidden_and_rows(parts, tokens, gain):
    group_count = lax.axis_size("expert")
    rows, width = tokens.shape
    dma = pltpu.SemaphoreType.DMA
    return call(
        hidden_kernel, 2, 60,
        (jax.ShapeDtypeStruct((rows, width), F32),
         jax.ShapeDtypeStruct((group_count, rows, width), BF)),
        scatter_scratch("seq", rows, width, HIDDEN_CHUNKS)
        + [pltpu.VMEM((rows, width), BF), dma((HIDDEN_CHUNKS,)),
           dma((HIDDEN_CHUNKS, group_count // 2, 2)), dma((HIDDEN_CHUNKS, group_count // 2, 2))],
        parts, tokens, gain[None],
        specs=[ANY, IN_VMEM, IN_VMEM], out_specs=(IN_VMEM, ANY),
    )


ROW_CHUNKS = 2


def rows_kernel(parts, out, *scratch):
    group = Ring("expert")
    greet(group.partners())
    scatter = Scatter(group, parts, ROW_CHUNKS, *scratch)
    scatter.start()
    for t in scatter.order:
        for c in range(ROW_CHUNKS):
            total = scatter.step(t, c)
            if not t:
                out[scatter.cut(c)] = total
    scatter.finish()


def sum_rows(parts):
    rows, width = parts.shape[1:]
    return call(
        rows_kernel, 3, 50, jax.ShapeDtypeStruct((rows, width), F32),
        scatter_scratch("expert", rows, width, ROW_CHUNKS), parts, out_specs=IN_VMEM,
    )


def pack_kernel(rows_in, out, own_sems, g_send, g_recv):
    seq = Ring("seq")
    greet(seq.partners())
    chunks = g_send.shape[0]
    rows = rows_in.shape[0] // chunks
    gathers = []
    for c in range(chunks):
        cut = pl.ds(c * rows, rows)
        pltpu.make_async_copy(rows_in.at[cut], out.at[seq.me, cut], own_sems.at[c]).start()
        gathers.append(
            Gather(seq, lambda s, cut=cut: out.at[s, cut], g_send.at[c], g_recv.at[c])
        )
        gathers[c].start(rows_in.at[cut])
    for back in range(1, seq.outer_count):
        for gather in gathers:
            gather.relay(back)
    for c in range(chunks):
        gathers[c].finish()
        cut = pl.ds(c * rows, rows)
        pltpu.make_async_copy(rows_in.at[cut], out.at[seq.me, cut], own_sems.at[c]).wait()


def gather_pack(rows_in, chunks=2):
    seq_count = lax.axis_size("seq")
    dma = pltpu.SemaphoreType.DMA
    return call(
        pack_kernel, 4, 18, jax.ShapeDtypeStruct((seq_count,) + rows_in.shape, BF),
        [dma((chunks,)), dma((chunks, seq_count // 2, 2)), dma((chunks, seq_count // 2, 2))],
        rows_in,
    )


def dot(left, right, left_dim=1, right_dim=0):
    return lax.dot_general(
        left, right, (((left_dim,), (right_dim,)), ((), ())), preferred_element_type=F32
    )


GRAD_CHUNKS = 2
TILE = 256


def expert_kernel(
    n2, cot, sel, sel_t, gates, wg, wu, wd,
    rows_out, out_parts, d_gate, d_up, d_down,
    stage, parts, routed, cot_rows, wg_v, wu_v, wd_v, scaled, ggate, gup, gate_sums,
    land, ringbuf, in_sems, w_sems, part_sems, wide_sems, out_sems, *dw_scratch,
):
    seq, group = Ring("seq"), Ring("expert")
    greet(seq.partners() + group.partners())
    groups, toks, width = n2.shape
    experts, rows, _ = routed.shape
    slots = rows // groups
    ff = wg_v.shape[1]
    n_total = experts * groups

    def stage_copy(e):
        return pltpu.make_async_copy(n2.at[e], stage.at[e], in_sems.at[0, e])

    def cot_copy(e):
        return pltpu.make_async_copy(cot.at[e], parts.at[e, :, pl.ds(0, width)], in_sems.at[1, e])

    def weight_copy(i, j):
        src, dst = ((wg, wg_v), (wu, wu_v), (wd, wd_v))[i]
        return pltpu.make_async_copy(src.at[j], dst, w_sems.at[i])

    def each(count, body):
        lax.fori_loop(0, count, lambda i, _: (body(i), 0)[1], 0)

    each(groups, lambda e: stage_copy(e).start())
    for i in range(3):
        weight_copy(i, 0).start()
    each(groups, lambda e: cot_copy(e).start())

    def pick(copy, src, dst):
        def body(e):
            copy(e).wait()
            got = dot(sel[e], src[e, :, pl.ds(0, width)]).astype(BF)
            at = pl.ds(pl.multiple_of(e * slots, slots), slots)
            for j in range(experts):
                dst[j, at] = got[j * slots : (j + 1) * slots]
        return body

    each(groups, pick(stage_copy, stage, routed))
    each(groups, pick(cot_copy, parts, cot_rows))

    for j in range(experts):
        for i in range(3):
            weight_copy(i, j).wait()
        gate_sums[j] = jnp.zeros_like(gate_sums[j])

        def hidden_tile(f, j=j):
            at = pl.ds(pl.multiple_of(f * TILE, TILE), TILE)
            gate_pre = dot(routed[j], wg_v[:, at])
            up_pre = dot(routed[j], wu_v[:, at])
            unit = dot(cot_rows[j], wd_v[at, :], 1, 1)
            gate = gates[j][:, :1]
            sig = 1.0 / (1.0 + jnp.exp(-gate_pre))
            silu = gate_pre * sig
            active = silu * up_pre
            low = active.astype(BF).astype(F32)
            gate_sums[j] += jnp.sum(unit * low, axis=-1, keepdims=True)
            scaled[j, :, at] = (low * gate).astype(BF)
            grad_active = unit * gate
            ggate[j, :, at] = (grad_active * up_pre * sig * (1.0 + gate_pre * (1.0 - sig))).astype(BF)
            gup[j, :, at] = (grad_active * silu).astype(BF)

        each(ff // TILE, hidden_tile)
        if j + 1 < experts:
            weight_copy(2, j + 1).start()

        def row_tile(d, j=j):
            at = pl.ds(pl.multiple_of(d * TILE, TILE), TILE)
            grad = dot(ggate[j], wg_v[at, :], 1, 1) + dot(gup[j], wu_v[at, :], 1, 1)
            stage[:, j * slots : (j + 1) * slots, at] = grad.astype(BF).reshape(groups, slots, TILE)

        each(width // TILE, row_tile)
        if j + 1 < experts:
            weight_copy(0, j + 1).start()
            weight_copy(1, j + 1).start()
    weight_copy(2, 0).start()

    scatter = PlaceScatter(group, parts, GRAD_CHUNKS, land, ringbuf, part_sems)
    lanes = lax.broadcasted_iota(jnp.int32, (slots, 128), 1)

    def place(e):
        parts[e, :, pl.ds(0, width)] = dot(sel_t[e], stage[e]).astype(BF)
        at = pl.ds(pl.multiple_of(e * slots, slots), slots)
        high, low = [], []
        for j in range(experts):
            value = gate_sums[j, at]
            first = value.astype(BF)
            rest = (value - first.astype(F32)).astype(BF)
            mine = group.me * experts + j
            high.append(jnp.where(lanes == mine, first.astype(F32),
                                  jnp.where(lanes == mine + n_total, rest.astype(F32), 0.0)))
        parts[e, :, pl.ds(width, 128)] = dot(
            sel_t[e], jnp.concatenate(high, axis=0).astype(BF)
        ).astype(BF)

    for t in scatter.order:
        place(group.at(t) * 2 + 1 - group.inner)
        scatter.start_place(t)
        place(group.at(t) * 2 + group.inner)

    def grad_step(t):
        for c in range(GRAD_CHUNKS):
            total = scatter.step(t, c)
            if not t:
                rows_out[scatter.cut(c)] = total

    side, short = width // seq.size, ff // seq.size

    def wide_grad(right, s, j):
        at = pl.ds(pl.multiple_of(s * side, side), side)
        return dot(routed[j, :, at], right[j], 0, 0).astype(BF)

    def send_wide(right, out, s):
        copies = [
            pltpu.make_async_copy(
                wg_v.at[pl.ds(j * side, side)], out.at[s, pl.ds(j * side, side)], wide_sems.at[j]
            )
            for j in range(experts)
        ]
        for j in range(experts):
            wg_v[pl.ds(j * side, side)] = wide_grad(right, s, j)
            copies[j].start()
        for copy in copies:
            copy.wait()

    def send_tall(s):
        at = pl.ds(pl.multiple_of(s * short, short), short)
        per = short // toks
        copies = []
        for j in range(experts):
            value = dot(scaled[j, :, at], cot_rows[j], 0, 0).astype(BF)
            for i in range(per):
                place_at = j * per + i
                stage[place_at] = value[i * toks : (i + 1) * toks]
                copies.append(pltpu.make_async_copy(
                    stage.at[place_at], d_down.at[s, pl.ds(place_at * toks, toks)],
                    out_sems.at[place_at]))
                copies[-1].start()
        for copy in copies:
            copy.wait()

    dw = KeptScatter(seq, d_gate[0], 1, wu_v, *dw_scratch)
    for t in dw.order:
        send_wide(ggate, d_gate[0], seq.at(t) * 2 + 1 - seq.inner)
        dw.start_place(t)
    grad_step(scatter.order[0])
    for t in dw.order:
        for j in range(experts):
            wu_v[pl.ds((t * experts + j) * side, side)] = wide_grad(
                ggate, seq.at(t) * 2 + seq.inner, j
            )
        if t:
            dw.step(t, 0)
    if len(scatter.order) > 2:
        grad_step(scatter.order[1])
    each(seq.size, lambda s: send_wide(gup, d_up, s))
    for t in scatter.order[2:-1]:
        grad_step(t)
    each(seq.size, send_tall)

    for j in range(experts):
        weight_copy(2, j).wait()

        def out_tile(d, j=j):
            at = pl.ds(pl.multiple_of(d * TILE, TILE), TILE)
            value = dot(scaled[j], wd_v[:, at])
            stage[:, j * slots : (j + 1) * slots, at] = value.astype(BF).reshape(groups, slots, TILE)

        each(width // TILE, out_tile)
        if j + 1 < experts:
            weight_copy(2, j + 1).start()

    def out_copy(e):
        return pltpu.make_async_copy(stage.at[e], out_parts.at[e], out_sems.at[e])

    def out_place(e):
        stage[e] = dot(sel_t[e], stage[e]).astype(BF)
        out_copy(e).start()

    each(groups, out_place)
    grad_step(0)
    d_gate[1][...] = dw.step(0, 0)
    each(groups, lambda e: out_copy(e).wait())
    scatter.finish()
    dw.finish()


def run_experts(n2, cot, sel, sel_t, gates, wg, wu, wd):
    seq_count, group_count = lax.axis_size("seq"), lax.axis_size("expert")
    experts, width, ff = wg.shape
    toks = n2.shape[1]
    rows = gates.shape[1]
    outer_count = group_count // 2
    columns = width + 128
    dma = pltpu.SemaphoreType.DMA
    side, short = width // seq_count, ff // seq_count

    def kernel(*refs):
        ins, outs, scratch = refs[:8], refs[8:14], refs[14:]
        expert_kernel(*ins, outs[0], outs[1], (outs[2], outs[3]), outs[4], outs[5], *scratch)

    low = lambda *shape: pltpu.VMEM(shape, BF)
    return call(
        kernel, 6, 120,
        (jax.ShapeDtypeStruct((toks, columns), F32),
         jax.ShapeDtypeStruct((group_count, toks, width), BF),
         jax.ShapeDtypeStruct((seq_count, experts * side, ff), BF),
         jax.ShapeDtypeStruct((experts * side, ff), F32),
         jax.ShapeDtypeStruct((seq_count, experts * side, ff), BF),
         jax.ShapeDtypeStruct((seq_count, experts * short, width), BF)),
        [low(group_count, toks, width), low(group_count, toks, columns),
         low(experts, rows, width), low(experts, rows, width),
         low(width, ff), low(width, ff), low(ff, width),
         low(experts, rows, ff), low(experts, rows, ff), low(experts, rows, ff),
         pltpu.VMEM((experts, rows, 128), F32),
         low(outer_count, toks, columns), low(outer_count - 1, toks, columns),
         dma((2, group_count)), dma((3,)), dma((4, outer_count, GRAD_CHUNKS)), dma((experts,)),
         dma((group_count,))]
        + kept_scratch("seq", experts * side, ff, 1),
        n2, cot, sel, sel_t, gates, wg, wu, wd,
        specs=[ANY, ANY, IN_VMEM, IN_VMEM, IN_VMEM, ANY, ANY, ANY],
        out_specs=(IN_VMEM, ANY, ANY, IN_VMEM, ANY, ANY),
    )


LAST_CHUNKS = 2


def last_kernel(
    normed_parts, three_parts, out_parts, tokens, gain, grad_hidden, small, *refs, extra
):
    expert_parts, refs = refs[:extra], refs[extra:]
    d_tokens, d_three, d_out, small_out = refs[:4]
    expert_sums, scratch = refs[4 : 4 + extra], refs[4 + extra :]
    expert_scratch, scratch = scratch[: extra * SCATTER_REFS], scratch[extra * SCATTER_REFS :]
    seq, group = Ring("seq"), Ring("expert")
    others = [{"seq": seq.me ^ d} for d in range(1, seq.size)]
    steps = [{"expert": group.me ^ (1 << i)} for i in range((group.size - 1).bit_length())]
    steps += [{"seq": seq.me ^ (1 << i)} for i in range((seq.size - 1).bit_length())]
    known = [{"expert": group.me ^ (1 << i)} for i in range((group.size - 1).bit_length())]
    greet(others + known + [group.next, group.last])
    n = SCATTER_REFS
    normed = Scatter(seq, normed_parts, LAST_CHUNKS, *scratch[:n])
    outs = Scatter(group, out_parts, 1, *scratch[n : 2 * n])
    three = Scatter(group, three_parts, LAST_CHUNKS, *scratch[2 * n : 3 * n])
    three_low, sum_buf, sum_land, own_sem, swap_sems, sum_sems = scratch[3 * n :]
    experts = [
        Scatter(seq, ref, 1, *expert_scratch[i * n : (i + 1) * n])
        for i, ref in enumerate(expert_parts)
    ]
    normed.start()
    for t in three.order:
        three.start_place(t)
        outs.start_place(t)
    for scatter in experts:
        scatter.start()
    for t in normed.order[:-1]:
        for c in range(LAST_CHUNKS):
            normed.step(t, c)
    for scatter in experts:
        scatter.step(scatter.order[0], 0)
    gain_sum = jnp.zeros((1, tokens.shape[1]), F32)
    for c in range(LAST_CHUNKS):
        cut = normed.cut(c)
        grad = normed.step(0, c)
        value = tokens[cut].astype(F32)
        scale = lax.rsqrt(jnp.mean(value * value, axis=-1, keepdims=True) + norm_eps)
        unit = value * scale
        gained = grad * gain[...]
        mean = jnp.mean(gained * unit, axis=-1, keepdims=True)
        d_tokens[cut] = grad_hidden[cut] + scale * (gained - unit * mean)
        gain_sum = gain_sum + jnp.sum(grad * unit, axis=0, keepdims=True)
    sum_buf[0] = small[...]
    last_row = small.shape[0] - 1
    sum_buf[0, pl.ds(last_row, 1)] = gain_sum

    def sum_copy(i):
        return remote(sum_buf.at[i], sum_land.at[i], sum_sems.at[0, i], sum_sems.at[1, i], steps[i])

    def sum_step(i):
        sum_copy(i).wait_recv()
        total = sum_buf[i] + sum_land[i]
        if i + 1 < len(steps):
            sum_buf[i + 1] = total
            sum_copy(i + 1).start()
        else:
            small_out[...] = total

    for t in three.order[:-1]:
        for c in range(LAST_CHUNKS):
            three.step(t, c)
        outs.step(t, 0)
    for c in range(LAST_CHUNKS):
        three_low[three.cut(c)] = three.step(0, c).astype(BF)
    wrows = three_low.shape[0] // seq.size

    def swap_copy(d):
        src = three_low.at[pl.ds((seq.me ^ d) * wrows, wrows)]
        return remote(src, d_three.at[seq.me], swap_sems.at[0, d], swap_sems.at[1, d], others[d - 1])

    for d in range(1, seq.size):
        swap_copy(d).start()
    own = pltpu.make_async_copy(
        three_low.at[pl.ds(seq.me * wrows, wrows)], d_three.at[seq.me], own_sem.at[0]
    )
    own.start()
    d_out[...] = outs.step(0, 0)
    sum_copy(0).start()
    for i in range(len(steps)):
        sum_step(i)
    for scatter, out in zip(experts, expert_sums):
        for t in scatter.order[1:-1]:
            scatter.step(t, 0)
        out[...] = scatter.step(0, 0)
    for d in range(1, seq.size):
        there = d_three.at[seq.me ^ d]
        remote(there, there, swap_sems.at[0, d], swap_sems.at[1, d], others[d - 1]).wait_recv()
        swap_copy(d).wait_send()
    own.wait()
    for i in range(len(steps)):
        sum_copy(i).wait_send()
    for scatter in (normed, three, outs, *experts):
        scatter.finish()


def finish_all(normed_parts, three_parts, out_parts, tokens, gain, grad_hidden, small, *expert_parts):
    seq_count, group_count = lax.axis_size("seq"), lax.axis_size("expert")
    rows, width = tokens.shape
    rows3, cols3 = three_parts.shape[1:]
    wrows = rows3 // seq_count
    count = (seq_count - 1).bit_length() + (group_count - 1).bit_length()
    dma = pltpu.SemaphoreType.DMA
    return call(
        partial(last_kernel, extra=len(expert_parts)), 5, 110,
        (jax.ShapeDtypeStruct((rows, width), F32),
         jax.ShapeDtypeStruct((seq_count, wrows, cols3), BF),
         jax.ShapeDtypeStruct(out_parts.shape[1:], F32),
         jax.ShapeDtypeStruct(small.shape, F32))
        + tuple(jax.ShapeDtypeStruct(e.shape[1:], F32) for e in expert_parts),
        sum([scatter_scratch("seq", e.shape[1], e.shape[2], 1) for e in expert_parts], [])
        + scatter_scratch("seq", rows, width, LAST_CHUNKS)
        + scatter_scratch("expert", out_parts.shape[1], width, 1)
        + scatter_scratch("expert", rows3, cols3, LAST_CHUNKS)
        + [pltpu.VMEM((rows3, cols3), BF), pltpu.VMEM((count,) + small.shape, F32),
           pltpu.VMEM((count,) + small.shape, F32), dma((1,)), dma((2, seq_count)), dma((2, count))],
        normed_parts, three_parts, out_parts, tokens, gain[None], grad_hidden, small, *expert_parts,
        specs=[ANY, ANY, ANY, IN_VMEM, IN_VMEM, IN_VMEM, IN_VMEM] + [ANY] * len(expert_parts),
        out_specs=(IN_VMEM, ANY, IN_VMEM, IN_VMEM) + (IN_VMEM,) * len(expert_parts),
    )


def each(left, right, how):
    return jnp.einsum(how, left, right, preferred_element_type=F32)


def plain_experts(normed2_all, cot_all, chosen, gate_rows, w_gate, w_up, w_down):
    seq_count, group_count = lax.axis_size("seq"), lax.axis_size("expert")
    experts_local, tok_rows = w_gate.shape[0], chosen.shape[-1]
    total_experts = experts_local * group_count
    chosen_low = chosen.astype(BF)

    def pick_rows(values):
        return jnp.einsum("ejmt,etd->jemd", chosen_low, values, preferred_element_type=F32).astype(BF)

    def place_rows(values):
        return jnp.einsum("ejmt,jemd->etd", chosen_low, values, preferred_element_type=F32).astype(BF)

    routed = pick_rows(normed2_all)
    cot_rows = pick_rows(cot_all)

    gate_pre = each(routed, w_gate, "jemd,jdf->jemf")
    up_pre = each(routed, w_up, "jemd,jdf->jemf")
    sigmoid_gate = jax.nn.sigmoid(gate_pre)
    silu_gate = gate_pre * sigmoid_gate
    active = silu_gate * up_pre
    active_low = active.astype(BF)
    grad_unit = each(cot_rows, w_down, "jemd,jfd->jemf")
    grad_gate_rows = jnp.sum(grad_unit * active_low.astype(F32), axis=-1)
    grad_active = grad_unit * gate_rows
    grad_gate_low = (
        grad_active * up_pre * sigmoid_gate * (1.0 + gate_pre * (1.0 - sigmoid_gate))
    ).astype(BF)
    grad_up_low = (grad_active * silu_gate).astype(BF)
    grad_routed = each(grad_gate_low, w_gate, "jemf,jdf->jemd")
    grad_routed = (grad_routed + each(grad_up_low, w_up, "jemf,jdf->jemd")).astype(BF)
    grad_parts = place_rows(grad_routed)
    grad_normed2 = sum_rows(grad_parts)
    grad_probs_parts = jnp.einsum(
        "ejmt,jem->etj", chosen.astype(F32), grad_gate_rows, precision=lax.Precision.HIGHEST
    )
    grad_probs = lax.all_to_all(grad_probs_parts, "expert", split_axis=0, concat_axis=0, tiled=True)
    grad_probs = grad_probs.transpose(1, 0, 2).reshape(tok_rows, total_experts)

    expert_out = each(active_low, w_down, "jemf,jfd->jemd") * gate_rows
    out_parts = place_rows(expert_out.astype(BF))

    active_scaled = (active_low.astype(F32) * gate_rows).astype(BF)

    def expert_grad(left, right):
        grad = jnp.einsum("jemd,jemf->jdf", left, right, preferred_element_type=F32).astype(BF)
        rows = grad.shape[1] // seq_count
        grad = grad.reshape(experts_local, seq_count, rows, grad.shape[2])
        return scatter_sum(
            [lax.dynamic_index_in_dim(grad, o, 1, keepdims=False) for o in owners("seq")], "seq"
        )

    d_w_gate = expert_grad(routed, grad_gate_low)
    d_w_up = expert_grad(routed, grad_up_low)
    d_w_down = expert_grad(active_scaled, cot_rows)
    return grad_normed2, grad_probs, out_parts, d_w_gate, d_w_up, d_w_down


def local(
    tokens,
    lengths,
    routes,
    gain_attn,
    w_query,
    w_key,
    w_value,
    gain_query,
    gain_key,
    w_out,
    gain_mlp,
    router,
    w_gate,
    w_up,
    w_down,
    cotangent,
):
    seq_count = lax.axis_size("seq")
    group_count = lax.axis_size("expert")
    seq_me = lax.axis_index("seq")
    group_me = lax.axis_index("expert")
    tok_rows, width = tokens.shape[1], tokens.shape[2]
    head_dim = width // HEADS
    heads = HEADS // seq_count
    cols = width // seq_count
    wrows = w_query.shape[0]
    length = tok_rows * seq_count
    experts_local = w_gate.shape[0]
    total_experts = experts_local * group_count
    slots = MOST
    score_scale = head_dim ** (-0.5)
    inputs = tokens[0].astype(F32)

    places = jnp.arange(length, dtype=jnp.int32)
    doc_ends = jnp.cumsum(lengths[0])
    passed = (places[:, None] >= doc_ends[None, :]).astype(jnp.int32)
    docs = jnp.sum(passed, axis=1)
    offsets = places - jnp.sum(passed * lengths[0][None, :], axis=1)
    allowed = (docs[:, None] == docs[None, :]) & (places[None, :] <= places[:, None])
    half = head_dim // 2
    inverse = 10000.0 ** (-jnp.arange(half, dtype=F32) / half)
    angles = offsets.astype(F32)[:, None] * inverse[None, :]
    cosine = jnp.cos(angles)[:, None, :]
    sine = jnp.sin(angles)[:, None, :]

    def turn(values, sine_table):
        first, second = values[..., :half], values[..., half:]
        return jnp.concatenate(
            [first * cosine - second * sine_table, second * cosine + first * sine_table], axis=-1
        )

    expert_ids = jnp.arange(128, dtype=jnp.int32)
    hits = jnp.any(routes[0][:, :, None] == expert_ids[None, None, :], axis=1).astype(BF)
    cot_all = lax.all_gather(cotangent[0], "expert", axis=0)
    w_rows = lax.all_gather(w_out, "expert", axis=0, tiled=True)
    normed, attn_norm_back = jax.vjp(rms_norm, inputs, gain_attn)
    wq_cols, wk_cols, wv_cols, normed_all, hits_all = gather_weights(
        w_query, w_key, w_value, normed.astype(BF), hits
    )
    normed_all = normed_all.reshape(length, width)
    w_cols = [w.reshape(width, cols) for w in (wq_cols, wk_cols, wv_cols)]
    query_raw = product(normed_all, w_cols[0])
    key_raw = product(normed_all, w_cols[1])
    value_low = product(normed_all, w_cols[2]).astype(BF).reshape(length, heads, head_dim)

    def row_sums(left, right):
        sums = jnp.stack([jnp.sum(left, axis=1), jnp.sum(right, axis=1)])
        return lax.psum(sums, "seq") / width

    inv_rms = lax.rsqrt(row_sums(query_raw**2, key_raw**2) + norm_eps)
    gain_q = lax.dynamic_slice_in_dim(gain_query, seq_me * cols, cols)
    gain_k = lax.dynamic_slice_in_dim(gain_key, seq_me * cols, cols)
    query_unit = query_raw * inv_rms[0][:, None]
    key_unit = key_raw * inv_rms[1][:, None]
    query_low = turn((query_unit * gain_q).reshape(length, heads, head_dim), sine).astype(BF)
    key_low = turn((key_unit * gain_k).reshape(length, heads, head_dim), sine).astype(BF)
    scores = jnp.einsum("qhd,khd->hqk", query_low, key_low, preferred_element_type=F32)
    scores = jnp.where(allowed[None], scores * score_scale, masked_score)
    top_score = jnp.max(scores, axis=-1, keepdims=True)
    weights = jnp.exp(scores - top_score)
    probs = weights / jnp.sum(weights, axis=-1, keepdims=True)
    probs_low = probs.astype(BF)
    attended = jnp.einsum("hqk,khd->qhd", probs_low, value_low, preferred_element_type=F32)
    attended_low = attended.reshape(length, cols).astype(BF)
    hidden_parts = product(attended_low, w_rows).astype(BF).reshape(seq_count, tok_rows, width)
    hidden, normed2_all = hidden_and_rows(hidden_parts, tokens[0], gain_mlp)
    normed2, mlp_norm_back = jax.vjp(rms_norm, hidden, gain_mlp)
    normed2_low = normed2.astype(BF)

    first_expert = group_me * experts_local
    hit = lax.dynamic_slice_in_dim(hits_all, first_expert, experts_local, axis=2)
    hit = hit.transpose(0, 2, 1)
    before = (jnp.arange(tok_rows)[:, None] < jnp.arange(tok_rows)[None, :]).astype(BF)
    rank = jnp.einsum("ejt,tu->eju", hit, before, preferred_element_type=F32)
    slot_ids = jnp.arange(slots, dtype=jnp.int32)
    chosen = (hit[:, :, None, :] > 0) & (rank.astype(jnp.int32)[:, :, None, :] == slot_ids[None, None, :, None])
    chosen_low = chosen.astype(BF)

    logits_all = jnp.einsum("etd,dn->etn", normed2_all, router, preferred_element_type=F32)
    probs_all = jax.nn.softmax(logits_all, axis=-1)
    mine = lax.dynamic_slice_in_dim(probs_all, first_expert, experts_local, axis=2)
    gate_rows = jnp.einsum(
        "ejmt,etj->jem", chosen.astype(F32), mine, precision=lax.Precision.HIGHEST
    )[..., None]

    roomy = group_count * slots <= 512
    if roomy:
        both = chosen_low.reshape(group_count, experts_local * slots, tok_rows)
        gate_wide = jnp.broadcast_to(
            gate_rows.reshape(experts_local, group_count * slots, 1),
            (experts_local, group_count * slots, 128),
        )
        rows_sum, out_parts, _, d_w_gate, up_parts, down_parts = run_experts(
            normed2_all, cot_all, both, both.transpose(0, 2, 1), gate_wide, w_gate, w_up, w_down
        )
        grad_normed2 = rows_sum[:, :width]
        grad_probs = (
            rows_sum[:, width : width + total_experts]
            + rows_sum[:, width + total_experts : width + 2 * total_experts]
        )
        expert_parts = (up_parts, down_parts)
    else:
        grad_normed2, grad_probs, out_parts, d_w_gate, d_w_up, d_w_down = plain_experts(
            normed2_all, cot_all, chosen, gate_rows, w_gate, w_up, w_down
        )
        expert_parts = ()
    out_sum = lax.psum_scatter(out_parts, "expert", scatter_dimension=0, tiled=False)

    router_probs, softmax_back = jax.vjp(
        partial(jax.nn.softmax, axis=-1), product(normed2_low, router)
    )
    (grad_logits,) = softmax_back(grad_probs)
    grad_logits_low = grad_logits.astype(BF)
    grad_router = jnp.einsum("td,te->ed", normed2_low, grad_logits_low, preferred_element_type=F32)
    grad_normed2 = grad_normed2 + jnp.einsum(
        "te,de->td", grad_logits_low, router, preferred_element_type=F32
    )
    grad_hidden_part, grad_gain_mlp = mlp_norm_back(grad_normed2)
    grad_hidden = cotangent[0].astype(F32) + grad_hidden_part

    grad_hidden_all = gather_pack(grad_hidden.astype(BF)).reshape(length, width)
    grad_attended = jnp.einsum(
        "te,de->td", grad_hidden_all, w_rows, preferred_element_type=F32
    ).astype(BF)
    grad_attended = grad_attended.reshape(length, heads, head_dim)
    grad_w_out = jnp.einsum(
        "td,te->de", attended_low, grad_hidden_all, preferred_element_type=F32
    ).astype(BF).reshape(group_count, wrows, width)
    grad_probs_attn = jnp.einsum(
        "qhd,khd->hqk", grad_attended, value_low, preferred_element_type=F32
    )
    row_dot = jnp.sum(probs * grad_probs_attn, axis=-1, keepdims=True)
    grad_scores = (probs * (grad_probs_attn - row_dot)).astype(BF)
    grad_query = jnp.einsum("hqk,khd->qhd", grad_scores, key_low, preferred_element_type=F32)
    grad_key = jnp.einsum("hqk,qhd->khd", grad_scores, query_low, preferred_element_type=F32)
    grad_value = jnp.einsum("hqk,qhd->khd", probs_low, grad_attended, preferred_element_type=F32)
    grad_query = turn(grad_query * score_scale, -sine).reshape(length, cols)
    grad_key = turn(grad_key * score_scale, -sine).reshape(length, cols)
    grad_gain_query = jnp.sum(grad_query * query_unit, axis=0)
    grad_gain_key = jnp.sum(grad_key * key_unit, axis=0)
    grad_query_g, grad_key_g = grad_query * gain_q, grad_key * gain_k
    means = row_sums(grad_query_g * query_unit, grad_key_g * key_unit)
    grad_query_low = (
        inv_rms[0][:, None] * (grad_query_g - query_unit * means[0][:, None])
    ).astype(BF)
    grad_key_low = (inv_rms[1][:, None] * (grad_key_g - key_unit * means[1][:, None])).astype(BF)
    grad_value_low = grad_value.reshape(length, cols).astype(BF)
    grad_three = jnp.concatenate([grad_query_low, grad_key_low, grad_value_low], axis=1)
    grad_normed_parts = each(grad_query_low, w_cols[0], "te,de->td")
    grad_normed_parts += each(grad_key_low, w_cols[1], "te,de->td")
    grad_normed_parts += each(grad_value_low, w_cols[2], "te,de->td")
    grad_normed_parts = grad_normed_parts.astype(BF).reshape(seq_count, tok_rows, width)
    grad_w_three = jnp.einsum(
        "td,te->de", normed_all, grad_three, preferred_element_type=F32
    ).astype(BF).reshape(seq_count, group_count, wrows, 3 * cols)
    grad_w_three = grad_w_three.transpose(1, 0, 2, 3).reshape(
        group_count, seq_count * wrows, 3 * cols
    )

    def full(value):
        return lax.dynamic_update_slice(jnp.zeros((width,), F32), value, (seq_me * cols,))

    rows = [grad_router, grad_gain_mlp[None], full(grad_gain_query)[None], full(grad_gain_key)[None]]
    small = jnp.concatenate(rows)
    spare = -(total_experts + 4) % 8 + 1
    small = jnp.concatenate([small, jnp.zeros((spare, width), F32)])
    d_tokens, d_three, d_w_out, small, *expert_sums = finish_all(
        grad_normed_parts, grad_w_three, grad_w_out, tokens[0], gain_attn, grad_hidden, small,
        *expert_parts,
    )
    mixed = hidden + after(out_sum, d_w_out).astype(F32)
    if roomy:
        d_w_gate = d_w_gate.reshape(experts_local, width // seq_count, -1)
        d_w_up = expert_sums[0].reshape(experts_local, width // seq_count, -1)
        d_w_down = expert_sums[1].reshape(experts_local, -1, width)
    d_three = d_three.reshape(seq_count, wrows, 3, cols).transpose(2, 1, 0, 3)
    d_three = d_three.reshape(3, wrows, width).astype(F32)
    return (
        mixed.astype(BF)[None],
        d_tokens[None],
        small[-1],
        d_three[0],
        d_three[1],
        d_three[2],
        small[total_experts + 1],
        small[total_experts + 2],
        d_w_out,
        small[total_experts],
        small[:total_experts].T,
        d_w_gate,
        d_w_up,
        d_w_down,
    )


def solution(mesh):
    return jax.shard_map(
        local,
        mesh=mesh,
        in_specs=(
            P("expert", "seq", None),
            P("expert", None),
            P("expert", "seq", None),
            P(),
            P(("seq", "expert"), None),
            P(("seq", "expert"), None),
            P(("seq", "expert"), None),
            P(),
            P(),
            P(("seq", "expert"), None),
            P(),
            P(),
            P("expert", None, None),
            P("expert", None, None),
            P("expert", None, None),
            P("expert", "seq", None),
        ),
        out_specs=(
            P("expert", "seq", None),
            P("expert", "seq", None),
            P(),
            P(("seq", "expert"), None),
            P(("seq", "expert"), None),
            P(("seq", "expert"), None),
            P(),
            P(),
            P(("seq", "expert"), None),
            P(),
            P(),
            P("expert", "seq", None),
            P("expert", "seq", None),
            P("expert", "seq", None),
        ),
        check_vma=False,
    )
```

time: 848 us -> 581 us (0.69)
  waiting for transfers between devices: 461 us -> 1.44 us
  Pallas kernels: 0 us -> 420 us
  matrix products: 136 us -> 47.3 us
  starting transfers between devices: 62 us -> 0.11 us
  other arithmetic: 71.2 us -> 26 us
  blocking collectives: 46.5 us -> 12.9 us
  between operations: 3.26 us -> 14.9 us
    ppermute x93 -> x0, waiting for transfers between devices: 461 us -> none  [the longest x31 261 us: shift(): return lax.ppermute(value, axis, [(i, (i + 2) % n) for i in range(n)])]
    pallas_call x0 -> x5, Pallas kernels: none -> 420 us  [call(): pl.pallas_call(kernel, out_shape=outs, in_specs=specs or [ANY] * len(args...]
    dot_general x6 -> x3, matrix products: 65 us -> 5.34 us  [each(): return jnp.einsum(how, left, right, preferred_element_type=F32)]
    ppermute x93 -> x0, starting transfers between devices: 58.3 us -> none  [the longest x46 36.2 us: swap(): return lax.ppermute(value, axis, [(i, i ^ 1) for i in range(n)])]
    dot_general x10 -> x1, matrix products: 39.4 us -> 0.15 us  [local(): rank = jnp.einsum('ejt,tu->eju', hit, before, preferred_element_type=F32)]
    all_gather x1 -> x0, blocking collectives: 30.7 us -> none  [local(): picks = lax.all_gather(routes[0], 'expert', axis=0)[order]]
    convert_element_type x20 -> x5, other arithmetic: 27 us -> 3.81 us  [the longest x1 1.53 us: local(): grad_hidden_all = gather_pack(grad_hidden.astype(BF)).reshape(length, width)]
    add x17 -> x0, other arithmetic: 18.7 us -> none  [the longest x5 18.4 us: scatter_sum(): total = arrived.astype(F32) + pairs[(t + 1) % outer_count]]
  transfers between devices with their start and end apart: 94 -> 3, of which waited for: 41 -> 0; matrix products, arithmetic and copies ran while one was open for 20% -> 19% of each run, Pallas kernels for 0% -> 54%
where the time goes in v2:
time: 581 us; the launch traced here: 575 us
  Pallas kernels  420 us (72%)
  local copies, waits for them, and re-layouts  52.4 us (9%)
  matrix products  47.3 us (8%)
  other arithmetic  26 us (4%)
  between operations  14.9 us (3%)
  blocking collectives  12.9 us (2%)
    pallas_call x5, Pallas kernels, call(): pl.pallas_call(kernel, out_shape=outs, in_specs=specs or [ANY] * len(args...  420 us
    unnamed x102, local copies, waits for them, and re-layouts  25.3 us
    psum x2, blocking collectives, row_sums(): return lax.psum(sums, 'seq') / width  12.9 us
    dot_general x5, matrix products, product(): return jnp.dot(left, right, preferred_element_type=F32)  12.6 us
  transfers between devices with their start and end apart: 3, of which 0 were waited for; matrix products, arithmetic and copies ran while one was open for 19% of the time, Pallas kernels for 54%

profile of v2, /device:TPU:0, one launch (start us, length us, event | category | flops | bytes accessed | tf_op | source)
XLA Modules:
  0.0 574.9 jit_solution(10983559912385024335)
XLA Ops:
  12.5 2.0 fusion.14.normed
  14.5 103.3 %shard_map.263 = (bf16[4,512,512]{2,1,0:T(8,128)(2,1)}, bf16[4,512,512]{2,1,0:T(8,128)(2,1)}, bf16[4,512,512]{2,1,0:T(8,128)(2,1)}, bf16[4,128,2048]{2,1,0:T(8,128)(2,1)}, bf16[8,128,128]{2,1,0:T(8,128)(2,1)}) custom-call(bf16[64,2048]{1,0:T(8,128)(2,1)} %wq.1, bf16[64,2048]{1,0:T(8,128)(2,1)} %wk.1, bf16[64,2048]{1,0:T(8,128)(2,1)} %wv.1, ...), custom_call_target="tpu_custom_call" | custom-call | bytes 270000000 | tf_op jit(solution)/shard_map/pallas_call | solution.py:326
  117.9 3.7 multiply_reduce_fusion.7
  122.9 6.8 %psum.14 = f32[2,512]{1,0:T(2,128)S(1)} all-reduce(f32[2,512]{1,0:T(2,128)S(1)} %pad_maximum_fusion.4), channel_id=1, replica_groups=mesh['seq'=4,'expert'=8] {'seq'}, use_global_device_ids=true, to_apply=%region_6.7 | all-reduce | flops 1024 | bytes 8192 | tf_op jit(solution)/shard_map/psum | solution.py:1022
  137.8 2.4 copy.209
  140.2 1.8 broadcast_compare_fusion
  143.8 1.8 copy.175
  146.7 2.0 copy.174
  152.0 2.0 fusion.28
  153.9 3.0 subtract_convert_fusion.1
  157.0 5.8 %fusion.49 = (f32[4,512]{1,0:T(4,128)S(1)}, f32[4,512,512]{1,2,0:T(8,128)}) fusion(pred[512,512]{0,1:T(8,128)(4,1)} %fusion.20, bf16[512,4,64]{2,0,1:T(8,128)(2,1)} %get-tuple-element.83, bf16[512,4,64]{2,0,1:T(8,128)(2,1)} %get-tuple-element.84, bf16[512,4,64]{2,0,1:T(8,128)(2,1)} %get-tuple-element.67, bf16[512,4,64]{2,0,1:T(8,128)(2,1)} %get-tuple-element.66), kind=kOutput, calls=%fused_computation.126 | convolution fusion | flops 274727424 | bytes 5513216 | tf_op jit(solution)/shard_map/sub | solution.py:1034
  162.7 3.0 convolution_convert_fusion.4
  166.3 4.4 convolution_convert_fusion.2
  170.7 60.1 %shard_map.264 = (f32[128,2048]{1,0:T(8,128)}, bf16[8,128,2048]{2,1,0:T(8,128)(2,1)}) custom-call(bf16[4,128,2048]{2,1,0:T(8,128)(2,1)} %bitcast.156, bf16[128,2048]{1,0:T(8,128)(2,1)} %bitcast.141, f32[1,2048]{1,0:T(1,128)} %bitcast.174), custom_call_target="tpu_custom_call" | custom-call | bytes 180000000 | tf_op jit(solution)/shard_map/pallas_call | solution.py:326
  230.8 3.5 fusion.50
  237.7 109.3 %shard_map.265 = (f32[128,2176]{1,0:T(8,128)}, bf16[8,128,2048]{2,1,0:T(8,128)(2,1)}, bf16[4,1024,1024]{2,1,0:T(8,128)(2,1)}, f32[1024,1024]{1,0:T(8,128)}, bf16...) custom-call(bf16[8,128,2048]{2,1,0:T(8,128)(2,1)} %get-tuple-element.38.refs_0_, ...), custom_call_target="tpu_custom_call" | custom-call | bytes 360000000 | tf_op jit(solution)/shard_map/pallas_call | solution.py:326
  348.2 1.9 multiply_reduce_fusion.1
  351.6 17.8 %shard_map.266 = bf16[4,128,2048]{2,1,0:T(8,128)(2,1)} custom-call(bf16[128,2048]{1,0:T(8,128)(2,1)} %get-tuple-element.60.rows_in), custom_call_target="tpu_custom_call" | custom-call | bytes 54000000 | tf_op jit(solution)/shard_map/pallas_call | solution.py:326
  369.5 3.8 convolution_convert_fusion.3
  381.5 1.6 copy.187
  384.7 6.2 %psum.15 = f32[2,512]{1,0:T(2,128)S(1)} all-reduce(f32[2,512]{1,0:T(2,128)S(1)} %pad_maximum_fusion.5), channel_id=1, replica_groups=mesh['seq'=4,'expert'=8] {'seq'}, use_global_device_ids=true, to_apply=%region_21.22 | all-reduce | flops 1024 | bytes 8192 | tf_op jit(solution)/shard_map/psum | solution.py:1022
  390.9 1.6 multiply_convert_fusion.2
  395.3 4.9 convolution_convert_fusion
  400.3 3.3 copy.189
  406.3 3.8 convolution_convert_fusion.1
  413.5 2.7 add_convert_fusion
  416.2 129.3 %shard_map.267 = (f32[128,2048]{1,0:T(8,128)}, bf16[4,64,1536]{2,1,0:T(8,128)(2,1)}, f32[64,2048]{1,0:T(8,128)}, f32[24,2048]{1,0:T(8,128)}, f32[1024,1024]{1,0:T(8,128)}, /*index=5*/f32[512,2048]{1,0:T(8,128)}) custom-call(bf16[4,128,2048]{2,1,0:T(8,128)(2,1)} %bitcast.143, bf16[8,256,1536]{2,1,0:T(8,128)(2,1)} %bitcast.140, ...), custom_call_target="tpu_custom_call" | custom-call | bytes 330000000 | tf_op jit(solution)/shard_map/pallas_call | solution.py:326
  545.5 2.7 reshape.342
  554.7 2.1 fusion.21
  558.5 2.1 copy.226
  562.2 2.1 copy.227
  565.9 2.0 copy.228
  (183 shorter events, 57.3 us)
Async XLA Ops:
  7.2 223.6 %copy-start = (bf16[2048,16]{0,1:T(8,128)(2,1)S(1)}, bf16[2048,16]{0,1:T(8,128)(2,1)}, u32[]{:S(2)}) copy-start(bf16[2048,16]{0,1:T(8,128)(2,1)} %param.27) | copy-start | bytes 196612
  7.2 159.1 %all-gather.3.cloned.1.call-start = ((), (), s32[]{:S(2)}) async-start(), calls=%async_computation.1 | async-start | bytes 2359296 | tf_op jit(solution)/shard_map/all_gather | solution.py:1009
  7.9 228.7 %all-gather.5.cloned.1.call-start = ((), (), s32[]{:S(2)}) async-start(), calls=%async_computation.2 | async-start | bytes 4718592 | tf_op jit(solution)/shard_map/all_gather | solution.py:1008
  8.7 546.0 %reduce-scatter.2.cloned.1.call-start = ((), (), s32[]{:S(2)}) async-start(), calls=%async_computation.3 | async-start | bytes 4718592 | tf_op jit(solution)/shard_map/reduce_scatter | solution.py:1081
  117.8 3.7 copy-start.27
  117.8 3.7 copy-start.40
  121.5 8.9 %copy-start.7 = (f32[512,512]{0,1:T(8,128)}, f32[512,512]{0,1:T(8,128)S(1)}, u32[]{:S(2)}) copy-start(f32[512,512]{0,1:T(8,128)S(1)} %get-tuple-element.99) | copy-start | bytes 3145732
  122.9 12.3 %copy-start.5 = (f32[512,512]{0,1:T(8,128)}, f32[512,512]{0,1:T(8,128)S(1)}, u32[]{:S(2)}) copy-start(f32[512,512]{0,1:T(8,128)S(1)} %get-tuple-element.97) | copy-start | bytes 3145732
  141.9 9.0 %copy-start.39 = (s32[1,4]{1,0:T(1,128)S(1)}, s32[1,4]{1,0:T(1,128)}, u32[]{:S(2)}) copy-start(s32[1,4]{1,0:T(1,128)} %param.17) | copy-start | bytes 52
  150.1 6.9 %copy-start.20 = (bf16[8,128,128]{1,2,0:T(8,128)(2,1)}, bf16[8,128,128]{1,2,0:T(8,128)(2,1)S(1)}, u32[]{:S(2)}) copy-start(bf16[8,128,128]{1,2,0:T(8,128)(2,1)S(1)} %and_convert_fusion) | copy-start | bytes 786436
  153.9 3.0 copy-start.21
  157.0 5.8 %copy-start.23 = (bf16[4,512,512]{2,1,0:T(8,128)(2,1)S(1)}, bf16[4,512,512]{2,1,0:T(8,128)(2,1)}, u32[]{:S(2)}) copy-start(bf16[4,512,512]{2,1,0:T(8,128)(2,1)} %get-tuple-element.34) | copy-start | bytes 6291460
  162.7 3.0 copy-start.12
  166.3 4.4 copy-start.42
  230.8 4.2 copy-start.2
  230.8 4.3 copy-start.38
  347.0 3.1 copy-start.26
  369.5 3.8 copy-start.13
  380.2 3.0 copy-start.6
  390.9 2.5 copy-start.14
  390.9 2.8 copy-start.44
  400.2 3.4 copy-start.11
  400.2 6.0 %copy-start.25 = (bf16[4,128,2048]{2,1,0:T(8,128)(2,1)S(1)}, bf16[4,128,2048]{2,1,0:T(8,128)(2,1)}, u32[]{:S(2)}) copy-start(bf16[4,128,2048]{2,1,0:T(8,128)(2,1)} %shard_map.266) | copy-start | bytes 6291460
  406.3 3.8 copy-start.19
  406.3 3.8 copy-start.29
  550.8 2.6 copy-start.37
  550.8 3.9 copy-start.4
  552.1 4.7 copy-start.34
  554.6 3.1 copy-start.36
  554.7 3.9 copy-start.15
  558.5 3.7 copy-start.17
  562.2 3.7 copy-start.16
  (16 other events, 22.0 us)
Sparse Core Ops, SparseCore 0:
  10.2 76.1 all-gather.2
  88.5 74.8 all-gather.4
  347.1 86.1 reduce-scatter.1

commit v3 on v2

--- a/solution.py
+++ b/solution.py
@@ -254,6 +254,55 @@
                 self.pair_copy(t, c).wait_send()
                 if t:
                     self.ring_copy(t, c).wait_send()
+
+
+class RingFirst:
+    def __init__(self, ring, parts, land, ringbuf, sems):
+        self.ring, self.parts, self.land, self.ringbuf, self.sems = ring, parts, land, ringbuf, sems
+        self.order = list(range(1, ring.outer_count)) + [0]
+
+    def two(self, t):
+        return pl.ds(self.ring.at(t) * 2, 2)
+
+    def ring_copy(self, t):
+        to = (t + 1) % self.ring.outer_count
+        slot = (to - 2) % self.ring.outer_count
+        return remote(self.parts.at[self.two(t)], self.ringbuf.at[slot], self.sems.at[0, t],
+                      self.sems.at[1, to], self.ring.next)
+
+    def pair_copy(self):
+        src = self.parts.at[self.ring.outer * 2 + 1 - self.ring.inner]
+        return remote(src, self.land, self.sems.at[2, 0], self.sems.at[3, 0], self.ring.pair)
+
+    def start(self):
+        self.ring_copy(1).start()
+
+    def step(self, t):
+        self.ring_copy((t - 1) % self.ring.outer_count).wait_recv()
+        slot = (t - 2) % self.ring.outer_count
+        total = self.parts[self.two(t)].astype(F32) + self.ringbuf[slot].astype(F32)
+        self.parts[self.two(t)] = total.astype(BF)
+        if t:
+            self.ring_copy(t).start()
+        else:
+            self.pair_copy().start()
+
+    def last(self):
+        self.pair_copy().wait_recv()
+        mine = self.parts[self.ring.outer * 2 + self.ring.inner]
+        return mine.astype(F32) + self.land[...].astype(F32)
+
+    def finish(self):
+        for t in self.order[:-1]:
+            self.ring_copy(t).wait_send()
+        self.pair_copy().wait_send()
+
+
+def ring_first_scratch(axis, rows, columns):
+    size = lax.axis_size(axis)
+    low = lambda *shape: pltpu.VMEM(shape, BF)
+    return [low(size, rows, columns), low(rows, columns), low(size // 2 - 1, 2, rows, columns),
+            pltpu.SemaphoreType.DMA((4, size // 2))]
 
 
 class KeptScatter(Scatter):
@@ -423,12 +472,103 @@
 HIDDEN_CHUNKS = 2
 
 
-def hidden_kernel(parts, tokens, gain, hidden_out, all_out, *scratch):
+def turn(values, cos_rows, sin_rows):
+    return values * cos_rows + pltpu.roll(values, values.shape[1] // 2, 1) * sin_rows
+
+
+def row_table(left, right):
+    lanes = lax.broadcasted_iota(jnp.int32, (left.shape[0], 128), 1)
+    return jnp.where(lanes == 0, left, jnp.where(lanes == 1, right, 0.0)).T[:8]
+
+
+def from_row_table(table):
+    return jnp.concatenate([table, jnp.zeros((120, table.shape[1]), F32)], axis=0).T
+
+
+def attend_kernel(
+    normed, wq, wk, wv, w_rows, bias, cosine, sine, gain_q, gain_k, tokens, gain,
+    hidden_out, all_out, q_low, k_low, v_low, attended, probs_out, q_unit, k_unit, scales,
+    parts, land, ringbuf, part_sems, low, normed_v, wq_v, wk_v, wv_v, rows_v, probs, row_send, row_land,
+    load_sems, low_sems, g_send, g_recv, row_sems, probs_sems,
+):
     seq, group = Ring("seq"), Ring("expert")
-    greet(seq.partners() + group.partners())
-    scatter = Scatter(seq, parts, HIDDEN_CHUNKS, *scratch[:SCATTER_REFS])
-    low, low_sems, g_send, g_recv = scratch[SCATTER_REFS:]
-    scatter.start()
+    others = [{"seq": seq.me ^ d} for d in range(1, seq.size)]
+    loads = [
+        pltpu.make_async_copy(src, dst, load_sems.at[i])
+        for i, (src, dst) in enumerate(
+            ((normed, normed_v), (wq, wq_v), (wk, wk_v), (wv, wv_v), (w_rows, rows_v))
+        )
+    ]
+    for load in loads:
+        load.start()
+    greet(others + group.partners())
+    length, cols = q_low.shape
+    toks, width = tokens.shape
+    head_dim = cosine.shape[1]
+    heads = cols // head_dim
+    scale = head_dim**-0.5
+
+    def head(h):
+        return slice(h * head_dim, (h + 1) * head_dim)
+
+    def project(w, out):
+        for c in range(0, cols, 256):
+            out[:, c : c + 256] = dot(normed_v[...], w[:, c : c + 256]).astype(out.dtype)
+
+    loads[0].wait()
+    loads[1].wait()
+    project(wq_v, q_unit)
+    loads[2].wait()
+    project(wk_v, k_unit)
+    squares = [jnp.sum(u[...] * u[...], axis=1, keepdims=True) for u in (q_unit, k_unit)]
+    row_send[...] = row_table(*squares)
+
+    def row_copy(d):
+        return remote(row_send, row_land.at[d], row_sems.at[0, d], row_sems.at[1, d], others[d - 1])
+
+    for d in range(1, seq.size):
+        row_copy(d).start()
+    loads[3].wait()
+    project(wv_v, v_low)
+    total = row_send[...]
+    for d in range(1, seq.size):
+        row_copy(d).wait_recv()
+        total = total + row_land[d]
+    for d in range(1, seq.size):
+        row_copy(d).wait_send()
+    inv = from_row_table(lax.rsqrt(total / width + norm_eps))
+    scales[...] = inv
+    cos_rows, sin_rows = cosine[...], -sine[...]
+    for i, (unit, gains, out) in enumerate(((q_unit, gain_q, q_low), (k_unit, gain_k, k_low))):
+        for h in range(heads):
+            value = unit[:, head(h)] * inv[:, i : i + 1]
+            unit[:, head(h)] = value
+            out[:, head(h)] = turn(value * gains[:, head(h)], cos_rows, sin_rows).astype(BF)
+
+    def probs_copy(h):
+        return pltpu.make_async_copy(probs.at[h], probs_out.at[h], probs_sems.at[h])
+
+    for h in range(heads):
+        for b in range(0, length, Q_BLOCK):
+            rows = slice(b, b + Q_BLOCK)
+            scores = dot(q_low[rows, head(h)], k_low[:, head(h)], 1, 1) * scale + bias[rows]
+            weights = jnp.exp(scores - jnp.max(scores, axis=-1, keepdims=True))
+            prob = weights / jnp.sum(weights, axis=-1, keepdims=True)
+            probs[h, rows] = prob
+            attended[rows, head(h)] = dot(prob.astype(BF), v_low[:, head(h)]).astype(BF)
+        probs_copy(h).start()
+
+    scatter = PlaceScatter(seq, parts, HIDDEN_CHUNKS, land, ringbuf, part_sems)
+    loads[4].wait()
+
+    def out_rows(s):
+        at = pl.ds(pl.multiple_of(s * toks, toks), toks)
+        parts[s] = dot(attended[at], rows_v[...]).astype(BF)
+
+    for t in scatter.order:
+        out_rows(seq.at(t) * 2 + 1 - seq.inner)
+        scatter.start_place(t)
+        out_rows(seq.at(t) * 2 + seq.inner)
     for t in scatter.order[:-1]:
         for c in range(HIDDEN_CHUNKS):
             scatter.step(t, c)
@@ -437,8 +577,8 @@
         cut = scatter.cut(c)
         hidden = tokens[cut].astype(F32) + scatter.step(0, c)
         hidden_out[cut] = hidden
-        scale = lax.rsqrt(jnp.mean(hidden * hidden, axis=-1, keepdims=True) + norm_eps)
-        low[cut] = (hidden * scale * gain[...]).astype(BF)
+        inv = lax.rsqrt(jnp.mean(hidden * hidden, axis=-1, keepdims=True) + norm_eps)
+        low[cut] = (hidden * inv * gain[...]).astype(BF)
         own.append(pltpu.make_async_copy(low.at[cut], all_out.at[group.me, cut], low_sems.at[c]))
         own[c].start()
         gathers.append(
@@ -452,21 +592,33 @@
         gathers[c].finish()
         own[c].wait()
     scatter.finish()
-
-
-def hidden_and_rows(parts, tokens, gain):
-    group_count = lax.axis_size("expert")
-    rows, width = tokens.shape
+    for h in range(heads):
+        probs_copy(h).wait()
+
+
+def attend(normed, wq, wk, wv, w_rows, bias, cosine, sine, gain_q, gain_k, tokens, gain):
+    seq_count, group_count = lax.axis_size("seq"), lax.axis_size("expert")
+    toks, width = tokens.shape
+    length, cols = normed.shape[0], wq.shape[1]
+    heads = cols // cosine.shape[1]
     dma = pltpu.SemaphoreType.DMA
+    low = lambda *shape: pltpu.VMEM(shape, BF)
+    full = lambda *shape: pltpu.VMEM(shape, F32)
+    out = jax.ShapeDtypeStruct
+    flat = [out((length, cols), BF)] * 4
     return call(
-        hidden_kernel, 2, 60,
-        (jax.ShapeDtypeStruct((rows, width), F32),
-         jax.ShapeDtypeStruct((group_count, rows, width), BF)),
-        scatter_scratch("seq", rows, width, HIDDEN_CHUNKS)
-        + [pltpu.VMEM((rows, width), BF), dma((HIDDEN_CHUNKS,)),
-           dma((HIDDEN_CHUNKS, group_count // 2, 2)), dma((HIDDEN_CHUNKS, group_count // 2, 2))],
-        parts, tokens, gain[None],
-        specs=[ANY, IN_VMEM, IN_VMEM], out_specs=(IN_VMEM, ANY),
+        attend_kernel, 2, 80,
+        (out((toks, width), F32), out((group_count, toks, width), BF), *flat,
+         out((heads, length, length), F32), out((length, cols), F32), out((length, cols), F32),
+         out((length, 128), F32)),
+        place_scratch("seq", seq_count, toks, width, HIDDEN_CHUNKS)
+        + [low(toks, width), low(length, width), low(width, cols), low(width, cols), low(width, cols),
+           low(cols, width), full(heads, length, length), full(8, length), full(seq_count, 8, length),
+           dma((5,)), dma((HIDDEN_CHUNKS,)), dma((HIDDEN_CHUNKS, group_count // 2, 2)),
+           dma((HIDDEN_CHUNKS, group_count // 2, 2)), dma((2, seq_count)), dma((heads,))],
+        normed, wq, wk, wv, w_rows, bias, cosine, sine, gain_q, gain_k, tokens, gain,
+        specs=[ANY] * 5 + [IN_VMEM] * 7,
+        out_specs=(IN_VMEM, ANY) + (IN_VMEM,) * 4 + (ANY,) + (IN_VMEM,) * 3,
     )
 
 
@@ -491,38 +643,6 @@
     return call(
         rows_kernel, 3, 50, jax.ShapeDtypeStruct((rows, width), F32),
         scatter_scratch("expert", rows, width, ROW_CHUNKS), parts, out_specs=IN_VMEM,
-    )
-
-
-def pack_kernel(rows_in, out, own_sems, g_send, g_recv):
-    seq = Ring("seq")
-    greet(seq.partners())
-    chunks = g_send.shape[0]
-    rows = rows_in.shape[0] // chunks
-    gathers = []
-    for c in range(chunks):
-        cut = pl.ds(c * rows, rows)
-        pltpu.make_async_copy(rows_in.at[cut], out.at[seq.me, cut], own_sems.at[c]).start()
-        gathers.append(
-            Gather(seq, lambda s, cut=cut: out.at[s, cut], g_send.at[c], g_recv.at[c])
-        )
-        gathers[c].start(rows_in.at[cut])
-    for back in range(1, seq.outer_count):
-        for gather in gathers:
-            gather.relay(back)
-    for c in range(chunks):
-        gathers[c].finish()
-        cut = pl.ds(c * rows, rows)
-        pltpu.make_async_copy(rows_in.at[cut], out.at[seq.me, cut], own_sems.at[c]).wait()
-
-
-def gather_pack(rows_in, chunks=2):
-    seq_count = lax.axis_size("seq")
-    dma = pltpu.SemaphoreType.DMA
-    return call(
-        pack_kernel, 4, 18, jax.ShapeDtypeStruct((seq_count,) + rows_in.shape, BF),
-        [dma((chunks,)), dma((chunks, seq_count // 2, 2)), dma((chunks, seq_count // 2, 2))],
-        rows_in,
     )
 
 
@@ -764,61 +884,328 @@
     )
 
 
-LAST_CHUNKS = 2
+NORMED_CHUNKS = 2
+CROSS_CHUNKS = 8
+
+
+class Cross:
+    def __init__(self, seq, parts, land, mine, crossed, bufs, stage, sems):
+        self.seq, self.parts, self.land, self.mine, self.crossed = seq, parts, land, mine, crossed
+        self.bufs, self.stage, self.sems = bufs, stage, sems
+        self.rows = parts.shape[1] // CROSS_CHUNKS
+
+    def swap(self, t):
+        src = self.parts.at[self.seq.at(t) * 2 + 1 - self.seq.inner]
+        return remote(src, self.land.at[t], self.sems.at[0, t], self.sems.at[1, t], self.seq.pair)
+
+    def start(self):
+        self.swap(1).start()
+        self.swap(0).start()
+
+    def loads(self, i):
+        t, c = 1 - i // CROSS_CHUNKS, i % CROSS_CHUNKS
+        cut = pl.ds(c * self.rows, self.rows)
+        own = self.parts.at[self.seq.at(t) * 2 + self.seq.inner, cut]
+        return [
+            pltpu.make_async_copy(own, self.bufs.at[i % 2, 0], self.sems.at[2, i % 2]),
+            pltpu.make_async_copy(self.land.at[t, cut], self.bufs.at[i % 2, 1], self.sems.at[3, i % 2]),
+        ]
+
+    def load(self, i):
+        if i >= 2 * CROSS_CHUNKS:
+            return
+        if i % CROSS_CHUNKS == 0:
+            self.swap(1 - i // CROSS_CHUNKS).wait_recv()
+        for copy in self.loads(i):
+            copy.start()
+
+    def send(self, i):
+        cut = pl.ds((i % CROSS_CHUNKS) * self.rows, self.rows)
+        if i < CROSS_CHUNKS:
+            return remote(self.stage.at[i % 2], self.crossed.at[cut], self.sems.at[4, i % 2],
+                          self.sems.at[5, i % CROSS_CHUNKS], self.seq.next)
+        return pltpu.make_async_copy(self.stage.at[i % 2], self.mine.at[cut], self.sems.at[4, i % 2])
+
+    def wait_sent(self, i):
+        if i < CROSS_CHUNKS:
+            self.send(i).wait_send()
+        else:
+            self.send(i).wait()
+
+    def tick(self, i):
+        if i == 0:
+            self.load(0)
+        for copy in self.loads(i):
+            copy.wait()
+        self.load(i + 1)
+        if i >= 2:
+            self.wait_sent(i - 2)
+        total = self.bufs[i % 2, 0].astype(F32) + self.bufs[i % 2, 1].astype(F32)
+        self.stage[i % 2] = total.astype(BF)
+        self.send(i).start()
+
+    def finish(self):
+        last = 2 * CROSS_CHUNKS
+        self.wait_sent(last - 2)
+        self.wait_sent(last - 1)
+        for c in range(CROSS_CHUNKS):
+            self.send(c).wait_recv()
+        self.swap(0).wait_send()
+        self.swap(1).wait_send()
+
+
+def cross_scratch(parts):
+    rows, columns = parts.shape[1] // CROSS_CHUNKS, parts.shape[2]
+    return [pltpu.VMEM((2, 2, rows, columns), BF), pltpu.VMEM((2, rows, columns), BF),
+            pltpu.SemaphoreType.DMA((6, CROSS_CHUNKS))]
+
+
+def place_scratch(axis, size, rows, columns, chunks):
+    outer_count = lax.axis_size(axis) // 2
+    return [pltpu.VMEM((size, rows, columns), BF), pltpu.VMEM((outer_count, rows, columns), BF),
+            pltpu.VMEM((max(outer_count - 1, 1), rows, columns), BF),
+            pltpu.SemaphoreType.DMA((4, outer_count, chunks))]
+
+
+Q_BLOCK = 256
+LATE = ("w_rows", "normed", "probs", "q_unit", "k_unit", "wq", "wk", "wv")
+LATE_AT = (4, 17, 9, 10, 11, 18, 19, 20)
 
 
 def last_kernel(
-    normed_parts, three_parts, out_parts, tokens, gain, grad_hidden, small, *refs, extra
+    grad_low, grad_hidden, tokens, gain, w_rows, q_low, k_low, v_low, attended, probs,
+    q_unit, k_unit, scales, gain_q, gain_k, cosine, sine, normed, wq, wk, wv, small, *refs,
+    crossings,
 ):
-    expert_parts, refs = refs[:extra], refs[extra:]
-    d_tokens, d_three, d_out, small_out = refs[:4]
-    expert_sums, scratch = refs[4 : 4 + extra], refs[4 + extra :]
-    expert_scratch, scratch = scratch[: extra * SCATTER_REFS], scratch[extra * SCATTER_REFS :]
+    expert_parts, refs = refs[:crossings], refs[crossings:]
+    late = {}
+    refs, copies, load_sems = refs[: -len(LATE) - 1], refs[-len(LATE) - 1 : -1], refs[-1]
+    arrays = dict(w_rows=w_rows, probs=probs, q_unit=q_unit, k_unit=k_unit, normed=normed,
+                  wq=wq, wk=wk, wv=wv)
+    for i, name in enumerate(LATE):
+        late[name] = pltpu.make_async_copy(arrays[name], copies[i], load_sems.at[i])
+    w_rows, normed, probs, q_unit, k_unit, wq, wk, wv = copies
+    d_tokens, d_q, d_k, d_v, d_out, small_out = refs[:6]
+    refs = refs[6:]
+    cross_out, refs = refs[: 3 * crossings], refs[3 * crossings :]
+    cross_bufs, refs = refs[: 3 * crossings], refs[3 * crossings :]
+    place = [refs[4 * i : 4 * i + 4] for i in range(5)]
+    (grad_all, normed_t, grad_att, grad_g, grad_three, dk_sum, row_send, row_land,
+     low_send, low_land, sum_buf, sum_land,
+     own_sem, pack_send, pack_recv, row_sems, swap_sems, sum_sems) = refs[20:]
     seq, group = Ring("seq"), Ring("expert")
     others = [{"seq": seq.me ^ d} for d in range(1, seq.size)]
-    steps = [{"expert": group.me ^ (1 << i)} for i in range((group.size - 1).bit_length())]
-    steps += [{"seq": seq.me ^ (1 << i)} for i in range((seq.size - 1).bit_length())]
     known = [{"expert": group.me ^ (1 << i)} for i in range((group.size - 1).bit_length())]
+    steps = known + [{"seq": seq.me ^ (1 << i)} for i in range((seq.size - 1).bit_length())]
+    for name in LATE:
+        late[name].start()
     greet(others + known + [group.next, group.last])
-    n = SCATTER_REFS
-    normed = Scatter(seq, normed_parts, LAST_CHUNKS, *scratch[:n])
-    outs = Scatter(group, out_parts, 1, *scratch[n : 2 * n])
-    three = Scatter(group, three_parts, LAST_CHUNKS, *scratch[2 * n : 3 * n])
-    three_low, sum_buf, sum_land, own_sem, swap_sems, sum_sems = scratch[3 * n :]
-    experts = [
-        Scatter(seq, ref, 1, *expert_scratch[i * n : (i + 1) * n])
-        for i, ref in enumerate(expert_parts)
+    length, cols = q_low.shape
+    width = tokens.shape[1]
+    toks = tokens.shape[0]
+    head_dim = cosine.shape[1]
+    heads = cols // head_dim
+    wrows = d_out.shape[0]
+    scale = head_dim**-0.5
+
+    crosses = [
+        Cross(seq, expert_parts[i], *cross_out[3 * i : 3 * i + 3], *cross_bufs[3 * i : 3 * i + 3])
+        for i in range(crossings)
     ]
-    normed.start()
-    for t in three.order:
-        three.start_place(t)
-        outs.start_place(t)
-    for scatter in experts:
-        scatter.start()
-    for t in normed.order[:-1]:
-        for c in range(LAST_CHUNKS):
-            normed.step(t, c)
-    for scatter in experts:
-        scatter.step(scatter.order[0], 0)
-    gain_sum = jnp.zeros((1, tokens.shape[1]), F32)
-    for c in range(LAST_CHUNKS):
-        cut = normed.cut(c)
-        grad = normed.step(0, c)
+    ticks = [(cross, i) for i in range(2 * CROSS_CHUNKS) for cross in crosses]
+    ticks = [t for t in ticks if t[1] < CROSS_CHUNKS] + [t for t in ticks if t[1] >= CROSS_CHUNKS]
+
+    def tick(count=1):
+        for _ in range(count):
+            if ticks:
+                cross, i = ticks.pop(0)
+                cross.tick(i)
+
+    own = pltpu.make_async_copy(grad_low, grad_all.at[seq.me], own_sem.at[0])
+    own.start()
+    pack = Gather(seq, lambda s: grad_all.at[s], pack_send, pack_recv)
+    pack.start(grad_low)
+    for cross in crosses:
+        cross.start()
+    size = width // seq.size
+    late["normed"].wait()
+    for s in range(seq.size):
+        normed_t[pl.ds(s * size, size)] = normed[:, s * size : (s + 1) * size].T
+    for back in range(1, seq.outer_count):
+        pack.relay(back)
+    tick()
+    own.wait()
+    pack.finish()
+
+    late["w_rows"].wait()
+    for c in range(0, cols, Q_BLOCK):
+        at = slice(c, c + Q_BLOCK)
+        grad_att[:, at] = dot(
+            grad_all[...].reshape(length, width), w_rows[at, :], 1, 1
+        ).astype(BF)
+
+    query_sums, key_sums, value_sums = [
+        PlaceScatter(group, p[0], 1, p[1], p[2], p[3]) for p in place[:3]
+    ]
+    out_sums = RingFirst(group, *place[3])
+    normed_sums = PlaceScatter(seq, place[4][0], NORMED_CHUNKS, *place[4][1:])
+
+    def head(h):
+        return slice(h * head_dim, (h + 1) * head_dim)
+
+    late["probs"].wait()
+    for h in range(heads):
+        grad_three[2, :, head(h)] = dot(
+            probs[h].astype(BF), grad_att[:, head(h)], 0, 0
+        ).astype(BF)
+
+    def weight_grad(i, sums):
+        for s in range(seq.size):
+            value = dot(normed_t[pl.ds(s * size, size)], grad_three[i])
+            sums.x_ref[:, pl.ds(s * wrows, wrows)] = value.astype(BF).reshape(
+                group.size, wrows, cols
+            )
+        sums.start()
+
+    weight_grad(2, value_sums)
+    tick()
+    for c in range(0, width, 512):
+        at = slice(c, c + 512)
+        value = dot(attended[...], grad_all[:, :, at].reshape(length, 512), 0, 0)
+        out_sums.parts[:, :, at] = value.astype(BF).reshape(group.size, wrows, 512)
+    out_sums.start()
+    tick()
+    out_order, value_order = list(out_sums.order[1:]), list(value_sums.order)
+
+    def out_step():
+        if len(out_order) > 1:
+            out_sums.step(out_order.pop(0))
+
+    def value_step():
+        if len(value_order) > 1:
+            value_sums.step(value_order.pop(0), 0)
+
+    row_sums = [jnp.zeros((length, 1), F32), jnp.zeros((length, 1), F32)]
+    gain_row = 0
+    cos_rows, sin_rows = cosine[...], sine[...]
+
+    def through_rope(i, h, grad, unit, gains):
+        turned = turn(grad, cos_rows, sin_rows)
+        sum_buf[0, pl.ds(gain_rows[i], 1), pl.ds(pl.multiple_of(seq.me * cols, 128) + h * head_dim, head_dim)] = (
+            jnp.sum(turned * unit, axis=0, keepdims=True)
+        )
+        gained = turned * gains
+        grad_g[i, :, head(h)] = gained
+        row_sums[i] = row_sums[i] + jnp.sum(gained * unit, axis=1, keepdims=True)
+
+    late["q_unit"].wait()
+    late["k_unit"].wait()
+    sum_buf[0] = small[...]
+    gain_rows = (small.shape[0] - 3, small.shape[0] - 2)
+    for h in range(heads):
+        queries = []
+        for b in range(0, length, Q_BLOCK):
+            rows = slice(b, b + Q_BLOCK)
+            prob = probs[h, rows]
+            grad = dot(grad_att[rows, head(h)], v_low[:, head(h)], 1, 1)
+            row_dot = jnp.sum(prob * grad, axis=-1, keepdims=True)
+            grad_scores = (prob * (grad - row_dot)).astype(BF)
+            queries.append(dot(grad_scores, k_low[:, head(h)]) * scale)
+            keys = dot(grad_scores, q_low[rows, head(h)], 0, 0)
+            dk_sum[...] = keys if b == 0 else dk_sum[...] + keys
+        through_rope(0, h, jnp.concatenate(queries, axis=0), q_unit[:, head(h)], gain_q[:, head(h)])
+        through_rope(1, h, dk_sum[...] * scale, k_unit[:, head(h)], gain_k[:, head(h)])
+        if h == 1:
+            value_step()
+
+    lanes = lax.broadcasted_iota(jnp.int32, (length, 128), 1)
+    table = jnp.where(lanes == 0, row_sums[0], jnp.where(lanes == 1, row_sums[1], 0.0))
+    row_send[...] = table.T[:8]
+
+    def row_copy(d):
+        return remote(row_send, row_land.at[d], row_sems.at[0, d], row_sems.at[1, d], others[d - 1])
+
+    for d in range(1, seq.size):
+        row_copy(d).start()
+    out_step()
+    total = row_send[...]
+    for d in range(1, seq.size):
+        row_copy(d).wait_recv()
+        total = total + row_land[d]
+    for d in range(1, seq.size):
+        row_copy(d).wait_send()
+    tick(2)
+    means = jnp.concatenate([total / width, jnp.zeros((120, length), F32)], axis=0).T
+    for i, (unit, sums) in enumerate(((q_unit, query_sums), (k_unit, key_sums))):
+        for h in range(heads):
+            value = grad_g[i, :, head(h)] - unit[:, head(h)] * means[:, i : i + 1]
+            grad_three[i, :, head(h)] = (value * scales[:, i : i + 1]).astype(BF)
+        weight_grad(i, sums)
+        value_step()
+    for name in ("wq", "wk", "wv"):
+        late[name].wait()
+    for c in range(0, width, 512):
+        at = slice(c, c + 512)
+        value = dot(grad_three[0], wq[at, :], 1, 1) + dot(grad_three[1], wk[at, :], 1, 1)
+        value = value + dot(grad_three[2], wv[at, :], 1, 1)
+        normed_sums.x_ref[:, :, at] = value.astype(BF).reshape(seq.size, toks, 512)
+    normed_sums.start()
+    out_step()
+    tick()
+
+    swaps = {}
+
+    def swap_copy(i, d):
+        src = low_send.at[i, pl.ds((seq.me ^ d) * wrows, wrows)]
+        return remote(src, low_land.at[i, seq.me], swap_sems.at[0, i, d], swap_sems.at[1, i, d], others[d - 1])
+
+    def send_columns(i, sums):
+        low_send[i] = sums.step(0, 0).astype(BF)
+        for d in range(1, seq.size):
+            swap_copy(i, d).start()
+
+    while len(value_order) > 1:
+        value_step()
+    for t in normed_sums.order[:-1]:
+        for c in range(NORMED_CHUNKS):
+            normed_sums.step(t, c)
+    first, *middle = group_order(group)[:-1]
+    query_sums.step(first, 0)
+    tick()
+    key_sums.step(first, 0)
+    tick()
+    while len(out_order) > 1:
+        out_step()
+    gain_sum = jnp.zeros((1, width), F32)
+    for c in range(NORMED_CHUNKS):
+        cut = normed_sums.cut(c)
+        grad = normed_sums.step(0, c)
         value = tokens[cut].astype(F32)
-        scale = lax.rsqrt(jnp.mean(value * value, axis=-1, keepdims=True) + norm_eps)
-        unit = value * scale
+        inv = lax.rsqrt(jnp.mean(value * value, axis=-1, keepdims=True) + norm_eps)
+        unit = value * inv
         gained = grad * gain[...]
         mean = jnp.mean(gained * unit, axis=-1, keepdims=True)
-        d_tokens[cut] = grad_hidden[cut] + scale * (gained - unit * mean)
+        d_tokens[cut] = grad_hidden[cut] + inv * (gained - unit * mean)
         gain_sum = gain_sum + jnp.sum(grad * unit, axis=0, keepdims=True)
-    sum_buf[0] = small[...]
-    last_row = small.shape[0] - 1
-    sum_buf[0, pl.ds(last_row, 1)] = gain_sum
+    sum_buf[0, pl.ds(small.shape[0] - 1, 1)] = gain_sum
+    tick()
+    send_columns(2, value_sums)
+    out_sums.step(0)
+    for t in middle:
+        query_sums.step(t, 0)
+        tick(2)
+        key_sums.step(t, 0)
+        tick(2)
+    d_out[...] = out_sums.last()
+    tick()
+    send_columns(0, query_sums)
+    send_columns(1, key_sums)
 
     def sum_copy(i):
         return remote(sum_buf.at[i], sum_land.at[i], sum_sems.at[0, i], sum_sems.at[1, i], steps[i])
 
-    def sum_step(i):
+    sum_copy(0).start()
+    for i in range(len(steps)):
         sum_copy(i).wait_recv()
         total = sum_buf[i] + sum_land[i]
         if i + 1 < len(steps):
@@ -826,67 +1213,69 @@
             sum_copy(i + 1).start()
         else:
             small_out[...] = total
-
-    for t in three.order[:-1]:
-        for c in range(LAST_CHUNKS):
-            three.step(t, c)
-        outs.step(t, 0)
-    for c in range(LAST_CHUNKS):
-        three_low[three.cut(c)] = three.step(0, c).astype(BF)
-    wrows = three_low.shape[0] // seq.size
-
-    def swap_copy(d):
-        src = three_low.at[pl.ds((seq.me ^ d) * wrows, wrows)]
-        return remote(src, d_three.at[seq.me], swap_sems.at[0, d], swap_sems.at[1, d], others[d - 1])
-
-    for d in range(1, seq.size):
-        swap_copy(d).start()
-    own = pltpu.make_async_copy(
-        three_low.at[pl.ds(seq.me * wrows, wrows)], d_three.at[seq.me], own_sem.at[0]
-    )
-    own.start()
-    d_out[...] = outs.step(0, 0)
-    sum_copy(0).start()
-    for i in range(len(steps)):
-        sum_step(i)
-    for scatter, out in zip(experts, expert_sums):
-        for t in scatter.order[1:-1]:
-            scatter.step(t, 0)
-        out[...] = scatter.step(0, 0)
-    for d in range(1, seq.size):
-        there = d_three.at[seq.me ^ d]
-        remote(there, there, swap_sems.at[0, d], swap_sems.at[1, d], others[d - 1]).wait_recv()
-        swap_copy(d).wait_send()
-    own.wait()
+        tick()
+    tick(len(ticks))
+    for i, out in ((2, d_v), (0, d_q), (1, d_k)):
+        for d in range(1, seq.size):
+            there = low_land.at[i, seq.me ^ d]
+            remote(there, there, swap_sems.at[0, i, d], swap_sems.at[1, i, d], others[d - 1]).wait_recv()
+            swap_copy(i, d).wait_send()
+        low_land[i, seq.me] = low_send[i, pl.ds(pl.multiple_of(seq.me * wrows, wrows), wrows)]
+        for s in range(seq.size):
+            out[:, s * cols : (s + 1) * cols] = low_land[i, s].astype(F32)
     for i in range(len(steps)):
         sum_copy(i).wait_send()
-    for scatter in (normed, three, outs, *experts):
-        scatter.finish()
-
-
-def finish_all(normed_parts, three_parts, out_parts, tokens, gain, grad_hidden, small, *expert_parts):
+    for cross in crosses:
+        cross.finish()
+    for sums in (query_sums, key_sums, value_sums, out_sums, normed_sums):
+        sums.finish()
+
+
+def group_order(ring):
+    return list(range(1, ring.outer_count)) + [0]
+
+
+def finish_all(ins, expert_parts):
     seq_count, group_count = lax.axis_size("seq"), lax.axis_size("expert")
+    (grad_low, grad_hidden, tokens, gain, w_rows, q_low, *_) = ins
+    small = ins[-1]
     rows, width = tokens.shape
-    rows3, cols3 = three_parts.shape[1:]
-    wrows = rows3 // seq_count
+    length, cols = q_low.shape
+    head_dim = width // HEADS
+    wrows = cols // group_count
+    side = seq_count * wrows
     count = (seq_count - 1).bit_length() + (group_count - 1).bit_length()
     dma = pltpu.SemaphoreType.DMA
+    low = lambda *shape: pltpu.VMEM(shape, BF)
+    full = lambda *shape: pltpu.VMEM(shape, F32)
+    shape = lambda *dims: jax.ShapeDtypeStruct(dims, F32)
+    outs = [shape(rows, width)] + [shape(wrows, width)] * 4 + [shape(*small.shape)]
+    cross_outs, scratch = [], []
+    for parts in expert_parts:
+        size = parts.shape[1:]
+        cross_outs += [jax.ShapeDtypeStruct((2,) + size, BF), jax.ShapeDtypeStruct(size, BF),
+                       jax.ShapeDtypeStruct(size, BF)]
+        scratch += cross_scratch(parts)
+    for _ in range(3):
+        scratch += place_scratch("expert", group_count, side, cols, 1)
+    scratch += ring_first_scratch("expert", wrows, width)
+    scratch += place_scratch("seq", seq_count, rows, width, NORMED_CHUNKS)
+    scratch += [
+        low(seq_count, rows, width), low(width, length), low(length, cols),
+        full(2, length, cols), low(3, length, cols), full(length, head_dim),
+        full(8, length), full(seq_count, 8, length),
+        low(3, side, cols), low(3, seq_count, wrows, cols),
+        full(count, *small.shape), full(count, *small.shape),
+        dma((1,)), dma((seq_count // 2, 2)), dma((seq_count // 2, 2)), dma((2, seq_count)),
+        dma((2, 3, seq_count)), dma((2, count)),
+    ]
+    scratch += [pltpu.VMEM(ins[i].shape, ins[i].dtype) for i in LATE_AT] + [dma((len(LATE),))]
     return call(
-        partial(last_kernel, extra=len(expert_parts)), 5, 110,
-        (jax.ShapeDtypeStruct((rows, width), F32),
-         jax.ShapeDtypeStruct((seq_count, wrows, cols3), BF),
-         jax.ShapeDtypeStruct(out_parts.shape[1:], F32),
-         jax.ShapeDtypeStruct(small.shape, F32))
-        + tuple(jax.ShapeDtypeStruct(e.shape[1:], F32) for e in expert_parts),
-        sum([scatter_scratch("seq", e.shape[1], e.shape[2], 1) for e in expert_parts], [])
-        + scatter_scratch("seq", rows, width, LAST_CHUNKS)
-        + scatter_scratch("expert", out_parts.shape[1], width, 1)
-        + scatter_scratch("expert", rows3, cols3, LAST_CHUNKS)
-        + [pltpu.VMEM((rows3, cols3), BF), pltpu.VMEM((count,) + small.shape, F32),
-           pltpu.VMEM((count,) + small.shape, F32), dma((1,)), dma((2, seq_count)), dma((2, count))],
-        normed_parts, three_parts, out_parts, tokens, gain[None], grad_hidden, small, *expert_parts,
-        specs=[ANY, ANY, ANY, IN_VMEM, IN_VMEM, IN_VMEM, IN_VMEM] + [ANY] * len(expert_parts),
-        out_specs=(IN_VMEM, ANY, IN_VMEM, IN_VMEM) + (IN_VMEM,) * len(expert_parts),
+        partial(last_kernel, crossings=len(expert_parts)), 5, 150,
+        tuple(outs + cross_outs), scratch, *ins, *expert_parts,
+        specs=[ANY if i in (0, *LATE_AT) else IN_VMEM for i in range(len(ins))]
+        + [ANY] * len(expert_parts),
+        out_specs=tuple([IN_VMEM] * len(outs) + [ANY] * len(cross_outs)),
     )
 
 
@@ -994,14 +1383,10 @@
     half = head_dim // 2
     inverse = 10000.0 ** (-jnp.arange(half, dtype=F32) / half)
     angles = offsets.astype(F32)[:, None] * inverse[None, :]
-    cosine = jnp.cos(angles)[:, None, :]
-    sine = jnp.sin(angles)[:, None, :]
-
-    def turn(values, sine_table):
-        first, second = values[..., :half], values[..., half:]
-        return jnp.concatenate(
-            [first * cosine - second * sine_table, second * cosine + first * sine_table], axis=-1
-        )
+    cosine, sine = jnp.cos(angles), jnp.sin(angles)
+    cosine = jnp.concatenate([cosine, cosine], axis=1)
+    sine = jnp.concatenate([sine, -sine], axis=1)
+    bias = jnp.where(allowed, 0.0, masked_score).astype(F32)
 
     expert_ids = jnp.arange(128, dtype=jnp.int32)
     hits = jnp.any(routes[0][:, :, None] == expert_ids[None, None, :], axis=1).astype(BF)
@@ -1013,31 +1398,11 @@
     )
     normed_all = normed_all.reshape(length, width)
     w_cols = [w.reshape(width, cols) for w in (wq_cols, wk_cols, wv_cols)]
-    query_raw = product(normed_all, w_cols[0])
-    key_raw = product(normed_all, w_cols[1])
-    value_low = product(normed_all, w_cols[2]).astype(BF).reshape(length, heads, head_dim)
-
-    def row_sums(left, right):
-        sums = jnp.stack([jnp.sum(left, axis=1), jnp.sum(right, axis=1)])
-        return lax.psum(sums, "seq") / width
-
-    inv_rms = lax.rsqrt(row_sums(query_raw**2, key_raw**2) + norm_eps)
     gain_q = lax.dynamic_slice_in_dim(gain_query, seq_me * cols, cols)
     gain_k = lax.dynamic_slice_in_dim(gain_key, seq_me * cols, cols)
-    query_unit = query_raw * inv_rms[0][:, None]
-    key_unit = key_raw * inv_rms[1][:, None]
-    query_low = turn((query_unit * gain_q).reshape(length, heads, head_dim), sine).astype(BF)
-    key_low = turn((key_unit * gain_k).reshape(length, heads, head_dim), sine).astype(BF)
-    scores = jnp.einsum("qhd,khd->hqk", query_low, key_low, preferred_element_type=F32)
-    scores = jnp.where(allowed[None], scores * score_scale, masked_score)
-    top_score = jnp.max(scores, axis=-1, keepdims=True)
-    weights = jnp.exp(scores - top_score)
-    probs = weights / jnp.sum(weights, axis=-1, keepdims=True)
-    probs_low = probs.astype(BF)
-    attended = jnp.einsum("hqk,khd->qhd", probs_low, value_low, preferred_element_type=F32)
-    attended_low = attended.reshape(length, cols).astype(BF)
-    hidden_parts = product(attended_low, w_rows).astype(BF).reshape(seq_count, tok_rows, width)
-    hidden, normed2_all = hidden_and_rows(hidden_parts, tokens[0], gain_mlp)
+    (hidden, normed2_all, query_low, key_low, value_low, attended_low, probs, query_unit, key_unit,
+     scales) = attend(normed_all, *w_cols, w_rows, bias, cosine, sine, gain_q[None], gain_k[None],
+                      tokens[0], gain_mlp[None])
     normed2, mlp_norm_back = jax.vjp(rms_norm, hidden, gain_mlp)
     normed2_low = normed2.astype(BF)
 
@@ -1092,72 +1457,30 @@
     grad_hidden_part, grad_gain_mlp = mlp_norm_back(grad_normed2)
     grad_hidden = cotangent[0].astype(F32) + grad_hidden_part
 
-    grad_hidden_all = gather_pack(grad_hidden.astype(BF)).reshape(length, width)
-    grad_attended = jnp.einsum(
-        "te,de->td", grad_hidden_all, w_rows, preferred_element_type=F32
-    ).astype(BF)
-    grad_attended = grad_attended.reshape(length, heads, head_dim)
-    grad_w_out = jnp.einsum(
-        "td,te->de", attended_low, grad_hidden_all, preferred_element_type=F32
-    ).astype(BF).reshape(group_count, wrows, width)
-    grad_probs_attn = jnp.einsum(
-        "qhd,khd->hqk", grad_attended, value_low, preferred_element_type=F32
-    )
-    row_dot = jnp.sum(probs * grad_probs_attn, axis=-1, keepdims=True)
-    grad_scores = (probs * (grad_probs_attn - row_dot)).astype(BF)
-    grad_query = jnp.einsum("hqk,khd->qhd", grad_scores, key_low, preferred_element_type=F32)
-    grad_key = jnp.einsum("hqk,qhd->khd", grad_scores, query_low, preferred_element_type=F32)
-    grad_value = jnp.einsum("hqk,qhd->khd", probs_low, grad_attended, preferred_element_type=F32)
-    grad_query = turn(grad_query * score_scale, -sine).reshape(length, cols)
-    grad_key = turn(grad_key * score_scale, -sine).reshape(length, cols)
-    grad_gain_query = jnp.sum(grad_query * query_unit, axis=0)
-    grad_gain_key = jnp.sum(grad_key * key_unit, axis=0)
-    grad_query_g, grad_key_g = grad_query * gain_q, grad_key * gain_k
-    means = row_sums(grad_query_g * query_unit, grad_key_g * key_unit)
-    grad_query_low = (
-        inv_rms[0][:, None] * (grad_query_g - query_unit * means[0][:, None])
-    ).astype(BF)
-    grad_key_low = (inv_rms[1][:, None] * (grad_key_g - key_unit * means[1][:, None])).astype(BF)
-    grad_value_low = grad_value.reshape(length, cols).astype(BF)
-    grad_three = jnp.concatenate([grad_query_low, grad_key_low, grad_value_low], axis=1)
-    grad_normed_parts = each(grad_query_low, w_cols[0], "te,de->td")
-    grad_normed_parts += each(grad_key_low, w_cols[1], "te,de->td")
-    grad_normed_parts += each(grad_value_low, w_cols[2], "te,de->td")
-    grad_normed_parts = grad_normed_parts.astype(BF).reshape(seq_count, tok_rows, width)
-    grad_w_three = jnp.einsum(
-        "td,te->de", normed_all, grad_three, preferred_element_type=F32
-    ).astype(BF).reshape(seq_count, group_count, wrows, 3 * cols)
-    grad_w_three = grad_w_three.transpose(1, 0, 2, 3).reshape(
-        group_count, seq_count * wrows, 3 * cols
-    )
-
-    def full(value):
-        return lax.dynamic_update_slice(jnp.zeros((width,), F32), value, (seq_me * cols,))
-
-    rows = [grad_router, grad_gain_mlp[None], full(grad_gain_query)[None], full(grad_gain_key)[None]]
-    small = jnp.concatenate(rows)
-    spare = -(total_experts + 4) % 8 + 1
-    small = jnp.concatenate([small, jnp.zeros((spare, width), F32)])
-    d_tokens, d_three, d_w_out, small, *expert_sums = finish_all(
-        grad_normed_parts, grad_w_three, grad_w_out, tokens[0], gain_attn, grad_hidden, small,
-        *expert_parts,
+    spare = -(total_experts + 4) % 8 + 3
+    small = jnp.concatenate([grad_router, grad_gain_mlp[None], jnp.zeros((spare, width), F32)])
+    d_tokens, d_w_query, d_w_key, d_w_value, d_w_out, small, *crossed = finish_all(
+        (grad_hidden.astype(BF), grad_hidden, tokens[0], gain_attn[None], w_rows, query_low,
+         key_low, value_low, attended_low, probs, query_unit, key_unit, scales,
+         gain_q[None], gain_k[None], cosine, sine, normed_all, *w_cols, small),
+        expert_parts,
     )
     mixed = hidden + after(out_sum, d_w_out).astype(F32)
     if roomy:
         d_w_gate = d_w_gate.reshape(experts_local, width // seq_count, -1)
-        d_w_up = expert_sums[0].reshape(experts_local, width // seq_count, -1)
-        d_w_down = expert_sums[1].reshape(experts_local, -1, width)
-    d_three = d_three.reshape(seq_count, wrows, 3, cols).transpose(2, 1, 0, 3)
-    d_three = d_three.reshape(3, wrows, width).astype(F32)
+        d_w_up = (crossed[1].astype(F32) + crossed[2].astype(F32)).reshape(d_w_gate.shape)
+        d_w_down = (crossed[4].astype(F32) + crossed[5].astype(F32)).reshape(
+            experts_local, -1, width
+        )
     return (
         mixed.astype(BF)[None],
         d_tokens[None],
         small[-1],
-        d_three[0],
-        d_three[1],
-        d_three[2],
-        small[total_experts + 1],
-        small[total_experts + 2],
+        d_w_query,
+        d_w_key,
+        d_w_value,
+        small[-3],
+        small[-2],
         d_w_out,
         small[total_experts],
         small[:total_experts].T,

time: 581 us -> 542 us (0.933)
  Pallas kernels: 420 us -> 464 us
  local copies, waits for them, and re-layouts: 52.4 us -> 15.2 us
  matrix products: 47.3 us -> 20.2 us
  blocking collectives: 12.9 us -> 0 us
    pallas_call x5 -> x4, Pallas kernels: 420 us -> 464 us  [call(): pl.pallas_call(kernel, out_shape=outs, in_specs=specs or [ANY] * len(args...]
    dot_general x11 -> x0, matrix products: 21.7 us -> none  [the longest x3 5.34 us: each(): return jnp.einsum(how, left, right, preferred_element_type=F32)]
    unnamed x102 -> x40, local copies, waits for them, and re-layouts: 25.3 us -> 7.32 us
    psum x2 -> x0, blocking collectives: 12.9 us -> none  [row_sums(): return lax.psum(sums, 'seq') / width]
    dot_general x1, matrix products: 3.48 us -> 16.2 us  [local(): jnp.einsum('etd,dn->etn', normed2_all, router, preferred_element_type=F32)]
    dot_general x5 -> x1, matrix products: 12.6 us -> 0.25 us  [product(): return jnp.dot(left, right, preferred_element_type=F32)]
    add x0 -> x2, other arithmetic: none -> 8.13 us  [the longest x1 5.31 us: local(): crossed[1].astype(F32) + crossed[2].astype(F32)]
  transfers between devices with their start and end apart: 3 -> 3, of which waited for: 0 -> 0; matrix products, arithmetic and copies ran while one was open for 19% -> 9% of each run, Pallas kernels for 54% -> 66%
where the time goes in v3:
time: 542 us; the launch traced here: 538 us
  Pallas kernels  464 us (86%)
  other arithmetic  23.7 us (4%)
  matrix products  20.2 us (4%)
  local copies, waits for them, and re-layouts  15.2 us (3%)
  between operations  14.3 us (3%)
    pallas_call x4, Pallas kernels, call(): pl.pallas_call(kernel, out_shape=outs, in_specs=specs or [ANY] * len(args...  464 us
    dot_general x1, matrix products, local(): jnp.einsum('etd,dn->etn', normed2_all, router, preferred_element_type=F32)  16.2 us
  transfers between devices with their start and end apart: 3, of which 0 were waited for; matrix products, arithmetic and copies ran while one was open for 9% of the time, Pallas kernels for 66%

profile of v3, /device:TPU:0, one launch (start us, length us, event | category | flops | bytes accessed | tf_op | source)
XLA Modules:
  0.0 538.5 jit_solution(3017151555726913891)
XLA Ops:
  8.7 0.8 copy.59
  10.4 0.8 reduce-window.8
  11.2 1.3 dynamic_slice.12
  12.6 1.3 dynamic_slice.13
  13.9 1.2 fusion
  15.2 2.0 fusion.2.normed
  17.2 101.0 %shard_map.263 = (bf16[4,512,512]{2,1,0:T(8,128)(2,1)}, bf16[4,512,512]{2,1,0:T(8,128)(2,1)}, bf16[4,512,512]{2,1,0:T(8,128)(2,1)}, bf16[4,128,2048]{2,1,0:T(8,128)(2,1)}, bf16[8,128,128]{2,1,0:T(8,128)(2,1)}) custom-call(bf16[64,2048]{1,0:T(8,128)(2,1)} %wq.1, bf16[64,2048]{1,0:T(8,128)(2,1)} %wk.1, bf16[64,2048]{1,0:T(8,128)(2,1)} %wv.1, ...), custom_call_target="tpu_custom_call" | custom-call | bytes 270000000 | tf_op jit(solution)/shard_map/pallas_call | solution.py:375
  118.2 1.1 broadcast_compare_fusion
  120.6 0.8 copy.66.refs_2_
  121.6 1.0 multiply_sine_fusion
  122.6 1.0 pad_maximum_fusion
  123.6 1.2 fusion.5.bias
  124.8 83.4 %shard_map.264 = (f32[128,2048]{1,0:T(8,128)}, bf16[8,128,2048]{2,1,0:T(8,128)(2,1)}, bf16[512,512]{1,0:T(8,128)(2,1)}, bf16[512,512]{1,0:T(8,128)(2,1)}, bf16[5...) custom-call(bf16[512,2048]{1,0:T(8,128)(2,1)} %bitcast.65, ...), custom_call_target="tpu_custom_call" | custom-call | bytes 240000000 | tf_op jit(solution)/shard_map/pallas_call | solution.py:375
  208.3 16.2 %fusion.24 = (f32[8,128]{1,0:T(8,128)S(1)}, f32[8,128,16]{1,2,0:T(8,128)S(1)}) fusion(bf16[8,128,2048]{2,1,0:T(8,128)(2,1)} %get-tuple-element.50.refs_0_, bf16[2048,16]{0,1:T(8,128)(2,1)S(1)} %copy-done), kind=kOutput, calls=%fused_computation.62 | convolution fusion | flops 67124224 | bytes 4329472 | tf_op jit(solution)/shard_map/etd,dn->etn/dot_general | solution.py:1418
  225.1 1.0 broadcast_in_dim.38.refs_4_
  226.1 108.7 %shard_map.265 = (f32[128,2176]{1,0:T(8,128)}, bf16[8,128,2048]{2,1,0:T(8,128)(2,1)}, bf16[4,1024,1024]{2,1,0:T(8,128)(2,1)}, f32[1024,1024]{1,0:T(8,128)}, bf16...) custom-call(bf16[8,128,2048]{2,1,0:T(8,128)(2,1)} %get-tuple-element.50.refs_0_, ...), custom_call_target="tpu_custom_call" | custom-call | bytes 360000000 | tf_op jit(solution)/shard_map/pallas_call | solution.py:375
  334.9 1.1 copy-done.2
  336.9 1.1 multiply_reduce_fusion.3
  338.0 1.9 multiply_reduce_fusion
  339.9 1.3 fusion.26
  341.2 0.8 maximum_maximum_fusion.small
  341.9 1.5 fusion.20
  343.4 170.5 %shard_map.266 = (f32[128,2048]{1,0:T(8,128)}, f32[64,2048]{1,0:T(8,128)}, f32[64,2048]{1,0:T(8,128)}, f32[64,2048]{1,0:T(8,128)}, f32[64,2048]{1,0:T(8,128)}, /...) custom-call(bf16[128,2048]{1,0:T(8,128)(2,1)} %get-tuple-element.80., ...), custom_call_target="tpu_custom_call" | custom-call | bytes 450000000 | tf_op jit(solution)/shard_map/pallas_call | solution.py:375
  514.0 5.3 convert_add_fusion.1
  520.6 2.8 convert_add_fusion
  523.5 2.1 fusion.6
  525.6 1.0 copy.81
  526.6 0.8 copy.82
  527.4 0.8 copy.83
  528.2 0.8 copy.84
  529.0 0.8 copy.85
  529.8 2.0 copy.86
  (76 shorter events, 6.7 us)
Async XLA Ops:
  7.2 201.1 %copy-start = (bf16[2048,16]{0,1:T(8,128)(2,1)S(1)}, bf16[2048,16]{0,1:T(8,128)(2,1)}, u32[]{:S(2)}) copy-start(bf16[2048,16]{0,1:T(8,128)(2,1)} %param.27) | copy-start | bytes 196612
  7.2 114.3 %copy-start.16 = (s32[1,4]{1,0:T(1,128)S(1)}, s32[1,4]{1,0:T(1,128)}, u32[]{:S(2)}) copy-start(s32[1,4]{1,0:T(1,128)} %param.17) | copy-start | bytes 52
  7.2 117.6 %all-gather.3.cloned.1.call-start = ((), (), s32[]{:S(2)}) async-start(), calls=%async_computation.1 | async-start | bytes 2359296 | tf_op jit(solution)/shard_map/all_gather | solution.py:1394
  7.9 217.1 %all-gather.5.cloned.1.call-start = ((), (), s32[]{:S(2)}) async-start(), calls=%async_computation.2 | async-start | bytes 4718592 | tf_op jit(solution)/shard_map/all_gather | solution.py:1393
  8.7 514.8 %reduce-scatter.2.cloned.1.call-start = ((), (), s32[]{:S(2)}) async-start(), calls=%async_computation.3 | async-start | bytes 4718592 | tf_op jit(solution)/shard_map/reduce_scatter | solution.py:1446
  120.6 87.6 %copy-start.5 = (bf16[8,128,128]{1,2,0:T(8,128)(2,1)}, bf16[8,128,128]{1,2,0:T(8,128)(2,1)S(1)}, u32[]{:S(2)}) copy-start(bf16[8,128,128]{1,2,0:T(8,128)(2,1)S(1)} %and_convert_fusion) | copy-start | bytes 786436
  334.8 1.2 copy-start.2
  334.8 1.4 copy-start.15
  334.8 7.1 %copy-start.6 = (bf16[1,128,2048]{2,1,0:T(8,128)(2,1)S(1)}, bf16[1,128,2048]{2,1,0:T(8,128)(2,1)}, u32[]{:S(2)}) copy-start(bf16[1,128,2048]{2,1,0:T(8,128)(2,1)} %param.31) | copy-start | bytes 1572868
  514.0 5.3 copy-start.14
  514.0 6.6 %copy-start.7 = (bf16[512,2048]{1,0:T(8,128)(2,1)S(1)}, bf16[512,2048]{1,0:T(8,128)(2,1)}, u32[]{:S(2)}) copy-start(bf16[512,2048]{1,0:T(8,128)(2,1)} %get-tuple-element.74) | copy-start | bytes 6291460
  514.0 6.6 %copy-start.8 = (bf16[512,2048]{1,0:T(8,128)(2,1)S(1)}, bf16[512,2048]{1,0:T(8,128)(2,1)}, u32[]{:S(2)}) copy-start(bf16[512,2048]{1,0:T(8,128)(2,1)} %get-tuple-element.75) | copy-start | bytes 6291460
  520.6 2.9 copy-start.3
  520.6 5.0 copy-start.9
  523.5 4.7 copy-start.11
  523.5 5.5 %copy-start.10 = (f32[64,2048]{1,0:T(8,128)S(1)}, f32[64,2048]{1,0:T(8,128)}, u32[]{:S(2)}) copy-start(f32[64,2048]{1,0:T(8,128)} %get-tuple-element.122) | copy-start | bytes 1572868
  523.5 3.1 copy-start.13
  523.5 3.9 copy-start.12
  523.5 6.3 %copy-start.4 = (f32[1024,1024]{1,0:T(8,128)S(1)}, f32[1024,1024]{1,0:T(8,128)}, u32[]{:S(2)}) copy-start(f32[1024,1024]{1,0:T(8,128)} %get-tuple-element.71) | copy-start | bytes 12582916
  529.0 2.8 copy-start.1
Sparse Core Ops, SparseCore 0:
  10.2 74.2 all-gather.2
  86.6 83.6 all-gather.4
  334.9 119.7 reduce-scatter.1

commit v4 on v3

--- a/solution.py
+++ b/solution.py
@@ -305,21 +305,6 @@
             pltpu.SemaphoreType.DMA((4, size // 2))]
 
 
-class KeptScatter(Scatter):
-    def __init__(self, ring, x_ref, chunks, own, land, ringbuf, out, sems):
-        super().__init__(ring, x_ref, chunks, own, land, ringbuf, out, None, sems)
-
-    def start_place(self, t):
-        for c in range(self.chunks):
-            self.pair_copy(t, c).start()
-
-    def mine(self, t, c):
-        return self.own[pl.ds(t * self.x_ref.shape[1] + c * self.rows, self.rows)]
-
-    def arrive(self, t, c):
-        self.pair_copy(t, c).wait_recv()
-
-
 class PlaceScatter(Scatter):
     def __init__(self, ring, parts, chunks, land, ringbuf, sems):
         super().__init__(ring, parts, chunks, None, land, ringbuf, None, None, sems)
@@ -355,11 +340,6 @@
     less = pltpu.VMEM((max(outer_count - 1, 1), rows, columns), BF)
     return [buf, buf, less, less, pltpu.SemaphoreType.DMA((outer_count,)),
             pltpu.SemaphoreType.DMA((4, outer_count, chunks))]
-
-
-def kept_scratch(axis, rows, columns, chunks):
-    scratch = scatter_scratch(axis, rows, columns, chunks)
-    return scratch[1:4] + scratch[5:]
 
 
 SCATTER_REFS = 6
@@ -386,11 +366,20 @@
 
 
 def weights_kernel(
-    wq, wk, wv, normed, hits, q_out, k_out, v_out, normed_out, hits_out,
-    own_sems, swap_send, swap_recv, tok_send, tok_recv, g_send, g_recv,
+    wq, wk, wv, tokens, gain, routes, lengths, frequency,
+    q_out, k_out, v_out, normed_out, hits_out, cos_out, sin_out, bias_out,
+    normed, hits, own_sems, swap_send, swap_recv, tok_send, tok_recv, g_send, g_recv,
 ):
     seq, group = Ring("seq"), Ring("expert")
     others = [{"seq": seq.me ^ d} for d in range(1, seq.size)]
+    value = tokens[...].astype(F32)
+    inv = lax.rsqrt(jnp.mean(value * value, axis=-1, keepdims=True) + norm_eps)
+    normed[...] = (value * inv * gain[...]).astype(BF)
+    names = lax.broadcasted_iota(jnp.int32, hits.shape, 1)
+    hit = jnp.zeros(hits.shape, F32)
+    for k in range(routes.shape[1]):
+        hit = jnp.where(routes[:, k : k + 1] == names, 1.0, hit)
+    hits[...] = hit.astype(BF)
     greet(others + group.partners())
     wrows = wq.shape[0]
     cols = wq.shape[1] // seq.size
@@ -422,6 +411,31 @@
     own[4].start()
     for d in range(1, seq.size):
         token_copy(d).start()
+
+    length = bias_out.shape[0]
+
+    def starts_of(places):
+        first, doc = jnp.zeros_like(places), jnp.zeros_like(places)
+        end = jnp.zeros((1, 1), jnp.int32)
+        for d in range(lengths.shape[1]):
+            end = end + lengths[:, d : d + 1]
+            passed = places >= end
+            first = jnp.where(passed, end, first)
+            doc = doc + jnp.where(passed, 1, 0)
+        return first, doc
+
+    column = lax.broadcasted_iota(jnp.int32, (length, 128), 0)
+    first, doc = starts_of(column)
+    angles = (column - first).astype(F32) * frequency[...]
+    left = lax.broadcasted_iota(jnp.int32, (length, 128), 1) < 64
+    cos_out[...] = jnp.cos(angles)
+    sine = jnp.sin(angles)
+    sin_out[...] = jnp.where(left, sine, -sine)
+    row = lax.broadcasted_iota(jnp.int32, (1, length), 1)
+    row_doc = starts_of(row)[1]
+    bias_out[...] = jnp.where(
+        (doc[:, :1] == row_doc) & (row <= column[:, :1]), 0.0, masked_score
+    )
 
     def placed(ref):
         return lambda e: ref.at[:, pl.ds(e * wrows, wrows)]
@@ -453,19 +467,24 @@
     own[4].wait()
 
 
-def gather_weights(wq, wk, wv, normed, hits):
+def gather_weights(wq, wk, wv, tokens, gain, routes, lengths, frequency):
     seq_count, group_count = lax.axis_size("seq"), lax.axis_size("expert")
     width = wq.shape[1]
     w_shape = jax.ShapeDtypeStruct((seq_count, width // seq_count, width // seq_count), BF)
+    rows = tokens.shape[0]
+    length = rows * seq_count
     dma = pltpu.SemaphoreType.DMA
     return call(
         weights_kernel, 1, 90,
         (w_shape, w_shape, w_shape,
-         jax.ShapeDtypeStruct((seq_count,) + normed.shape, BF),
-         jax.ShapeDtypeStruct((group_count,) + hits.shape, BF)),
-        [dma((5,)), dma((3, seq_count)), dma((3, seq_count)), dma((seq_count,)), dma((seq_count,)),
+         jax.ShapeDtypeStruct((seq_count,) + tokens.shape, BF),
+         jax.ShapeDtypeStruct((group_count, rows, 128), BF),
+         jax.ShapeDtypeStruct((length, 128), F32), jax.ShapeDtypeStruct((length, 128), F32),
+         jax.ShapeDtypeStruct((length, length), F32)),
+        [pltpu.VMEM(tokens.shape, BF), pltpu.VMEM((rows, 128), BF), dma((5,)), dma((3, seq_count)), dma((3, seq_count)), dma((seq_count,)), dma((seq_count,)),
          dma((4, group_count // 2, 2)), dma((4, group_count // 2, 2))],
-        wq, wk, wv, normed, hits,
+        wq, wk, wv, tokens, gain, routes, lengths, frequency,
+        specs=[ANY] * 3 + [IN_VMEM] * 5, out_specs=(ANY,) * 5 + (IN_VMEM,) * 3,
     )
 
 
@@ -543,7 +562,8 @@
         for h in range(heads):
             value = unit[:, head(h)] * inv[:, i : i + 1]
             unit[:, head(h)] = value
-            out[:, head(h)] = turn(value * gains[:, head(h)], cos_rows, sin_rows).astype(BF)
+            at = pl.ds(pl.multiple_of(seq.me * cols + h * head_dim, head_dim), head_dim)
+            out[:, head(h)] = turn(value * gains[:, at], cos_rows, sin_rows).astype(BF)
 
     def probs_copy(h):
         return pltpu.make_async_copy(probs.at[h], probs_out.at[h], probs_sems.at[h])
@@ -657,24 +677,30 @@
 
 
 def expert_kernel(
-    n2, cot, sel, sel_t, gates, wg, wu, wd,
-    rows_out, out_parts, d_gate, d_up, d_down,
-    stage, parts, routed, cot_rows, wg_v, wu_v, wd_v, scaled, ggate, gup, gate_sums,
-    land, ringbuf, in_sems, w_sems, part_sems, wide_sems, out_sems, *dw_scratch,
+    n2, cot, hits, router, wg, wu, wd, hidden, cot_mine, gain,
+    grad_out, low_out, small_out, out_parts, d_gate, d_up, d_down,
+    stage, parts, routed, cot_rows, wg_v, wu_v, wd_v, scaled, ggate, gup, gate_sums, gates, one_hots,
+    land, ringbuf, in_sems, w_sems, part_sems, wide_sems, out_sems, last_sem,
+    gate_send, gate_keep, gate_land, gate_out, gate_in, gate_sems,
 ):
     seq, group = Ring("seq"), Ring("expert")
-    greet(seq.partners() + group.partners())
     groups, toks, width = n2.shape
     experts, rows, _ = routed.shape
     slots = rows // groups
     ff = wg_v.shape[1]
     n_total = experts * groups
-
-    def stage_copy(e):
-        return pltpu.make_async_copy(n2.at[e], stage.at[e], in_sems.at[0, e])
-
-    def cot_copy(e):
-        return pltpu.make_async_copy(cot.at[e], parts.at[e, :, pl.ds(0, width)], in_sems.at[1, e])
+    order = group_order(group)
+    pairs = len(order)
+    wide_at = pl.ds(0, width)
+
+    def two(k):
+        return pl.ds(group.at(order[k]) * 2, 2)
+
+    def stage_copy(k):
+        return pltpu.make_async_copy(n2.at[two(k)], stage.at[pl.ds(2 * k, 2)], in_sems.at[0, k])
+
+    def cot_copy(k):
+        return pltpu.make_async_copy(cot.at[two(k)], parts.at[two(k), :, wide_at], in_sems.at[1, k])
 
     def weight_copy(i, j):
         src, dst = ((wg, wg_v), (wu, wu_v), (wd, wd_v))[i]
@@ -683,93 +709,207 @@
     def each(count, body):
         lax.fori_loop(0, count, lambda i, _: (body(i), 0)[1], 0)
 
-    each(groups, lambda e: stage_copy(e).start())
+    for k in range(pairs):
+        stage_copy(k).start()
     for i in range(3):
         weight_copy(i, 0).start()
-    each(groups, lambda e: cot_copy(e).start())
-
-    def pick(copy, src, dst):
-        def body(e):
-            copy(e).wait()
-            got = dot(sel[e], src[e, :, pl.ds(0, width)]).astype(BF)
-            at = pl.ds(pl.multiple_of(e * slots, slots), slots)
+    for k in range(pairs):
+        cot_copy(k).start()
+    greet(seq.partners() + group.partners())
+
+    lanes = lax.broadcasted_iota(jnp.int32, (toks, 128), 1)
+    first_half = lanes < slots
+    slot_of = jnp.where(first_half, lanes, lanes - slots).astype(F32)
+    earlier = jnp.where(
+        lax.broadcasted_iota(jnp.int32, (toks, toks), 0)
+        > lax.broadcasted_iota(jnp.int32, (toks, toks), 1), 1.0, 0.0
+    ).astype(BF)
+
+    def softmax(logits):
+        known = lax.broadcasted_iota(jnp.int32, logits.shape, 1) < n_total
+        logits = jnp.where(known, logits, masked_score)
+        weights = jnp.exp(logits - jnp.max(logits, axis=-1, keepdims=True))
+        return weights / jnp.sum(weights, axis=-1, keepdims=True)
+
+    def of_mine(values):
+        first, second = [
+            jnp.sum(jnp.where(lanes == group.me * experts + j, values, 0.0), axis=1, keepdims=True)
+            for j in range(experts)
+        ]
+        return jnp.where(first_half, first, second)
+
+    one_hots[...] = jnp.zeros_like(one_hots)
+    for k in range(pairs):
+        stage_copy(k).wait()
+        for b in range(2):
+            p = 2 * k + b
+            hit = hits[group.at(order[k]) * 2 + b]
+            rank = of_mine(dot(earlier, hit))
+            chosen = (of_mine(hit.astype(F32)) > 0.0) & (rank == slot_of)
+            one_hot = jnp.where(chosen, 1.0, 0.0)
+            gate = of_mine(softmax(dot(stage[p], router[...])))
+            row = jnp.sum(one_hot * gate, axis=0, keepdims=True)
+            column = jnp.broadcast_to(row, (128, 128)).T
             for j in range(experts):
-                dst[j, at] = got[j * slots : (j + 1) * slots]
-        return body
-
-    each(groups, pick(stage_copy, stage, routed))
-    each(groups, pick(cot_copy, parts, cot_rows))
-
-    for j in range(experts):
-        for i in range(3):
-            weight_copy(i, j).wait()
-        gate_sums[j] = jnp.zeros_like(gate_sums[j])
-
-        def hidden_tile(f, j=j):
+                gates[j, p * slots : (p + 1) * slots] = column[j * slots : (j + 1) * slots]
+            one_hots[k, b * toks : (b + 1) * toks, b * 128 : (b + 1) * 128] = one_hot.astype(BF)
+
+    def pick(k, values, dst):
+        got = dot(one_hots[k], values.reshape(2 * toks, width), 0, 0).astype(BF)
+        for b in range(2):
+            at = slice((2 * k + b) * slots, (2 * k + b + 1) * slots)
+            for j in range(experts):
+                start = b * 128 + j * slots
+                dst[j, at] = got[start : start + slots]
+
+    for k in range(pairs):
+        pick(k, stage[2 * k : 2 * k + 2], routed)
+    for k in range(pairs):
+        cot_copy(k).wait()
+        pick(k, parts[two(k), :, wide_at], cot_rows)
+
+    def hidden_tiles(j, start, count):
+        span = slice(start, start + count)
+
+        def tile(f):
             at = pl.ds(pl.multiple_of(f * TILE, TILE), TILE)
-            gate_pre = dot(routed[j], wg_v[:, at])
-            up_pre = dot(routed[j], wu_v[:, at])
-            unit = dot(cot_rows[j], wd_v[at, :], 1, 1)
-            gate = gates[j][:, :1]
+            gate_pre = dot(routed[j, span], wg_v[:, at])
+            up_pre = dot(routed[j, span], wu_v[:, at])
+            unit = dot(cot_rows[j, span], wd_v[at, :], 1, 1)
+            gate = gates[j, span][:, :1]
             sig = 1.0 / (1.0 + jnp.exp(-gate_pre))
             silu = gate_pre * sig
             active = silu * up_pre
             low = active.astype(BF).astype(F32)
-            gate_sums[j] += jnp.sum(unit * low, axis=-1, keepdims=True)
-            scaled[j, :, at] = (low * gate).astype(BF)
+            gate_sums[j, span] += jnp.sum(unit * low, axis=-1, keepdims=True)
+            scaled[j, span, at] = (low * gate).astype(BF)
             grad_active = unit * gate
-            ggate[j, :, at] = (grad_active * up_pre * sig * (1.0 + gate_pre * (1.0 - sig))).astype(BF)
-            gup[j, :, at] = (grad_active * silu).astype(BF)
-
-        each(ff // TILE, hidden_tile)
+            ggate[j, span, at] = (
+                grad_active * up_pre * sig * (1.0 + gate_pre * (1.0 - sig))
+            ).astype(BF)
+            gup[j, span, at] = (grad_active * silu).astype(BF)
+
+        each(ff // TILE, tile)
+
+    def row_tiles(j, start, count):
+        span = slice(start, start + count)
+        blocks = slice(start // slots, (start + count) // slots)
+
+        def tile(d):
+            at = pl.ds(pl.multiple_of(d * TILE, TILE), TILE)
+            grad = dot(ggate[j, span], wg_v[at, :], 1, 1) + dot(gup[j, span], wu_v[at, :], 1, 1)
+            stage[blocks, j * slots : (j + 1) * slots, at] = grad.astype(BF).reshape(
+                count // slots, slots, TILE
+            )
+
+        each(width // TILE, tile)
+
+    scatter = PlaceScatter(group, parts, GRAD_CHUNKS, land, ringbuf, part_sems)
+    row_lanes = lanes[:slots]
+
+    def place(k):
+        value = dot(one_hots[k], stage[2 * k : 2 * k + 2].reshape(2 * toks, width))
+        parts[two(k), :, wide_at] = value.astype(BF).reshape(2, toks, width)
+        sums = []
+        for p in (2 * k, 2 * k + 1):
+            for j in range(experts):
+                value = gate_sums[j, p * slots : (p + 1) * slots]
+                first = value.astype(BF).astype(F32)
+                mine = group.me * experts + j
+                sums.append(jnp.where(row_lanes == mine, first,
+                                      jnp.where(row_lanes == mine + n_total, value - first, 0.0)))
+        value = dot(one_hots[k], jnp.concatenate(sums, axis=0).astype(BF))
+        parts[two(k), :, pl.ds(width, 128)] = value.astype(BF).reshape(2, toks, 128)
+        scatter.start_place(order[k])
+
+    side, short = width // seq.size, ff // seq.size
+
+    def wide_grad(right, s, j):
+        at = pl.ds(pl.multiple_of(s * side, side), side)
+        return dot(routed[j, :, at], right[j], 0, 0).astype(BF)
+
+    def rows_of(j):
+        return pl.ds(j * side, side)
+
+    def gate_pair(t, j):
+        return remote(gate_send, gate_land.at[t, rows_of(j)], gate_sems.at[0, t, j],
+                      gate_sems.at[1, t, j], seq.pair)
+
+    def gate_cross(j):
+        return remote(gate_out.at[rows_of(j)], gate_in.at[rows_of(j)], gate_sems.at[2, 0, j],
+                      gate_sems.at[3, 0, j], seq.next)
+
+    def gate_part(j):
+        for t in (1, 0):
+            if t == 0:
+                gate_pair(1, j).wait_send()
+            elif j:
+                gate_pair(0, j - 1).wait_send()
+            gate_send[...] = wide_grad(ggate, seq.at(t) * 2 + 1 - seq.inner, j)
+            gate_pair(t, j).start()
+            mine = wide_grad(ggate, seq.at(t) * 2 + seq.inner, j)
+            if t:
+                gate_pair(t, j).wait_recv()
+                total = mine.astype(F32) + gate_land[t, rows_of(j)].astype(F32)
+                gate_out[rows_of(j)] = total.astype(BF)
+                gate_cross(j).start()
+            else:
+                gate_keep[rows_of(j)] = mine
+
+    gate_sums[...] = jnp.zeros_like(gate_sums)
+    half = rows // 2
+    for j in range(experts):
+        for i in range(3):
+            weight_copy(i, j).wait()
         if j + 1 < experts:
+            hidden_tiles(j, 0, rows)
             weight_copy(2, j + 1).start()
-
-        def row_tile(d, j=j):
-            at = pl.ds(pl.multiple_of(d * TILE, TILE), TILE)
-            grad = dot(ggate[j], wg_v[at, :], 1, 1) + dot(gup[j], wu_v[at, :], 1, 1)
-            stage[:, j * slots : (j + 1) * slots, at] = grad.astype(BF).reshape(groups, slots, TILE)
-
-        each(width // TILE, row_tile)
-        if j + 1 < experts:
+            row_tiles(j, 0, rows)
             weight_copy(0, j + 1).start()
             weight_copy(1, j + 1).start()
-    weight_copy(2, 0).start()
-
-    scatter = PlaceScatter(group, parts, GRAD_CHUNKS, land, ringbuf, part_sems)
-    lanes = lax.broadcasted_iota(jnp.int32, (slots, 128), 1)
-
-    def place(e):
-        parts[e, :, pl.ds(0, width)] = dot(sel_t[e], stage[e]).astype(BF)
-        at = pl.ds(pl.multiple_of(e * slots, slots), slots)
-        high, low = [], []
-        for j in range(experts):
-            value = gate_sums[j, at]
-            first = value.astype(BF)
-            rest = (value - first.astype(F32)).astype(BF)
-            mine = group.me * experts + j
-            high.append(jnp.where(lanes == mine, first.astype(F32),
-                                  jnp.where(lanes == mine + n_total, rest.astype(F32), 0.0)))
-        parts[e, :, pl.ds(width, 128)] = dot(
-            sel_t[e], jnp.concatenate(high, axis=0).astype(BF)
-        ).astype(BF)
-
-    for t in scatter.order:
-        place(group.at(t) * 2 + 1 - group.inner)
-        scatter.start_place(t)
-        place(group.at(t) * 2 + group.inner)
+            gate_part(j)
+        else:
+            hidden_tiles(j, 0, half)
+            row_tiles(j, 0, half)
+            for k in range(pairs // 2):
+                place(k)
+            hidden_tiles(j, half, half)
+            weight_copy(2, 0).start()
+            row_tiles(j, half, half)
+            for k in range(pairs // 2, pairs):
+                place(k)
 
     def grad_step(t):
         for c in range(GRAD_CHUNKS):
             total = scatter.step(t, c)
             if not t:
-                rows_out[scatter.cut(c)] = total
-
-    side, short = width // seq.size, ff // seq.size
-
-    def wide_grad(right, s, j):
-        at = pl.ds(pl.multiple_of(s * side, side), side)
-        return dot(routed[j, :, at], right[j], 0, 0).astype(BF)
+                finish_rows(c, total)
+
+    def finish_rows(c, total):
+        cut = scatter.cut(c)
+        value = hidden[cut]
+        inv = lax.rsqrt(jnp.mean(value * value, axis=-1, keepdims=True) + norm_eps)
+        unit = value * inv
+        normed2 = (unit * gain[...]).astype(BF)
+        probs = softmax(dot(normed2, router[...]))
+        both = total[:, width:]
+        grad_probs = jnp.where(
+            lax.broadcasted_iota(jnp.int32, both.shape, 1) < n_total,
+            both + pltpu.roll(both, 128 - n_total, 1), 0.0,
+        )
+        grad_logits = probs * (grad_probs - jnp.sum(probs * grad_probs, axis=-1, keepdims=True))
+        grad_logits = grad_logits.astype(BF)
+        grad = total[:, :width] + dot(grad_logits, router[...], 1, 1)
+        gained = grad * gain[...]
+        mean = jnp.mean(gained * unit, axis=-1, keepdims=True)
+        result = cot_mine[cut].astype(F32) + inv * (gained - unit * mean)
+        grad_out[cut] = result
+        low_out[cut] = result.astype(BF)
+        count = small_out.shape[0]
+        sums = dot(grad_logits, normed2, 0, 0)[:count]
+        line = lax.broadcasted_iota(jnp.int32, sums.shape, 0)
+        sums = jnp.where(line == n_total, jnp.sum(grad * unit, axis=0, keepdims=True), sums)
+        small_out[...] = sums if c == 0 else small_out[...] + sums
 
     def send_wide(right, out, s):
         copies = [
@@ -800,18 +940,9 @@
         for copy in copies:
             copy.wait()
 
-    dw = KeptScatter(seq, d_gate[0], 1, wu_v, *dw_scratch)
-    for t in dw.order:
-        send_wide(ggate, d_gate[0], seq.at(t) * 2 + 1 - seq.inner)
-        dw.start_place(t)
+    for j in range(1, experts):
+        gate_part(j)
     grad_step(scatter.order[0])
-    for t in dw.order:
-        for j in range(experts):
-            wu_v[pl.ds((t * experts + j) * side, side)] = wide_grad(
-                ggate, seq.at(t) * 2 + seq.inner, j
-            )
-        if t:
-            dw.step(t, 0)
     if len(scatter.order) > 2:
         grad_step(scatter.order[1])
     each(seq.size, lambda s: send_wide(gup, d_up, s))
@@ -831,56 +962,64 @@
         if j + 1 < experts:
             weight_copy(2, j + 1).start()
 
-    def out_copy(e):
-        return pltpu.make_async_copy(stage.at[e], out_parts.at[e], out_sems.at[e])
-
-    def out_place(e):
-        stage[e] = dot(sel_t[e], stage[e]).astype(BF)
-        out_copy(e).start()
-
-    each(groups, out_place)
+    def out_copy(k):
+        return pltpu.make_async_copy(stage.at[pl.ds(2 * k, 2)], out_parts.at[two(k)], out_sems.at[k])
+
+    for k in range(pairs):
+        value = dot(one_hots[k], stage[2 * k : 2 * k + 2].reshape(2 * toks, width))
+        stage[2 * k : 2 * k + 2] = value.astype(BF).reshape(2, toks, width)
+        out_copy(k).start()
     grad_step(0)
-    d_gate[1][...] = dw.step(0, 0)
-    each(groups, lambda e: out_copy(e).wait())
+    for j in range(experts):
+        gate_pair(0, j).wait_recv()
+        gate_cross(j).wait_recv()
+        at = rows_of(j)
+        total = gate_keep[at].astype(F32) + gate_land[0, at].astype(F32) + gate_in[at].astype(F32)
+        gate_keep[at] = total.astype(BF)
+    gate_copy = pltpu.make_async_copy(gate_keep, d_gate, last_sem.at[0])
+    gate_copy.start()
+    for k in range(pairs):
+        out_copy(k).wait()
+    gate_copy.wait()
     scatter.finish()
-    dw.finish()
-
-
-def run_experts(n2, cot, sel, sel_t, gates, wg, wu, wd):
+    gate_pair(0, experts - 1).wait_send()
+    for j in range(experts):
+        gate_cross(j).wait_send()
+
+
+def run_experts(n2, cot, hits, router, wg, wu, wd, hidden, cot_mine, gain):
     seq_count, group_count = lax.axis_size("seq"), lax.axis_size("expert")
     experts, width, ff = wg.shape
     toks = n2.shape[1]
-    rows = gates.shape[1]
+    rows = group_count * MOST
     outer_count = group_count // 2
     columns = width + 128
+    small_rows = -(-(experts * group_count + 1) // 8) * 8
     dma = pltpu.SemaphoreType.DMA
     side, short = width // seq_count, ff // seq_count
 
-    def kernel(*refs):
-        ins, outs, scratch = refs[:8], refs[8:14], refs[14:]
-        expert_kernel(*ins, outs[0], outs[1], (outs[2], outs[3]), outs[4], outs[5], *scratch)
-
     low = lambda *shape: pltpu.VMEM(shape, BF)
+    out = jax.ShapeDtypeStruct
     return call(
-        kernel, 6, 120,
-        (jax.ShapeDtypeStruct((toks, columns), F32),
-         jax.ShapeDtypeStruct((group_count, toks, width), BF),
-         jax.ShapeDtypeStruct((seq_count, experts * side, ff), BF),
-         jax.ShapeDtypeStruct((experts * side, ff), F32),
-         jax.ShapeDtypeStruct((seq_count, experts * side, ff), BF),
-         jax.ShapeDtypeStruct((seq_count, experts * short, width), BF)),
+        expert_kernel, 6, 100,
+        (out((toks, width), F32), out((toks, width), BF), out((small_rows, width), F32),
+         out((group_count, toks, width), BF),
+         out((experts * side, ff), BF),
+         out((seq_count, experts * side, ff), BF), out((seq_count, experts * short, width), BF)),
         [low(group_count, toks, width), low(group_count, toks, columns),
          low(experts, rows, width), low(experts, rows, width),
          low(width, ff), low(width, ff), low(ff, width),
          low(experts, rows, ff), low(experts, rows, ff), low(experts, rows, ff),
-         pltpu.VMEM((experts, rows, 128), F32),
+         pltpu.VMEM((experts, rows, 128), F32), pltpu.VMEM((experts, rows, 128), F32),
+         low(outer_count, 2 * toks, 256),
          low(outer_count, toks, columns), low(outer_count - 1, toks, columns),
-         dma((2, group_count)), dma((3,)), dma((4, outer_count, GRAD_CHUNKS)), dma((experts,)),
-         dma((group_count,))]
-        + kept_scratch("seq", experts * side, ff, 1),
-        n2, cot, sel, sel_t, gates, wg, wu, wd,
-        specs=[ANY, ANY, IN_VMEM, IN_VMEM, IN_VMEM, ANY, ANY, ANY],
-        out_specs=(IN_VMEM, ANY, ANY, IN_VMEM, ANY, ANY),
+         dma((2, outer_count)), dma((3,)), dma((4, outer_count, GRAD_CHUNKS)), dma((experts,)),
+         dma((group_count,)), dma((1,)),
+         low(side, ff), low(experts * side, ff), low(2, experts * side, ff),
+         low(experts * side, ff), low(experts * side, ff), dma((4, 2, experts))],
+        n2, cot, hits, router, wg, wu, wd, hidden, cot_mine, gain,
+        specs=[ANY, ANY, IN_VMEM, IN_VMEM, ANY, ANY, ANY, IN_VMEM, IN_VMEM, IN_VMEM],
+        out_specs=(IN_VMEM, IN_VMEM, IN_VMEM, ANY, ANY, ANY, ANY),
     )
 
 
@@ -888,9 +1027,38 @@
 CROSS_CHUNKS = 8
 
 
+class AllSum:
+    def __init__(self, steps, sums, land, sems):
+        self.steps, self.sums, self.land, self.sems = steps, sums, land, sems
+        self.at = 0
+
+    def copy(self, i):
+        return remote(self.sums.at[i], self.land.at[i], self.sems.at[0, i], self.sems.at[1, i], self.steps[i])
+
+    def start(self):
+        self.copy(0).start()
+
+    def hop(self):
+        i = self.at
+        if i == len(self.steps):
+            return
+        self.at += 1
+        self.copy(i).wait_recv()
+        self.sums[i + 1] = self.sums[i] + self.land[i]
+        if self.at < len(self.steps):
+            self.copy(self.at).start()
+
+    def result(self):
+        while self.at < len(self.steps):
+            self.hop()
+        for i in range(len(self.steps)):
+            self.copy(i).wait_send()
+        return self.sums[len(self.steps)]
+
+
 class Cross:
-    def __init__(self, seq, parts, land, mine, crossed, bufs, stage, sems):
-        self.seq, self.parts, self.land, self.mine, self.crossed = seq, parts, land, mine, crossed
+    def __init__(self, seq, parts, land, crossed, bufs, stage, sems):
+        self.seq, self.parts, self.land, self.crossed = seq, parts, land, crossed
         self.bufs, self.stage, self.sems = bufs, stage, sems
         self.rows = parts.shape[1] // CROSS_CHUNKS
 
@@ -898,39 +1066,25 @@
         src = self.parts.at[self.seq.at(t) * 2 + 1 - self.seq.inner]
         return remote(src, self.land.at[t], self.sems.at[0, t], self.sems.at[1, t], self.seq.pair)
 
-    def start(self):
-        self.swap(1).start()
-        self.swap(0).start()
-
     def loads(self, i):
-        t, c = 1 - i // CROSS_CHUNKS, i % CROSS_CHUNKS
-        cut = pl.ds(c * self.rows, self.rows)
-        own = self.parts.at[self.seq.at(t) * 2 + self.seq.inner, cut]
+        cut = pl.ds(i * self.rows, self.rows)
+        own = self.parts.at[self.seq.at(1) * 2 + self.seq.inner, cut]
         return [
             pltpu.make_async_copy(own, self.bufs.at[i % 2, 0], self.sems.at[2, i % 2]),
-            pltpu.make_async_copy(self.land.at[t, cut], self.bufs.at[i % 2, 1], self.sems.at[3, i % 2]),
+            pltpu.make_async_copy(self.land.at[1, cut], self.bufs.at[i % 2, 1], self.sems.at[3, i % 2]),
         ]
 
     def load(self, i):
-        if i >= 2 * CROSS_CHUNKS:
-            return
-        if i % CROSS_CHUNKS == 0:
-            self.swap(1 - i // CROSS_CHUNKS).wait_recv()
-        for copy in self.loads(i):
-            copy.start()
+        if i == 0:
+            self.swap(1).wait_recv()
+        if i < CROSS_CHUNKS:
+            for copy in self.loads(i):
+                copy.start()
 
     def send(self, i):
-        cut = pl.ds((i % CROSS_CHUNKS) * self.rows, self.rows)
-        if i < CROSS_CHUNKS:
-            return remote(self.stage.at[i % 2], self.crossed.at[cut], self.sems.at[4, i % 2],
-                          self.sems.at[5, i % CROSS_CHUNKS], self.seq.next)
-        return pltpu.make_async_copy(self.stage.at[i % 2], self.mine.at[cut], self.sems.at[4, i % 2])
-
-    def wait_sent(self, i):
-        if i < CROSS_CHUNKS:
-            self.send(i).wait_send()
-        else:
-            self.send(i).wait()
+        cut = pl.ds(i * self.rows, self.rows)
+        return remote(self.stage.at[i % 2], self.crossed.at[cut], self.sems.at[4, i % 2],
+                      self.sems.at[5, i], self.seq.next)
 
     def tick(self, i):
         if i == 0:
@@ -939,17 +1093,17 @@
             copy.wait()
         self.load(i + 1)
         if i >= 2:
-            self.wait_sent(i - 2)
+            self.send(i - 2).wait_send()
         total = self.bufs[i % 2, 0].astype(F32) + self.bufs[i % 2, 1].astype(F32)
         self.stage[i % 2] = total.astype(BF)
         self.send(i).start()
 
     def finish(self):
-        last = 2 * CROSS_CHUNKS
-        self.wait_sent(last - 2)
-        self.wait_sent(last - 1)
+        self.send(CROSS_CHUNKS - 2).wait_send()
+        self.send(CROSS_CHUNKS - 1).wait_send()
         for c in range(CROSS_CHUNKS):
             self.send(c).wait_recv()
+        self.swap(0).wait_recv()
         self.swap(0).wait_send()
         self.swap(1).wait_send()
 
@@ -987,16 +1141,19 @@
     w_rows, normed, probs, q_unit, k_unit, wq, wk, wv = copies
     d_tokens, d_q, d_k, d_v, d_out, small_out = refs[:6]
     refs = refs[6:]
-    cross_out, refs = refs[: 3 * crossings], refs[3 * crossings :]
+    cross_out, refs = refs[: 2 * crossings], refs[2 * crossings :]
     cross_bufs, refs = refs[: 3 * crossings], refs[3 * crossings :]
     place = [refs[4 * i : 4 * i + 4] for i in range(5)]
     (grad_all, normed_t, grad_att, grad_g, grad_three, dk_sum, row_send, row_land,
-     low_send, low_land, sum_buf, sum_land,
-     own_sem, pack_send, pack_recv, row_sems, swap_sems, sum_sems) = refs[20:]
+     low_send, low_land, early_buf, early_land, late_buf, late_land,
+     own_sem, pack_send, pack_recv, row_sems, swap_sems, early_sems, late_sems) = refs[20:]
     seq, group = Ring("seq"), Ring("expert")
     others = [{"seq": seq.me ^ d} for d in range(1, seq.size)]
     known = [{"expert": group.me ^ (1 << i)} for i in range((group.size - 1).bit_length())]
-    steps = known + [{"seq": seq.me ^ (1 << i)} for i in range((seq.size - 1).bit_length())]
+    across = [{"seq": seq.me ^ (1 << i)} for i in range((seq.size - 1).bit_length())]
+    early_sums = AllSum(known[::-1] + across, early_buf, early_land, early_sems)
+    late_sums = AllSum(across[:1] + known[::-1] + across[1:], late_buf, late_land, late_sems)
+    early_rows = small.shape[0]
     for name in LATE:
         late[name].start()
     greet(others + known + [group.next, group.last])
@@ -1009,11 +1166,10 @@
     scale = head_dim**-0.5
 
     crosses = [
-        Cross(seq, expert_parts[i], *cross_out[3 * i : 3 * i + 3], *cross_bufs[3 * i : 3 * i + 3])
+        Cross(seq, expert_parts[i], *cross_out[2 * i : 2 * i + 2], *cross_bufs[3 * i : 3 * i + 3])
         for i in range(crossings)
     ]
-    ticks = [(cross, i) for i in range(2 * CROSS_CHUNKS) for cross in crosses]
-    ticks = [t for t in ticks if t[1] < CROSS_CHUNKS] + [t for t in ticks if t[1] >= CROSS_CHUNKS]
+    ticks = [(cross, i) for i in range(CROSS_CHUNKS) for cross in crosses]
 
     def tick(count=1):
         for _ in range(count):
@@ -1025,15 +1181,21 @@
     own.start()
     pack = Gather(seq, lambda s: grad_all.at[s], pack_send, pack_recv)
     pack.start(grad_low)
-    for cross in crosses:
-        cross.start()
+    early_buf[0] = small[...]
+    early_sums.start()
+    late_buf[0] = jnp.zeros_like(late_buf[0])
+    for t in (1, 0):
+        for cross in crosses:
+            cross.swap(t).start()
     size = width // seq.size
     late["normed"].wait()
     for s in range(seq.size):
         normed_t[pl.ds(s * size, size)] = normed[:, s * size : (s + 1) * size].T
+        if s % 2:
+            early_sums.hop()
     for back in range(1, seq.outer_count):
         pack.relay(back)
-    tick()
+    tick(2)
     own.wait()
     pack.finish()
 
@@ -1053,6 +1215,7 @@
     def head(h):
         return slice(h * head_dim, (h + 1) * head_dim)
 
+    early_sums.hop()
     late["probs"].wait()
     for h in range(heads):
         grad_three[2, :, head(h)] = dot(
@@ -1067,8 +1230,9 @@
             )
         sums.start()
 
+    tick()
     weight_grad(2, value_sums)
-    tick()
+    early_sums.hop()
     for c in range(0, width, 512):
         at = slice(c, c + 512)
         value = dot(attended[...], grad_all[:, :, at].reshape(length, 512), 0, 0)
@@ -1091,7 +1255,7 @@
 
     def through_rope(i, h, grad, unit, gains):
         turned = turn(grad, cos_rows, sin_rows)
-        sum_buf[0, pl.ds(gain_rows[i], 1), pl.ds(pl.multiple_of(seq.me * cols, 128) + h * head_dim, head_dim)] = (
+        late_buf[0, pl.ds(i, 1), pl.ds(pl.multiple_of(seq.me * cols, 128) + h * head_dim, head_dim)] = (
             jnp.sum(turned * unit, axis=0, keepdims=True)
         )
         gained = turned * gains
@@ -1100,8 +1264,7 @@
 
     late["q_unit"].wait()
     late["k_unit"].wait()
-    sum_buf[0] = small[...]
-    gain_rows = (small.shape[0] - 3, small.shape[0] - 2)
+    early_sums.hop()
     for h in range(heads):
         queries = []
         for b in range(0, length, Q_BLOCK):
@@ -1113,8 +1276,9 @@
             queries.append(dot(grad_scores, k_low[:, head(h)]) * scale)
             keys = dot(grad_scores, q_low[rows, head(h)], 0, 0)
             dk_sum[...] = keys if b == 0 else dk_sum[...] + keys
-        through_rope(0, h, jnp.concatenate(queries, axis=0), q_unit[:, head(h)], gain_q[:, head(h)])
-        through_rope(1, h, dk_sum[...] * scale, k_unit[:, head(h)], gain_k[:, head(h)])
+        at = pl.ds(pl.multiple_of(seq.me * cols + h * head_dim, head_dim), head_dim)
+        through_rope(0, h, jnp.concatenate(queries, axis=0), q_unit[:, head(h)], gain_q[:, at])
+        through_rope(1, h, dk_sum[...] * scale, k_unit[:, head(h)], gain_k[:, at])
         if h == 1:
             value_step()
 
@@ -1134,7 +1298,7 @@
         total = total + row_land[d]
     for d in range(1, seq.size):
         row_copy(d).wait_send()
-    tick(2)
+    tick(3)
     means = jnp.concatenate([total / width, jnp.zeros((120, length), F32)], axis=0).T
     for i, (unit, sums) in enumerate(((q_unit, query_sums), (k_unit, key_sums))):
         for h in range(heads):
@@ -1151,7 +1315,7 @@
         normed_sums.x_ref[:, :, at] = value.astype(BF).reshape(seq.size, toks, 512)
     normed_sums.start()
     out_step()
-    tick()
+    tick(2)
 
     swaps = {}
 
@@ -1187,7 +1351,9 @@
         mean = jnp.mean(gained * unit, axis=-1, keepdims=True)
         d_tokens[cut] = grad_hidden[cut] + inv * (gained - unit * mean)
         gain_sum = gain_sum + jnp.sum(grad * unit, axis=0, keepdims=True)
-    sum_buf[0, pl.ds(small.shape[0] - 1, 1)] = gain_sum
+    late_buf[0, pl.ds(2, 1)] = gain_sum
+
+    late_sums.start()
     tick()
     send_columns(2, value_sums)
     out_sums.step(0)
@@ -1196,24 +1362,14 @@
         tick(2)
         key_sums.step(t, 0)
         tick(2)
+        late_sums.hop()
     d_out[...] = out_sums.last()
     tick()
     send_columns(0, query_sums)
+    late_sums.hop()
     send_columns(1, key_sums)
-
-    def sum_copy(i):
-        return remote(sum_buf.at[i], sum_land.at[i], sum_sems.at[0, i], sum_sems.at[1, i], steps[i])
-
-    sum_copy(0).start()
-    for i in range(len(steps)):
-        sum_copy(i).wait_recv()
-        total = sum_buf[i] + sum_land[i]
-        if i + 1 < len(steps):
-            sum_buf[i + 1] = total
-            sum_copy(i + 1).start()
-        else:
-            small_out[...] = total
-        tick()
+    late_sums.hop()
+
     tick(len(ticks))
     for i, out in ((2, d_v), (0, d_q), (1, d_k)):
         for d in range(1, seq.size):
@@ -1223,8 +1379,8 @@
         low_land[i, seq.me] = low_send[i, pl.ds(pl.multiple_of(seq.me * wrows, wrows), wrows)]
         for s in range(seq.size):
             out[:, s * cols : (s + 1) * cols] = low_land[i, s].astype(F32)
-    for i in range(len(steps)):
-        sum_copy(i).wait_send()
+    small_out[pl.ds(0, early_rows)] = early_sums.result()
+    small_out[pl.ds(early_rows, 8)] = late_sums.result()
     for cross in crosses:
         cross.finish()
     for sums in (query_sums, key_sums, value_sums, out_sums, normed_sums):
@@ -1249,12 +1405,11 @@
     low = lambda *shape: pltpu.VMEM(shape, BF)
     full = lambda *shape: pltpu.VMEM(shape, F32)
     shape = lambda *dims: jax.ShapeDtypeStruct(dims, F32)
-    outs = [shape(rows, width)] + [shape(wrows, width)] * 4 + [shape(*small.shape)]
+    outs = [shape(rows, width)] + [shape(wrows, width)] * 4 + [shape(small.shape[0] + 8, width)]
     cross_outs, scratch = [], []
     for parts in expert_parts:
         size = parts.shape[1:]
-        cross_outs += [jax.ShapeDtypeStruct((2,) + size, BF), jax.ShapeDtypeStruct(size, BF),
-                       jax.ShapeDtypeStruct(size, BF)]
+        cross_outs += [jax.ShapeDtypeStruct((2,) + size, BF), jax.ShapeDtypeStruct(size, BF)]
         scratch += cross_scratch(parts)
     for _ in range(3):
         scratch += place_scratch("expert", group_count, side, cols, 1)
@@ -1265,9 +1420,10 @@
         full(2, length, cols), low(3, length, cols), full(length, head_dim),
         full(8, length), full(seq_count, 8, length),
         low(3, side, cols), low(3, seq_count, wrows, cols),
-        full(count, *small.shape), full(count, *small.shape),
+        full(count + 1, *small.shape), full(count, *small.shape),
+        full(count + 1, 8, width), full(count, 8, width),
         dma((1,)), dma((seq_count // 2, 2)), dma((seq_count // 2, 2)), dma((2, seq_count)),
-        dma((2, 3, seq_count)), dma((2, count)),
+        dma((2, 3, seq_count)), dma((2, count)), dma((2, count)),
     ]
     scratch += [pltpu.VMEM(ins[i].shape, ins[i].dtype) for i in LATE_AT] + [dma((len(LATE),))]
     return call(
@@ -1277,6 +1433,52 @@
         + [ANY] * len(expert_parts),
         out_specs=tuple([IN_VMEM] * len(outs) + [ANY] * len(cross_outs)),
     )
+
+
+ADD_STEPS = 8
+
+
+def add_kernel(
+    place, gate, up, up_land, up_in, down, down_land, down_in, hidden, out_sum, *refs
+):
+    copies, refs = refs[:5], refs[5:]
+    d_gate, d_up, d_down, mixed = refs[:4]
+    d_gate[...] = gate[...].astype(F32)
+    d_up[...] = up[0].astype(F32) + up_land[0].astype(F32) + up_in[...].astype(F32)
+    d_down[...] = down[0].astype(F32) + down_land[0].astype(F32) + down_in[...].astype(F32)
+    mixed[...] = (hidden[...] + out_sum[...].astype(F32)).astype(BF)
+    for src, dst in zip(copies, refs[4:]):
+        dst[...] = src[...]
+
+
+def add_up(place, gate, up, up_land, up_in, down, down_land, down_in, hidden, out_sum, *copies):
+    def flat(array):
+        rows, columns = array.shape
+        return pl.BlockSpec((rows // ADD_STEPS, columns), lambda i, s: (i, 0))
+
+    def first(array):
+        _, rows, columns = array.shape
+        return pl.BlockSpec((1, rows // ADD_STEPS, columns), lambda i, s: (0, i, 0))
+
+    def own(array):
+        _, rows, columns = array.shape
+        return pl.BlockSpec((1, rows // ADD_STEPS, columns), lambda i, s: (s[0], i, 0))
+
+    outs = [jax.ShapeDtypeStruct(a.shape, F32) for a in (gate, up_in, down_in)]
+    outs += [jax.ShapeDtypeStruct(hidden.shape, BF)]
+    outs += [jax.ShapeDtypeStruct(c.shape, c.dtype) for c in copies]
+    return pl.pallas_call(
+        add_kernel,
+        out_shape=outs,
+        grid_spec=pltpu.PrefetchScalarGridSpec(
+            num_scalar_prefetch=1,
+            grid=(ADD_STEPS,),
+            in_specs=[flat(gate), own(up), first(up_land), flat(up_in),
+                      own(down), first(down_land), flat(down_in), flat(hidden), flat(out_sum)]
+            + [flat(c) for c in copies],
+            out_specs=[flat(o) for o in outs],
+        ),
+    )(place, gate, up, up_land, up_in, down, down_land, down_in, hidden, out_sum, *copies)
 
 
 def each(left, right, how):
@@ -1372,115 +1574,99 @@
     total_experts = experts_local * group_count
     slots = MOST
     score_scale = head_dim ** (-0.5)
-    inputs = tokens[0].astype(F32)
-
-    places = jnp.arange(length, dtype=jnp.int32)
-    doc_ends = jnp.cumsum(lengths[0])
-    passed = (places[:, None] >= doc_ends[None, :]).astype(jnp.int32)
-    docs = jnp.sum(passed, axis=1)
-    offsets = places - jnp.sum(passed * lengths[0][None, :], axis=1)
-    allowed = (docs[:, None] == docs[None, :]) & (places[None, :] <= places[:, None])
     half = head_dim // 2
     inverse = 10000.0 ** (-jnp.arange(half, dtype=F32) / half)
-    angles = offsets.astype(F32)[:, None] * inverse[None, :]
-    cosine, sine = jnp.cos(angles), jnp.sin(angles)
-    cosine = jnp.concatenate([cosine, cosine], axis=1)
-    sine = jnp.concatenate([sine, -sine], axis=1)
-    bias = jnp.where(allowed, 0.0, masked_score).astype(F32)
-
-    expert_ids = jnp.arange(128, dtype=jnp.int32)
-    hits = jnp.any(routes[0][:, :, None] == expert_ids[None, None, :], axis=1).astype(BF)
+    frequency = jnp.concatenate([inverse, inverse])[None]
+
     cot_all = lax.all_gather(cotangent[0], "expert", axis=0)
     w_rows = lax.all_gather(w_out, "expert", axis=0, tiled=True)
-    normed, attn_norm_back = jax.vjp(rms_norm, inputs, gain_attn)
-    wq_cols, wk_cols, wv_cols, normed_all, hits_all = gather_weights(
-        w_query, w_key, w_value, normed.astype(BF), hits
+    wq_cols, wk_cols, wv_cols, normed_all, hits_all, cosine, sine, bias = gather_weights(
+        w_query, w_key, w_value, tokens[0], gain_attn[None], routes[0], lengths, frequency
     )
     normed_all = normed_all.reshape(length, width)
     w_cols = [w.reshape(width, cols) for w in (wq_cols, wk_cols, wv_cols)]
-    gain_q = lax.dynamic_slice_in_dim(gain_query, seq_me * cols, cols)
-    gain_k = lax.dynamic_slice_in_dim(gain_key, seq_me * cols, cols)
     (hidden, normed2_all, query_low, key_low, value_low, attended_low, probs, query_unit, key_unit,
-     scales) = attend(normed_all, *w_cols, w_rows, bias, cosine, sine, gain_q[None], gain_k[None],
+     scales) = attend(normed_all, *w_cols, w_rows, bias, cosine, sine, gain_query[None], gain_key[None],
                       tokens[0], gain_mlp[None])
-    normed2, mlp_norm_back = jax.vjp(rms_norm, hidden, gain_mlp)
-    normed2_low = normed2.astype(BF)
-
-    first_expert = group_me * experts_local
-    hit = lax.dynamic_slice_in_dim(hits_all, first_expert, experts_local, axis=2)
-    hit = hit.transpose(0, 2, 1)
-    before = (jnp.arange(tok_rows)[:, None] < jnp.arange(tok_rows)[None, :]).astype(BF)
-    rank = jnp.einsum("ejt,tu->eju", hit, before, preferred_element_type=F32)
-    slot_ids = jnp.arange(slots, dtype=jnp.int32)
-    chosen = (hit[:, :, None, :] > 0) & (rank.astype(jnp.int32)[:, :, None, :] == slot_ids[None, None, :, None])
-    chosen_low = chosen.astype(BF)
-
-    logits_all = jnp.einsum("etd,dn->etn", normed2_all, router, preferred_element_type=F32)
-    probs_all = jax.nn.softmax(logits_all, axis=-1)
-    mine = lax.dynamic_slice_in_dim(probs_all, first_expert, experts_local, axis=2)
-    gate_rows = jnp.einsum(
-        "ejmt,etj->jem", chosen.astype(F32), mine, precision=lax.Precision.HIGHEST
-    )[..., None]
-
-    roomy = group_count * slots <= 512
+    roomy = group_count * slots <= 512 and seq_count == 4
     if roomy:
-        both = chosen_low.reshape(group_count, experts_local * slots, tok_rows)
-        gate_wide = jnp.broadcast_to(
-            gate_rows.reshape(experts_local, group_count * slots, 1),
-            (experts_local, group_count * slots, 128),
+        router_wide = jnp.concatenate(
+            [router, jnp.zeros((width, 128 - total_experts), BF)], axis=1
         )
-        rows_sum, out_parts, _, d_w_gate, up_parts, down_parts = run_experts(
-            normed2_all, cot_all, both, both.transpose(0, 2, 1), gate_wide, w_gate, w_up, w_down
-        )
-        grad_normed2 = rows_sum[:, :width]
-        grad_probs = (
-            rows_sum[:, width : width + total_experts]
-            + rows_sum[:, width + total_experts : width + 2 * total_experts]
+        grad_hidden, grad_low, small, out_parts, gate_sum, up_parts, down_parts = run_experts(
+            normed2_all, cot_all, hits_all, router_wide, w_gate, w_up, w_down, hidden,
+            cotangent[0], gain_mlp[None]
         )
         expert_parts = (up_parts, down_parts)
     else:
+        normed2, mlp_norm_back = jax.vjp(rms_norm, hidden, gain_mlp)
+        normed2_low = normed2.astype(BF)
+
+        first_expert = group_me * experts_local
+        hit = lax.dynamic_slice_in_dim(hits_all, first_expert, experts_local, axis=2)
+        hit = hit.transpose(0, 2, 1)
+        before = (jnp.arange(tok_rows)[:, None] < jnp.arange(tok_rows)[None, :]).astype(BF)
+        rank = jnp.einsum("ejt,tu->eju", hit, before, preferred_element_type=F32)
+        slot_ids = jnp.arange(slots, dtype=jnp.int32)
+        chosen = (hit[:, :, None, :] > 0) & (rank.astype(jnp.int32)[:, :, None, :] == slot_ids[None, None, :, None])
+        chosen_low = chosen.astype(BF)
+
+        logits_all = jnp.einsum("etd,dn->etn", normed2_all, router, preferred_element_type=F32)
+        probs_all = jax.nn.softmax(logits_all, axis=-1)
+        mine = lax.dynamic_slice_in_dim(probs_all, first_expert, experts_local, axis=2)
+        gate_rows = jnp.einsum(
+            "ejmt,etj->jem", chosen.astype(F32), mine, precision=lax.Precision.HIGHEST
+        )[..., None]
+
         grad_normed2, grad_probs, out_parts, d_w_gate, d_w_up, d_w_down = plain_experts(
             normed2_all, cot_all, chosen, gate_rows, w_gate, w_up, w_down
         )
         expert_parts = ()
+        router_probs, softmax_back = jax.vjp(
+            partial(jax.nn.softmax, axis=-1), product(normed2_low, router)
+        )
+        (grad_logits,) = softmax_back(grad_probs)
+        grad_logits_low = grad_logits.astype(BF)
+        grad_router = jnp.einsum("td,te->ed", normed2_low, grad_logits_low, preferred_element_type=F32)
+        grad_normed2 = grad_normed2 + jnp.einsum(
+            "te,de->td", grad_logits_low, router, preferred_element_type=F32
+        )
+        grad_hidden_part, grad_gain_mlp = mlp_norm_back(grad_normed2)
+        grad_hidden = cotangent[0].astype(F32) + grad_hidden_part
+        grad_low = grad_hidden.astype(BF)
+        spare = -(total_experts + 1) % 8
+        small = jnp.concatenate([grad_router, grad_gain_mlp[None], jnp.zeros((spare, width), F32)])
+
     out_sum = lax.psum_scatter(out_parts, "expert", scatter_dimension=0, tiled=False)
 
-    router_probs, softmax_back = jax.vjp(
-        partial(jax.nn.softmax, axis=-1), product(normed2_low, router)
-    )
-    (grad_logits,) = softmax_back(grad_probs)
-    grad_logits_low = grad_logits.astype(BF)
-    grad_router = jnp.einsum("td,te->ed", normed2_low, grad_logits_low, preferred_element_type=F32)
-    grad_normed2 = grad_normed2 + jnp.einsum(
-        "te,de->td", grad_logits_low, router, preferred_element_type=F32
-    )
-    grad_hidden_part, grad_gain_mlp = mlp_norm_back(grad_normed2)
-    grad_hidden = cotangent[0].astype(F32) + grad_hidden_part
-
-    spare = -(total_experts + 4) % 8 + 3
-    small = jnp.concatenate([grad_router, grad_gain_mlp[None], jnp.zeros((spare, width), F32)])
     d_tokens, d_w_query, d_w_key, d_w_value, d_w_out, small, *crossed = finish_all(
-        (grad_hidden.astype(BF), grad_hidden, tokens[0], gain_attn[None], w_rows, query_low,
+        (grad_low, grad_hidden, tokens[0], gain_attn[None], w_rows, query_low,
          key_low, value_low, attended_low, probs, query_unit, key_unit, scales,
-         gain_q[None], gain_k[None], cosine, sine, normed_all, *w_cols, small),
+         gain_query[None], gain_key[None], cosine, sine, normed_all, *w_cols, small),
         expert_parts,
     )
-    mixed = hidden + after(out_sum, d_w_out).astype(F32)
+    out_sum = after(out_sum, d_w_out)
     if roomy:
+        (d_w_gate, d_w_up, d_w_down, mixed, d_tokens, d_w_query, d_w_key, d_w_value,
+         d_w_out) = add_up(
+            seq_me.astype(jnp.int32)[None], gate_sum,
+            up_parts, crossed[0], crossed[1], down_parts, crossed[2], crossed[3],
+            hidden, out_sum, d_tokens, d_w_query, d_w_key, d_w_value, d_w_out,
+        )
         d_w_gate = d_w_gate.reshape(experts_local, width // seq_count, -1)
-        d_w_up = (crossed[1].astype(F32) + crossed[2].astype(F32)).reshape(d_w_gate.shape)
-        d_w_down = (crossed[4].astype(F32) + crossed[5].astype(F32)).reshape(
-            experts_local, -1, width
-        )
+        d_w_up = d_w_up.reshape(d_w_gate.shape)
+        d_w_down = d_w_down.reshape(experts_local, -1, width)
+    else:
+        mixed = (hidden + out_sum.astype(F32)).astype(BF)
     return (
-        mixed.astype(BF)[None],
+        mixed[None],
         d_tokens[None],
-        small[-1],
+        small[-6],
         d_w_query,
         d_w_key,
         d_w_value,
-        small[-3],
-        small[-2],
+        small[-8],
+        small[-7],
         d_w_out,
         small[total_experts],
         small[:total_experts].T,

time: 542 us -> 521 us (0.961)
  Pallas kernels: 464 us -> 495 us
  other arithmetic: 23.7 us -> 0.6 us
  matrix products: 20.2 us -> 0 us
  local copies, waits for them, and re-layouts: 15.2 us -> 6.61 us
    dot_general x6 -> x0, matrix products: 20.2 us -> none  [the longest x1 16.2 us: local(): jnp.einsum('etd,dn->etn', normed2_all, router, preferred_element_type=F32)]
    pallas_call x4, Pallas kernels: 464 us -> 482 us  [call(): pl.pallas_call(kernel, out_shape=outs, in_specs=specs or [ANY] * len(args...]
    pallas_call x0 -> x1, Pallas kernels: none -> 13.4 us  [add_up(): pl.pallas_call(add_kernel, out_shape=outs, grid_spec=pltpu.PrefetchScalar...]
    add x2 -> x0, other arithmetic: 8.13 us -> none  [the longest x1 5.31 us: local(): crossed[1].astype(F32) + crossed[2].astype(F32)]
  transfers between devices with their start and end apart: 3 -> 3, of which waited for: 0 -> 0; matrix products, arithmetic and copies ran while one was open for 9% -> 1% of each run, Pallas kernels for 66% -> 70%
where the time goes in v4:
time: 521 us; the launch traced here: 518 us
  Pallas kernels  495 us (95%)
  between operations  14 us (3%)
  local copies, waits for them, and re-layouts  6.61 us (1%)
    pallas_call x4, Pallas kernels, call(): pl.pallas_call(kernel, out_shape=outs, in_specs=specs or [ANY] * len(args...  482 us
    pallas_call x1, Pallas kernels, add_up(): pl.pallas_call(add_kernel, out_shape=outs, grid_spec=pltpu.PrefetchScalar...  13.4 us
  transfers between devices with their start and end apart: 3, of which 0 were waited for; matrix products, arithmetic and copies ran while one was open for 1% of the time, Pallas kernels for 70%

profile of v4, /device:TPU:0, one launch (start us, length us, event | category | flops | bytes accessed | tf_op | source)
XLA Modules:
  0.0 518.1 jit_solution(4396045425345558188)
XLA Ops:
  7.2 0.0 all-gather.3.cloned.1.call-start
  7.2 0.7 all-gather.3.cloned.1.call-update
  7.9 0.0 all-gather.5.cloned.1.call-start
  8.0 0.7 all-gather.5.cloned.1.call-update
  8.7 0.0 reduce-scatter.2.cloned.1.call-start
  8.7 1.4 copy.32
  10.1 1.1 copy.33
  11.2 0.9 concatenate.7.router
  12.2 0.6 maximum_bitcast_fusion.frequency
  12.7 106.2 %shard_map.263 = (bf16[4,512,512]{2,1,0:T(8,128)(2,1)}, bf16[4,512,512]{2,1,0:T(8,128)(2,1)}, bf16[4,512,512]{2,1,0:T(8,128)(2,1)}, bf16[4,128,2048]{2,1,0:T(8,1...) custom-call(bf16[64,2048]{1,0:T(8,128)(2,1)} %wq.1, ...), custom_call_target="tpu_custom_call" | custom-call | bytes 270000000 | tf_op jit(solution)/shard_map/pallas_call | solution.py:355
  118.9 0.0 all-gather.3.cloned.1.call-done.w_rows
  119.0 86.9 %shard_map.264 = (f32[128,2048]{1,0:T(8,128)}, bf16[8,128,2048]{2,1,0:T(8,128)(2,1)}, bf16[512,512]{1,0:T(8,128)(2,1)}, bf16[512,512]{1,0:T(8,128)(2,1)}, bf16[5...) custom-call(bf16[512,2048]{1,0:T(8,128)(2,1)} %bitcast.32, ...), custom_call_target="tpu_custom_call" | custom-call | bytes 240000000 | tf_op jit(solution)/shard_map/pallas_call | solution.py:355
  205.9 0.0 all-gather.5.cloned.1.call-done.cot
  205.9 119.1 %shard_map.265 = (f32[128,2048]{1,0:T(8,128)}, bf16[128,2048]{1,0:T(8,128)(2,1)}, f32[24,2048]{1,0:T(8,128)}, bf16[8,128,2048]{2,1,0:T(8,128)(2,1)}, bf16[1024,1...) custom-call(bf16[8,128,2048]{2,1,0:T(8,128)(2,1)} %get-tuple-element.66.n2, ...), custom_call_target="tpu_custom_call" | custom-call | bytes 300000000 | tf_op jit(solution)/shard_map/pallas_call | solution.py:355
  325.1 0.0 reduce-scatter.2.cloned.1.call-update
  325.1 169.7 %shard_map.266 = (f32[128,2048]{1,0:T(8,128)}, f32[64,2048]{1,0:T(8,128)}, f32[64,2048]{1,0:T(8,128)}, f32[64,2048]{1,0:T(8,128)}, f32[64,2048]{1,0:T(8,128)}, /...) custom-call(bf16[128,2048]{1,0:T(8,128)(2,1)} %get-tuple-element.71., ...), custom_call_target="tpu_custom_call" | custom-call | bytes 450000000 | tf_op jit(solution)/shard_map/pallas_call | solution.py:355
  494.7 1.6 fusion
  496.4 1.6 slice_bitcast_fusion
  497.9 0.0 reduce-scatter.2.cloned.1.call-done
  497.9 13.4 %shard_map.267 = (f32[1024,1024]{1,0:T(8,128)}, f32[1024,1024]{1,0:T(8,128)}, f32[512,2048]{1,0:T(8,128)}, bf16[128,2048]{1,0:T(8,128)(2,1)}, f32[128,2048]{1,0:...) custom-call(s32[1]{0:T(128)} %bitcast.place, ...), custom_call_target="tpu_custom_call" | custom-call | tf_op jit(solution)/shard_map/pallas_call | solution.py:1470
  (1 shorter events, 0.0 us)
Async XLA Ops:
  7.2 111.8 %all-gather.3.cloned.1.call-start = ((), (), s32[]{:S(2)}) async-start(), calls=%async_computation.1 | async-start | bytes 2359296 | tf_op jit(solution)/shard_map/all_gather | solution.py:1582
  7.9 198.0 %all-gather.5.cloned.1.call-start = ((), (), s32[]{:S(2)}) async-start(), calls=%async_computation.2 | async-start | bytes 4718592 | tf_op jit(solution)/shard_map/all_gather | solution.py:1581
  8.7 489.3 %reduce-scatter.2.cloned.1.call-start = ((), (), s32[]{:S(2)}) async-start(), calls=%async_computation.3 | async-start | bytes 4718592 | tf_op jit(solution)/shard_map/reduce_scatter | solution.py:1640
Sparse Core Ops, SparseCore 0:
  10.1 76.5 all-gather.2
  88.9 92.6 all-gather.4
  325.2 126.3 reduce-scatter.1

commit v5 on v4

--- a/solution.py
+++ b/solution.py
@@ -372,14 +372,6 @@
 ):
     seq, group = Ring("seq"), Ring("expert")
     others = [{"seq": seq.me ^ d} for d in range(1, seq.size)]
-    value = tokens[...].astype(F32)
-    inv = lax.rsqrt(jnp.mean(value * value, axis=-1, keepdims=True) + norm_eps)
-    normed[...] = (value * inv * gain[...]).astype(BF)
-    names = lax.broadcasted_iota(jnp.int32, hits.shape, 1)
-    hit = jnp.zeros(hits.shape, F32)
-    for k in range(routes.shape[1]):
-        hit = jnp.where(routes[:, k : k + 1] == names, 1.0, hit)
-    hits[...] = hit.astype(BF)
     greet(others + group.partners())
     wrows = wq.shape[0]
     cols = wq.shape[1] // seq.size
@@ -407,6 +399,14 @@
         own[i].start()
         for d in range(1, seq.size):
             swap_copy(i, d).start()
+    value = tokens[...].astype(F32)
+    inv = lax.rsqrt(jnp.mean(value * value, axis=-1, keepdims=True) + norm_eps)
+    normed[...] = (value * inv * gain[...]).astype(BF)
+    names = lax.broadcasted_iota(jnp.int32, hits.shape, 1)
+    hit = jnp.zeros(hits.shape, F32)
+    for k in range(routes.shape[1]):
+        hit = jnp.where(routes[:, k : k + 1] == names, 1.0, hit)
+    hits[...] = hit.astype(BF)
     own[3].start()
     own[4].start()
     for d in range(1, seq.size):
@@ -488,7 +488,7 @@
     )
 
 
-HIDDEN_CHUNKS = 2
+HIDDEN_CHUNKS = 4
 
 
 def turn(values, cos_rows, sin_rows):

time: 521 us -> 519 us (level)
  no operation moved by 1% of the time
where the time goes in v5:
time: 519 us; the launch traced here: 516 us
  Pallas kernels  493 us (95%)
  between operations  14 us (3%)
  local copies, waits for them, and re-layouts  6.61 us (1%)
    pallas_call x4, Pallas kernels, call(): pl.pallas_call(kernel, out_shape=outs, in_specs=specs or [ANY] * len(args...  480 us
    pallas_call x1, Pallas kernels, add_up(): pl.pallas_call(add_kernel, out_shape=outs, grid_spec=pltpu.PrefetchScalar...  13.4 us
  transfers between devices with their start and end apart: 3, of which 0 were waited for; matrix products, arithmetic and copies ran while one was open for 1% of the time, Pallas kernels for 70%

profile of v5, /device:TPU:0, one launch (start us, length us, event | category | flops | bytes accessed | tf_op | source)
XLA Modules:
  0.0 515.8 jit_solution(14825448813040217833)
XLA Ops:
  7.2 0.0 all-gather.3.cloned.1.call-start
  7.2 0.7 all-gather.3.cloned.1.call-update
  7.9 0.0 all-gather.5.cloned.1.call-start
  8.0 0.7 all-gather.5.cloned.1.call-update
  8.7 0.0 reduce-scatter.2.cloned.1.call-start
  8.7 1.4 copy.32
  10.1 1.1 copy.33
  11.2 0.9 concatenate.7.router
  12.2 0.6 maximum_bitcast_fusion.frequency
  12.7 106.2 %shard_map.263 = (bf16[4,512,512]{2,1,0:T(8,128)(2,1)}, bf16[4,512,512]{2,1,0:T(8,128)(2,1)}, bf16[4,512,512]{2,1,0:T(8,128)(2,1)}, bf16[4,128,2048]{2,1,0:T(8,1...) custom-call(bf16[64,2048]{1,0:T(8,128)(2,1)} %wq.1, ...), custom_call_target="tpu_custom_call" | custom-call | bytes 270000000 | tf_op jit(solution)/shard_map/pallas_call | solution.py:355
  118.9 0.0 all-gather.3.cloned.1.call-done.w_rows
  119.0 84.6 %shard_map.264 = (f32[128,2048]{1,0:T(8,128)}, bf16[8,128,2048]{2,1,0:T(8,128)(2,1)}, bf16[512,512]{1,0:T(8,128)(2,1)}, bf16[512,512]{1,0:T(8,128)(2,1)}, bf16[5...) custom-call(bf16[512,2048]{1,0:T(8,128)(2,1)} %bitcast.32, ...), custom_call_target="tpu_custom_call" | custom-call | bytes 240000000 | tf_op jit(solution)/shard_map/pallas_call | solution.py:355
  203.6 0.0 all-gather.5.cloned.1.call-done.cot
  203.7 119.2 %shard_map.265 = (f32[128,2048]{1,0:T(8,128)}, bf16[128,2048]{1,0:T(8,128)(2,1)}, f32[24,2048]{1,0:T(8,128)}, bf16[8,128,2048]{2,1,0:T(8,128)(2,1)}, bf16[1024,1...) custom-call(bf16[8,128,2048]{2,1,0:T(8,128)(2,1)} %get-tuple-element.66.n2, ...), custom_call_target="tpu_custom_call" | custom-call | bytes 300000000 | tf_op jit(solution)/shard_map/pallas_call | solution.py:355
  322.9 0.0 reduce-scatter.2.cloned.1.call-update
  322.9 169.6 %shard_map.266 = (f32[128,2048]{1,0:T(8,128)}, f32[64,2048]{1,0:T(8,128)}, f32[64,2048]{1,0:T(8,128)}, f32[64,2048]{1,0:T(8,128)}, f32[64,2048]{1,0:T(8,128)}, /...) custom-call(bf16[128,2048]{1,0:T(8,128)(2,1)} %get-tuple-element.71., ...), custom_call_target="tpu_custom_call" | custom-call | bytes 450000000 | tf_op jit(solution)/shard_map/pallas_call | solution.py:355
  492.5 1.6 fusion
  494.1 1.6 slice_bitcast_fusion
  495.7 0.0 reduce-scatter.2.cloned.1.call-done
  495.7 13.4 %shard_map.267 = (f32[1024,1024]{1,0:T(8,128)}, f32[1024,1024]{1,0:T(8,128)}, f32[512,2048]{1,0:T(8,128)}, bf16[128,2048]{1,0:T(8,128)(2,1)}, f32[128,2048]{1,0:...) custom-call(s32[1]{0:T(128)} %bitcast.place, ...), custom_call_target="tpu_custom_call" | custom-call | tf_op jit(solution)/shard_map/pallas_call | solution.py:1470
  (1 shorter events, 0.0 us)
Async XLA Ops:
  7.2 111.8 %all-gather.3.cloned.1.call-start = ((), (), s32[]{:S(2)}) async-start(), calls=%async_computation.1 | async-start | bytes 2359296 | tf_op jit(solution)/shard_map/all_gather | solution.py:1582
  7.9 195.7 %all-gather.5.cloned.1.call-start = ((), (), s32[]{:S(2)}) async-start(), calls=%async_computation.2 | async-start | bytes 4718592 | tf_op jit(solution)/shard_map/all_gather | solution.py:1581
  8.7 487.1 %reduce-scatter.2.cloned.1.call-start = ((), (), s32[]{:S(2)}) async-start(), calls=%async_computation.3 | async-start | bytes 4718592 | tf_op jit(solution)/shard_map/reduce_scatter | solution.py:1640
Sparse Core Ops, SparseCore 0:
  10.1 77.0 all-gather.2
  89.3 95.1 all-gather.4
  323.1 126.0 reduce-scatter.1
